TPU v7x, 32 devices: a whole 2x2x4 slice. The times are simulated.
32 devices in a mesh: rows: 8 (over z, y), cols: 4 (over x, core).
Axes of the slice: x: 2, y: 2, z: 4, core: 2. Of those that a mesh axis runs over, the one named last changes fastest.
Arguments:
- image_pair: bfloat16 [1, 256, 256, 6], P(None, 'rows', 'cols'), may hold values from -6 to 6
- noise_target: float32 [1, 256, 256, 3], P(None, 'rows', 'cols'), may hold values from -6 to 6
- timesteps: int32 [1, 5, 5], replicated, may hold values from 0 to 999
- text_pooled: bfloat16 [1, 5, 5, 4096], replicated, may hold values from -6 to 6
- slot_live: int32 [1, 5, 5], replicated, may hold values 0 or 1
- edgeconv_weight: float32 [9, 128, 9], replicated
- edgeconv_first: float32 [9, 128, 9], replicated, may hold values from -7.6293945e-05 to 7.6293945e-05
- edgeconv_second: float32 [9, 128, 9], replicated, may hold values from 4.4475685e-12 to 1.9766971e-10
- convlow_weight: float32 [4, 9, 128, 128], P(None, None, 'rows', 'cols')
- convlow_first: float32 [4, 9, 128, 128], P(None, None, 'rows', 'cols'), may hold values from -1.5258789e-05 to 1.5258789e-05
- convlow_second: float32 [4, 9, 128, 128], P(None, None, 'rows', 'cols'), may hold values from 4.9417425e-13 to 1.976697e-12
- convhigh_weight: float32 [2, 9, 256, 256], P(None, None, 'rows', 'cols')
- convhigh_first: float32 [2, 9, 256, 256], P(None, None, 'rows', 'cols'), may hold values from -1.5258789e-05 to 1.5258789e-05
- convhigh_second: float32 [2, 9, 256, 256], P(None, None, 'rows', 'cols'), may hold values from 4.9417425e-13 to 1.976697e-12
- downconv_weight: float32 [9, 128, 256], P(None, 'rows', 'cols')
- downconv_first: float32 [9, 128, 256], P(None, 'rows', 'cols'), may hold values from -1.5258789e-05 to 1.5258789e-05
- downconv_second: float32 [9, 128, 256], P(None, 'rows', 'cols'), may hold values from 4.9417425e-13 to 1.976697e-12
- upconv_weight: float32 [9, 256, 128], P(None, 'rows', 'cols')
- upconv_first: float32 [9, 256, 128], P(None, 'rows', 'cols'), may hold values from -1.5258789e-05 to 1.5258789e-05
- upconv_second: float32 [9, 256, 128], P(None, 'rows', 'cols'), may hold values from 4.9417425e-13 to 1.976697e-12
- condproj_weight: float32 [4224, 512], P(None, ('rows', 'cols'))
- condproj_first: float32 [4224, 512], P(None, ('rows', 'cols')), may hold values from -1.5258789e-05 to 1.5258789e-05
- condproj_second: float32 [4224, 512], P(None, ('rows', 'cols')), may hold values from 4.9417425e-13 to 1.976697e-12
- filmproj_weight: float32 [512, 1024], P('rows', 'cols')
- filmproj_first: float32 [512, 1024], P('rows', 'cols'), may hold values from -1.5258789e-05 to 1.5258789e-05
- filmproj_second: float32 [512, 1024], P('rows', 'cols'), may hold values from 4.9417425e-13 to 1.976697e-12
- normparams_weight: float32 [2, 1152], replicated, may hold values from -0.5 to 1.3, as said below
- normparams_first: float32 [2, 1152], replicated, may hold values from -7.6293945e-05 to 7.6293945e-05
- normparams_second: float32 [2, 1152], replicated, may hold values from 1.2354357e-11 to 4.941743e-11
Outputs:
- edgeconv_grad: float32 [9, 128, 9], replicated
- edgeconv_moment: float32 [9, 128, 9], replicated
- edgeconv_new: float32 [9, 128, 9], replicated
- convlow_grad: float32 [4, 9, 128, 128], P(None, None, 'rows', 'cols')
- convlow_moment: float32 [4, 9, 128, 128], P(None, None, 'rows', 'cols')
- convlow_new: float32 [4, 9, 128, 128], P(None, None, 'rows', 'cols')
- convhigh_grad: float32 [2, 9, 256, 256], P(None, None, 'rows', 'cols')
- convhigh_moment: float32 [2, 9, 256, 256], P(None, None, 'rows', 'cols')
- convhigh_new: float32 [2, 9, 256, 256], P(None, None, 'rows', 'cols')
- downconv_grad: float32 [9, 128, 256], P(None, 'rows', 'cols')
- downconv_moment: float32 [9, 128, 256], P(None, 'rows', 'cols')
- downconv_new: float32 [9, 128, 256], P(None, 'rows', 'cols')
- upconv_grad: float32 [9, 256, 128], P(None, 'rows', 'cols')
- upconv_moment: float32 [9, 256, 128], P(None, 'rows', 'cols')
- upconv_new: float32 [9, 256, 128], P(None, 'rows', 'cols')
- condproj_grad: float32 [4224, 512], P(None, ('rows', 'cols'))
- condproj_moment: float32 [4224, 512], P(None, ('rows', 'cols'))
- condproj_new: float32 [4224, 512], P(None, ('rows', 'cols'))
- filmproj_grad: float32 [512, 1024], P('rows', 'cols')
- filmproj_moment: float32 [512, 1024], P('rows', 'cols')
- filmproj_new: float32 [512, 1024], P('rows', 'cols')
- normparams_grad: float32 [2, 1152], replicated
- normparams_moment: float32 [2, 1152], replicated
- normparams_new: float32 [2, 1152], replicated
- loss_sum: float32 [], replicated
- loss_count: float32 [], replicated
- clip_norm: float32 [], replicated
- image_grad: float32 [1, 256, 256, 6], P(None, 'rows', 'cols')
Inputs may be any that keep to these rules, and one draw needn't show every extreme that they name: `normparams_weight`: row 0 holds the norms' gains, row 1 their biases.
All inputs are finite; a program needn't handle non-finite values.
Results may differ from a plain program's by a relative error of at most 0.018.
Values may be sent and summed in bfloat16 or wider, within the bound.
A program may use at most 256 MiB of HBM per device.

v0:
```python
import math

import jax
import jax.numpy as jnp
from jax import lax
from jax.sharding import PartitionSpec as P

SLOT = 64
SLOTS = 5
C1 = 128
C2 = 256
GROUPS = 32
TEMB = 128
STEP = 10


HIGH = lax.Precision.HIGHEST
EPS_NORM = 1e-05
CLIP_AT = 0.05
RATE = 0.5
BETA_ONE = 0.9
BETA_TWO = 0.999
EPS_ADAM = 1e-06
DECAY = 0.01


def entering(part, axis, combine, identity, reverse):
    count = lax.axis_size(axis)
    place = lax.axis_index(axis)
    ahead = count - 1 - place if reverse else place
    gathered = jax.tree.map(lambda a: lax.all_gather(a, axis), part)
    state = jax.tree.map(lambda a, e: jnp.zeros_like(a) + jnp.asarray(e, a.dtype), part, identity)

    def one(turn, state):
        source = count - 1 - turn if reverse else turn
        return combine(
            state, jax.tree.map(lambda a: lax.dynamic_index_in_dim(a, source, 0, False), gathered)
        )

    return lax.fori_loop(0, ahead, one, state)


def padded_2(block, sides, width):
    for axis, dim in sides:
        count = lax.axis_size(axis)
        forward = [(i, i + 1) for i in range(count - 1)]
        backward = [(target, source) for source, target in forward]
        low = lax.ppermute(
            lax.slice_in_dim(block, block.shape[dim] - width, None, axis=dim), axis, forward
        )
        high = lax.ppermute(lax.slice_in_dim(block, 0, width, axis=dim), axis, backward)
        block = jnp.concatenate([low, block, high], axis=dim)
    return block


def time_embed(steps):
    half = TEMB // 2
    freq = jnp.exp(-math.log(10000.0) * jnp.arange(half, dtype=jnp.float32) / half)
    angle = steps.astype(jnp.float32)[..., None] * freq
    return jnp.concatenate([jnp.sin(angle), jnp.cos(angle)], axis=-1)


def silu_grad(values):
    sigma = jax.nn.sigmoid(values)
    return sigma * (1.0 + values * (1.0 - sigma))


def tap_masks(rows, cols, slot):
    half = slot // 2
    row_pos = lax.axis_index("rows") * rows + jnp.arange(rows)
    col_pos = lax.axis_index("cols") * cols + jnp.arange(cols)
    row_ok = [
        (row_pos + offset + half) // slot == (row_pos + half) // slot for offset in (-1, 0, 1)
    ]
    col_ok = [
        (col_pos + offset + half) // slot == (col_pos + half) // slot for offset in (-1, 0, 1)
    ]
    return [
        (row_ok[tap // 3][:, None] & col_ok[tap % 3][None, :]).astype(jnp.bfloat16)
        for tap in range(9)
    ]


def slot_level(rows, cols, slot, size):
    half = slot // 2
    labels = jnp.arange(SLOTS)
    row_pos = lax.axis_index("rows") * rows + jnp.arange(rows)
    col_pos = lax.axis_index("cols") * cols + jnp.arange(cols)
    row_map = (((row_pos + half) // slot)[:, None] == labels[None, :]).astype(jnp.float32)
    col_map = (((col_pos + half) // slot)[:, None] == labels[None, :]).astype(jnp.float32)
    every = (jnp.arange(size) + half) // slot
    side = jnp.sum((every[:, None] == labels[None, :]).astype(jnp.float32), axis=0)
    return (row_map, col_map, side[:, None] * side[None, :])


def to_slots(values, level):
    return jnp.einsum("nhwk,ha,wb->nabk", values, level[0], level[1], precision=HIGH)


def to_pixels(table, level):
    return jnp.einsum("nabk,ha,wb->nhwk", table, level[0], level[1], precision=HIGH)


def add_pair(earlier, later):
    return (earlier[0] + later[0], earlier[1] + later[1])


def slot_total(tables):
    empty = (jnp.zeros_like(tables[0]), jnp.zeros_like(tables[1]))
    before = entering(tables, ("rows", "cols"), add_pair, empty, False)
    after = entering(tables, ("rows", "cols"), add_pair, empty, True)
    return (before[0] + tables[0] + after[0], before[1] + tables[1] + after[1])


def pad_rim(values):
    return padded_2(values, (("rows", 1), ("cols", 2)), 1)


def tap_patch(padded, masks, tap, stride):
    rows = padded.shape[1] - 2
    cols = padded.shape[2] - 2
    row_off, col_off = (tap // 3, tap % 3)
    patch = padded[:, row_off : row_off + rows : stride, col_off : col_off + cols : stride, :]
    return patch * masks[tap][::stride, ::stride][None, :, :, None]


def conv_taps(padded, weight, masks, stride):
    total = None
    for tap in range(9):
        term = jnp.einsum(
            "nhwc,cd->nhwd",
            tap_patch(padded, masks, tap, stride),
            weight[tap],
            preferred_element_type=jnp.float32,
        )
        total = term if total is None else total + term
    return total


def conv_weight_grad(padded, grad_out, masks, stride):
    return jnp.stack(
        [
            jnp.einsum(
                "nhwc,nhwd->cd",
                tap_patch(padded, masks, tap, stride),
                grad_out,
                preferred_element_type=jnp.float32,
            )
            for tap in range(9)
        ]
    )


def conv_input_grad(grad_out, weight, masks, stride):
    spread = grad_out
    if stride == 2:
        canvases, rows, cols, width = grad_out.shape
        spread = jnp.stack([grad_out, jnp.zeros_like(grad_out)], axis=2).reshape(
            canvases, 2 * rows, cols, width
        )
        spread = jnp.stack([spread, jnp.zeros_like(spread)], axis=3).reshape(
            canvases, 2 * rows, 2 * cols, width
        )
    flipped = jnp.swapaxes(weight[::-1], 1, 2)
    padded = padded_2(spread, (("rows", 1), ("cols", 2)), 1)
    return conv_taps(padded, flipped, masks, 1)


def norm_forward(values, gain, bias, scale, shift, level):
    count_n, rows, cols, width = values.shape
    grouped = values.reshape(count_n, rows, cols, GROUPS, width // GROUPS)
    total, squares = slot_total(
        (
            to_slots(jnp.sum(grouped, axis=4), level),
            to_slots(jnp.sum(grouped * grouped, axis=4), level),
        )
    )
    count = level[2][None, :, :, None] * (width // GROUPS)
    mean = total / count
    var = squares / count - mean * mean
    inverse = lax.rsqrt(var + EPS_NORM)
    mean_pix = to_pixels(mean, level)
    inv_pix = to_pixels(inverse, level)
    hat = ((grouped - mean_pix[..., None]) * inv_pix[..., None]).reshape(values.shape)
    normed = hat * gain + bias
    if scale is None:
        return (normed, (hat, inv_pix, normed, None))
    factor = 1.0 + to_pixels(scale, level)
    return (normed * factor + to_pixels(shift, level), (hat, inv_pix, normed, factor))


def norm_backward(grad_out, kept, gain, level):
    hat, inv_pix, normed, factor = kept
    count_n, rows, cols, width = hat.shape
    if factor is None:
        film_grad = None
        grad_normed = grad_out
    else:
        film_grad = jnp.concatenate(
            [to_slots(grad_out * normed, level), to_slots(grad_out, level)], axis=-1
        )
        grad_normed = grad_out * factor
    grad_gain = jnp.sum(grad_normed * hat, axis=(0, 1, 2))
    grad_bias = jnp.sum(grad_normed, axis=(0, 1, 2))
    shape = (count_n, rows, cols, GROUPS, width // GROUPS)
    grad_hat = (grad_normed * gain).reshape(shape)
    grouped_hat = hat.reshape(shape)
    first, second = slot_total(
        (
            to_slots(jnp.sum(grad_hat, axis=4), level),
            to_slots(jnp.sum(grad_hat * grouped_hat, axis=4), level),
        )
    )
    count = level[2][None, :, :, None] * (width // GROUPS)
    mean_one = to_pixels(first / count, level)[..., None]
    mean_two = to_pixels(second / count, level)[..., None]
    grad_in = inv_pix[..., None] * (grad_hat - mean_one - grouped_hat * mean_two)
    return (grad_in.reshape(hat.shape), grad_gain, grad_bias, film_grad)


def block_forward(hidden, weights, gains, film, level, masks):
    pre_one, saved_one = norm_forward(hidden, gains[0], gains[1], None, None, level)
    rim_one = pad_rim(jax.nn.silu(pre_one).astype(jnp.bfloat16))
    conv_one = conv_taps(rim_one, weights[0], masks, 1)
    pre_two, saved_two = norm_forward(conv_one, gains[2], gains[3], film[0], film[1], level)
    rim_two = pad_rim(jax.nn.silu(pre_two).astype(jnp.bfloat16))
    out = hidden + conv_taps(rim_two, weights[1], masks, 1)
    return (out, (pre_one, saved_one, rim_one, pre_two, saved_two, rim_two))


def block_backward(grad_out, weights, gains, kept, level, masks):
    pre_one, saved_one, rim_one, pre_two, saved_two, rim_two = kept
    grad_two = grad_out.astype(jnp.bfloat16)
    weight_two = conv_weight_grad(rim_two, grad_two, masks, 1)
    grad_pre_two = conv_input_grad(grad_two, weights[1], masks, 1) * silu_grad(pre_two)
    grad_conv, gain_two, bias_two, film_grad = norm_backward(
        grad_pre_two, saved_two, gains[2], level
    )
    grad_one = grad_conv.astype(jnp.bfloat16)
    weight_one = conv_weight_grad(rim_one, grad_one, masks, 1)
    grad_pre_one = conv_input_grad(grad_one, weights[0], masks, 1) * silu_grad(pre_one)
    grad_in, gain_one, bias_one, _ = norm_backward(grad_pre_one, saved_one, gains[0], level)
    return (
        grad_out + grad_in,
        (weight_one, weight_two),
        (gain_one, bias_one, gain_two, bias_two),
        film_grad,
    )


def per_device(
    image_pair,
    noise_target,
    timesteps,
    text_pooled,
    slot_live,
    edgeconv_weight,
    edgeconv_first,
    edgeconv_second,
    convlow_weight,
    convlow_first,
    convlow_second,
    convhigh_weight,
    convhigh_first,
    convhigh_second,
    downconv_weight,
    downconv_first,
    downconv_second,
    upconv_weight,
    upconv_first,
    upconv_second,
    condproj_weight,
    condproj_first,
    condproj_second,
    filmproj_weight,
    filmproj_first,
    filmproj_second,
    normparams_weight,
    normparams_first,
    normparams_second,
):
    canvases, rows_one, cols_one = image_pair.shape[:3]
    size_full = rows_one * lax.axis_size("rows")
    level_full = slot_level(rows_one, cols_one, SLOT, size_full)
    level_half = slot_level(rows_one // 2, cols_one // 2, SLOT // 2, size_full // 2)
    by_rows = (
        lax.all_gather(convlow_weight.astype(jnp.bfloat16), "rows", axis=2, tiled=True),
        lax.all_gather(convhigh_weight.astype(jnp.bfloat16), "rows", axis=2, tiled=True),
        lax.all_gather(downconv_weight.astype(jnp.bfloat16), "rows", axis=1, tiled=True),
        lax.all_gather(upconv_weight.astype(jnp.bfloat16), "rows", axis=1, tiled=True),
        lax.all_gather(filmproj_weight.astype(jnp.bfloat16), "rows", axis=0, tiled=True),
    )
    low_convs, high_convs, down_conv, up_conv, film_full = (
        lax.all_gather(by_rows[0], "cols", axis=3, tiled=True),
        lax.all_gather(by_rows[1], "cols", axis=3, tiled=True),
        lax.all_gather(by_rows[2], "cols", axis=2, tiled=True),
        lax.all_gather(by_rows[3], "cols", axis=2, tiled=True),
        lax.all_gather(by_rows[4], "cols", axis=1, tiled=True),
    )
    joined = jnp.concatenate([time_embed(timesteps).astype(jnp.bfloat16), text_pooled], axis=-1)
    cond_full = lax.all_gather(
        condproj_weight.astype(jnp.bfloat16), ("rows", "cols"), axis=1, tiled=True
    )
    pre_cond = jnp.einsum("nabk,kf->nabf", joined, cond_full, preferred_element_type=jnp.float32)
    cond_low = jax.nn.silu(pre_cond).astype(jnp.bfloat16)
    film_all = jnp.einsum("nabk,kf->nabf", cond_low, film_full, preferred_element_type=jnp.float32)
    offsets = [0, C1, 2 * C1, 3 * C1, 4 * C1, 4 * C1 + C2, 4 * C1 + 2 * C2, 5 * C1 + 2 * C2]

    def norm_part(index, which):
        return normparams_weight[which, offsets[index] : offsets[index + 1]]

    def block_gains(index):
        return (
            norm_part(2 * index, 0),
            norm_part(2 * index, 1),
            norm_part(2 * index + 1, 0),
            norm_part(2 * index + 1, 1),
        )

    def block_film(index):
        base = (0, 2 * C1, 4 * C1)[index]
        width = (C1, C1, C2)[index]
        return (film_all[..., base : base + width], film_all[..., base + width : base + 2 * width])

    masks_one = tap_masks(rows_one, cols_one, SLOT)
    masks_two = tap_masks(rows_one // 2, cols_one // 2, SLOT // 2)
    edge_low = edgeconv_weight.astype(jnp.bfloat16)
    inconv_low = jnp.swapaxes(edge_low[:, :, 0:6], 1, 2)
    head_low = edge_low[:, :, 6:9]
    rim_in = pad_rim(image_pair)
    hidden = conv_taps(rim_in, inconv_low, masks_one, 1)
    kept_blocks = []
    for index in range(2):
        hidden, kept = block_forward(
            hidden,
            (low_convs[2 * index], low_convs[2 * index + 1]),
            block_gains(index),
            block_film(index),
            level_full,
            masks_one,
        )
        kept_blocks.append(kept)
    rim_skip = pad_rim(hidden.astype(jnp.bfloat16))
    deep, kept_deep = block_forward(
        conv_taps(rim_skip, down_conv, masks_one, 2),
        (high_convs[0], high_convs[1]),
        block_gains(2),
        block_film(2),
        level_half,
        masks_two,
    )
    upsampled = jnp.repeat(jnp.repeat(deep.astype(jnp.bfloat16), 2, axis=1), 2, axis=2)
    rim_up = pad_rim(upsampled)
    merged = conv_taps(rim_up, up_conv, masks_one, 1) + hidden
    pre_head, kept_head = norm_forward(
        merged, norm_part(6, 0), norm_part(6, 1), None, None, level_full
    )
    rim_head = pad_rim(jax.nn.silu(pre_head).astype(jnp.bfloat16))
    pred = conv_taps(rim_head, head_low, masks_one, 1)
    live_slots = slot_live.astype(jnp.float32)
    live = to_pixels(live_slots[..., None], level_full)
    count = 3.0 * jnp.sum(live_slots * level_full[2][None, :, :])
    diff = pred - noise_target
    loss_local = jnp.sum(live * diff * diff)
    grad_pred = (2.0 * live * diff / count).astype(jnp.bfloat16)
    grad_head = conv_weight_grad(rim_head, grad_pred, masks_one, 1)
    grad_act = conv_input_grad(grad_pred, head_low, masks_one, 1) * silu_grad(pre_head)
    grad_merged, head_gain, head_bias, _ = norm_backward(
        grad_act, kept_head, norm_part(6, 0), level_full
    )
    merged_low = grad_merged.astype(jnp.bfloat16)
    grad_upconv = conv_weight_grad(rim_up, merged_low, masks_one, 1)
    grad_up = conv_input_grad(merged_low, up_conv, masks_one, 1)
    grad_deep = grad_up.reshape(canvases, rows_one // 2, 2, cols_one // 2, 2, C2).sum(axis=(2, 4))
    grad_down, deep_convs, deep_norms, deep_film = block_backward(
        grad_deep, (high_convs[0], high_convs[1]), block_gains(2), kept_deep, level_half, masks_two
    )
    down_low = grad_down.astype(jnp.bfloat16)
    grad_downconv = conv_weight_grad(rim_skip, down_low, masks_one, 2)
    grad_hidden = grad_merged + conv_input_grad(down_low, down_conv, masks_one, 2)
    block_convs = [None, None]
    block_norms = [None, None]
    block_films = [None, None]
    for index in (1, 0):
        grad_hidden, block_convs[index], block_norms[index], block_films[index] = block_backward(
            grad_hidden,
            (low_convs[2 * index], low_convs[2 * index + 1]),
            block_gains(index),
            kept_blocks[index],
            level_full,
            masks_one,
        )
    hidden_low = grad_hidden.astype(jnp.bfloat16)
    grad_inconv = conv_weight_grad(rim_in, hidden_low, masks_one, 1)
    image_grad = conv_input_grad(hidden_low, inconv_low, masks_one, 1) * count
    all_norms = block_norms + [deep_norms]
    gain_vector = jnp.concatenate([part[k] for part in all_norms for k in (0, 2)] + [head_gain])
    bias_vector = jnp.concatenate([part[k] for part in all_norms for k in (1, 3)] + [head_bias])
    film_grads = jnp.concatenate([block_films[0], block_films[1], deep_film], axis=-1)
    edge_local = jnp.concatenate([jnp.swapaxes(grad_inconv, 1, 2), grad_head], axis=2)
    film_sum, edge_sum, norm_sum, loss_sum = lax.psum(
        (film_grads, edge_local, jnp.stack([gain_vector, bias_vector]), loss_local),
        ("rows", "cols"),
    )
    grad_film_full = jnp.einsum(
        "nabk,nabf->kf", cond_low.astype(jnp.float32), film_sum, precision=HIGH
    )
    grad_cond = jnp.einsum(
        "nabf,kf->nabk", film_sum, film_full.astype(jnp.float32), precision=HIGH
    ) * silu_grad(pre_cond)
    grad_cond_full = jnp.einsum(
        "nabk,nabf->kf", joined.astype(jnp.float32), grad_cond, precision=HIGH
    )
    film_rows, film_cols = filmproj_weight.shape
    film_own = lax.dynamic_slice_in_dim(
        grad_film_full, lax.axis_index("rows") * film_rows, film_rows, 0
    )
    film_own = lax.dynamic_slice_in_dim(film_own, lax.axis_index("cols") * film_cols, film_cols, 1)
    cond_cols = condproj_weight.shape[1]
    cond_own = lax.dynamic_slice_in_dim(
        grad_cond_full, lax.axis_index(("rows", "cols")) * cond_cols, cond_cols, 1
    )
    by_cols = (
        lax.psum_scatter(
            jnp.stack(
                [block_convs[0][0], block_convs[0][1], block_convs[1][0], block_convs[1][1]]
            ).astype(jnp.bfloat16),
            "cols",
            scatter_dimension=3,
            tiled=True,
        ).astype(jnp.float32),
        lax.psum_scatter(
            jnp.stack([deep_convs[0], deep_convs[1]]).astype(jnp.bfloat16),
            "cols",
            scatter_dimension=3,
            tiled=True,
        ).astype(jnp.float32),
        lax.psum_scatter(
            grad_downconv.astype(jnp.bfloat16), "cols", scatter_dimension=2, tiled=True
        ).astype(jnp.float32),
        lax.psum_scatter(
            grad_upconv.astype(jnp.bfloat16), "cols", scatter_dimension=2, tiled=True
        ).astype(jnp.float32),
    )
    lowconv_own, highconv_own, downconv_own, upconv_own = (
        lax.psum_scatter(
            by_cols[0].astype(jnp.bfloat16), "rows", scatter_dimension=2, tiled=True
        ).astype(jnp.float32),
        lax.psum_scatter(
            by_cols[1].astype(jnp.bfloat16), "rows", scatter_dimension=2, tiled=True
        ).astype(jnp.float32),
        lax.psum_scatter(
            by_cols[2].astype(jnp.bfloat16), "rows", scatter_dimension=1, tiled=True
        ).astype(jnp.float32),
        lax.psum_scatter(
            by_cols[3].astype(jnp.bfloat16), "rows", scatter_dimension=1, tiled=True
        ).astype(jnp.float32),
    )
    weights = (
        edgeconv_weight,
        convlow_weight,
        convhigh_weight,
        downconv_weight,
        upconv_weight,
        condproj_weight,
        filmproj_weight,
        normparams_weight,
    )
    firsts = (
        edgeconv_first,
        convlow_first,
        convhigh_first,
        downconv_first,
        upconv_first,
        condproj_first,
        filmproj_first,
        normparams_first,
    )
    seconds = (
        edgeconv_second,
        convlow_second,
        convhigh_second,
        downconv_second,
        upconv_second,
        condproj_second,
        filmproj_second,
        normparams_second,
    )
    grads = (
        edge_sum,
        lowconv_own,
        highconv_own,
        downconv_own,
        upconv_own,
        cond_own,
        film_own,
        norm_sum,
    )
    sharded = (1, 2, 3, 4, 5, 6)
    stacked = (1, 2)
    owned_sq = sum((jnp.sum(grads[k] * grads[k]) for k in sharded))
    shared_sq = sum((jnp.sum(grads[k] * grads[k]) for k in range(8) if k not in sharded))
    clip_norm = jnp.sqrt(lax.psum(owned_sq, ("rows", "cols")) + shared_sq)
    factor = jnp.minimum(1.0, CLIP_AT / clip_norm)
    clipped, moments, updates = ([], [], [])
    for k in range(8):
        grad = grads[k] * factor
        first_new = BETA_ONE * firsts[k] + (1.0 - BETA_ONE) * grad
        second_new = BETA_TWO * seconds[k] + (1.0 - BETA_TWO) * grad * grad
        first_hat = first_new / (1.0 - BETA_ONE**STEP)
        second_hat = second_new / (1.0 - BETA_TWO**STEP)
        clipped.append(grad)
        moments.append(second_new)
        updates.append(first_hat / (jnp.sqrt(second_hat) + EPS_ADAM) + DECAY * weights[k])

    def matrix_squares(values, k):
        if k in stacked:
            return jnp.sum(values * values, axis=tuple(range(1, values.ndim)))
        return jnp.sum(values * values).reshape(1)

    weight_sq, update_sq = lax.psum(
        (
            jnp.concatenate([matrix_squares(weights[k], k) for k in sharded]),
            jnp.concatenate([matrix_squares(updates[k], k) for k in sharded]),
        ),
        ("rows", "cols"),
    )
    ratios = jnp.sqrt(weight_sq) / jnp.sqrt(update_sq)
    position = 0
    results = []
    for k in range(8):
        if k in sharded:
            span = weights[k].shape[0] if k in stacked else 1
            ratio = ratios[position : position + span]
            position += span
            ratio = (
                ratio.reshape((span,) + (1,) * (weights[k].ndim - 1)) if k in stacked else ratio[0]
            )
        elif k == 0:
            part = (jnp.arange(9) < 6)[None, None, :]
            other = jnp.logical_not(part)
            weight_sq_two = weights[k] * weights[k]
            update_sq_two = updates[k] * updates[k]
            ratio_in = jnp.sqrt(jnp.sum(jnp.where(part, weight_sq_two, 0.0))) / jnp.sqrt(
                jnp.sum(jnp.where(part, update_sq_two, 0.0))
            )
            ratio_out = jnp.sqrt(jnp.sum(jnp.where(other, weight_sq_two, 0.0))) / jnp.sqrt(
                jnp.sum(jnp.where(other, update_sq_two, 0.0))
            )
            ratio = jnp.where(part, ratio_in, ratio_out)
        else:
            ratio = jnp.sqrt(jnp.sum(weights[k] * weights[k])) / jnp.sqrt(
                jnp.sum(updates[k] * updates[k])
            )
        results.extend([clipped[k], moments[k], weights[k] - RATE * ratio * updates[k]])
    return (
        results[0],
        results[1],
        results[2],
        results[3],
        results[4],
        results[5],
        results[6],
        results[7],
        results[8],
        results[9],
        results[10],
        results[11],
        results[12],
        results[13],
        results[14],
        results[15],
        results[16],
        results[17],
        results[18],
        results[19],
        results[20],
        results[21],
        results[22],
        results[23],
        loss_sum,
        count,
        clip_norm,
        image_grad,
    )


def solution(mesh):
    placed = (
        P(None, "rows", "cols", None),
        P(None, "rows", "cols", None),
        P(),
        P(),
        P(),
        P(),
        P(),
        P(),
        P(None, None, "rows", "cols"),
        P(None, None, "rows", "cols"),
        P(None, None, "rows", "cols"),
        P(None, None, "rows", "cols"),
        P(None, None, "rows", "cols"),
        P(None, None, "rows", "cols"),
        P(None, "rows", "cols"),
        P(None, "rows", "cols"),
        P(None, "rows", "cols"),
        P(None, "rows", "cols"),
        P(None, "rows", "cols"),
        P(None, "rows", "cols"),
        P(None, ("rows", "cols")),
        P(None, ("rows", "cols")),
        P(None, ("rows", "cols")),
        P("rows", "cols"),
        P("rows", "cols"),
        P("rows", "cols"),
        P(),
        P(),
        P(),
    )
    return jax.shard_map(
        per_device,
        mesh=mesh,
        in_specs=placed,
        out_specs=(
            P(),
            P(),
            P(),
            P(None, None, "rows", "cols"),
            P(None, None, "rows", "cols"),
            P(None, None, "rows", "cols"),
            P(None, None, "rows", "cols"),
            P(None, None, "rows", "cols"),
            P(None, None, "rows", "cols"),
            P(None, "rows", "cols"),
            P(None, "rows", "cols"),
            P(None, "rows", "cols"),
            P(None, "rows", "cols"),
            P(None, "rows", "cols"),
            P(None, "rows", "cols"),
            P(None, ("rows", "cols")),
            P(None, ("rows", "cols")),
            P(None, ("rows", "cols")),
            P("rows", "cols"),
            P("rows", "cols"),
            P("rows", "cols"),
            P(),
            P(),
            P(),
            P(),
            P(),
            P(),
            P(None, "rows", "cols", None),
        ),
        check_vma=False,
    )
```

profile of v0, /device:TPU:0, one launch (start us, length us, event | category | flops | bytes accessed | tf_op | source)
XLA Modules:
  0.0 2690.9 jit_solution(11031846181514343203)
XLA Ops:
  238.5 44.5 %all-gather = f32[32,5,5,32]{3,2,1,0:T(8,128)S(1)} all-gather(f32[1,5,5,32]{3,2,1,0:T(8,128)S(1)} %copy.2564), channel_id=2, replica_groups=mesh['rows'=8,'cols'=4] {'rows','cols'}, dimensions={0}, use_global_device_ids=true | all-gather | bytes 105600 | tf_op jit(solution)/shard_map/all_gather | solution.py:31
  282.9 38.4 %all-gather.1 = f32[32,5,5,32]{3,2,1,0:T(8,128)S(1)} all-gather(f32[1,5,5,32]{3,2,1,0:T(8,128)S(1)} %copy.2568), channel_id=3, replica_groups=mesh['rows'=8,'cols'=4] {'rows','cols'}, dimensions={0}, use_global_device_ids=true | all-gather | bytes 105600 | tf_op jit(solution)/shard_map/all_gather | solution.py:31
  393.2 40.1 %all-gather.2 = f32[32,5,5,32]{3,2,1,0:T(8,128)S(1)} all-gather(f32[1,5,5,32]{3,2,1,0:T(8,128)S(1)} %copy.2597), channel_id=4, replica_groups=mesh['rows'=8,'cols'=4] {'rows','cols'}, dimensions={0}, use_global_device_ids=true | all-gather | bytes 105600 | tf_op jit(solution)/shard_map/all_gather | solution.py:31
  433.4 38.4 %all-gather.3 = f32[32,5,5,32]{3,2,1,0:T(8,128)S(1)} all-gather(f32[1,5,5,32]{3,2,1,0:T(8,128)S(1)} %copy.2601), channel_id=5, replica_groups=mesh['rows'=8,'cols'=4] {'rows','cols'}, dimensions={0}, use_global_device_ids=true | all-gather | bytes 105600 | tf_op jit(solution)/shard_map/all_gather | solution.py:31
  529.7 44.5 %all-gather.4 = f32[32,5,5,32]{3,2,1,0:T(8,128)S(1)} all-gather(f32[1,5,5,32]{3,2,1,0:T(8,128)S(1)} %copy.2633), channel_id=6, replica_groups=mesh['rows'=8,'cols'=4] {'rows','cols'}, dimensions={0}, use_global_device_ids=true | all-gather | bytes 105600 | tf_op jit(solution)/shard_map/all_gather | solution.py:31
  574.3 38.4 %all-gather.5 = f32[32,5,5,32]{3,2,1,0:T(8,128)S(1)} all-gather(f32[1,5,5,32]{3,2,1,0:T(8,128)S(1)} %copy.2637), channel_id=7, replica_groups=mesh['rows'=8,'cols'=4] {'rows','cols'}, dimensions={0}, use_global_device_ids=true | all-gather | bytes 105600 | tf_op jit(solution)/shard_map/all_gather | solution.py:31
  656.2 40.7 %all-gather.6 = f32[32,5,5,32]{3,2,1,0:T(8,128)S(1)} all-gather(f32[1,5,5,32]{3,2,1,0:T(8,128)S(1)} %copy.2664), channel_id=8, replica_groups=mesh['rows'=8,'cols'=4] {'rows','cols'}, dimensions={0}, use_global_device_ids=true | all-gather | bytes 105600 | tf_op jit(solution)/shard_map/all_gather | solution.py:31
  697.0 38.5 %all-gather.7 = f32[32,5,5,32]{3,2,1,0:T(8,128)S(1)} all-gather(f32[1,5,5,32]{3,2,1,0:T(8,128)S(1)} %copy.2668), channel_id=9, replica_groups=mesh['rows'=8,'cols'=4] {'rows','cols'}, dimensions={0}, use_global_device_ids=true | all-gather | bytes 105600 | tf_op jit(solution)/shard_map/all_gather | solution.py:31
  825.4 41.6 %all-gather.8 = f32[32,5,5,32]{3,2,1,0:T(8,128)S(1)} all-gather(f32[1,5,5,32]{3,2,1,0:T(8,128)S(1)} %copy.2709), channel_id=10, replica_groups=mesh['rows'=8,'cols'=4] {'rows','cols'}, dimensions={0}, use_global_device_ids=true | all-gather | bytes 105600 | tf_op jit(solution)/shard_map/all_gather | solution.py:31
  867.0 38.4 %all-gather.9 = f32[32,5,5,32]{3,2,1,0:T(8,128)S(1)} all-gather(f32[1,5,5,32]{3,2,1,0:T(8,128)S(1)} %copy.2713), channel_id=11, replica_groups=mesh['rows'=8,'cols'=4] {'rows','cols'}, dimensions={0}, use_global_device_ids=true | all-gather | bytes 105600 | tf_op jit(solution)/shard_map/all_gather | solution.py:31
  934.3 41.5 %all-gather.10 = f32[32,5,5,32]{3,2,1,0:T(8,128)S(1)} all-gather(f32[1,5,5,32]{3,2,1,0:T(8,128)S(1)} %copy.2740), channel_id=12, replica_groups=mesh['rows'=8,'cols'=4] {'rows','cols'}, dimensions={0}, use_global_device_ids=true | all-gather | bytes 105600 | tf_op jit(solution)/shard_map/all_gather | solution.py:31
  975.8 38.4 %all-gather.11 = f32[32,5,5,32]{3,2,1,0:T(8,128)S(1)} all-gather(f32[1,5,5,32]{3,2,1,0:T(8,128)S(1)} %copy.2744), channel_id=13, replica_groups=mesh['rows'=8,'cols'=4] {'rows','cols'}, dimensions={0}, use_global_device_ids=true | all-gather | bytes 105600 | tf_op jit(solution)/shard_map/all_gather | solution.py:31
  1088.7 47.1 %all-gather.12 = f32[32,5,5,32]{3,2,1,0:T(8,128)} all-gather(f32[1,5,5,32]{3,2,1,0:T(8,128)S(1)} %copy.2798), channel_id=14, replica_groups=mesh['rows'=8,'cols'=4] {'rows','cols'}, dimensions={0}, use_global_device_ids=true | all-gather | bytes 105600 | tf_op jit(solution)/shard_map/all_gather | solution.py:31
  1135.8 41.1 %all-gather.13 = f32[32,5,5,32]{3,2,1,0:T(8,128)} all-gather(f32[1,5,5,32]{3,2,1,0:T(8,128)S(1)} %copy.2802), channel_id=15, replica_groups=mesh['rows'=8,'cols'=4] {'rows','cols'}, dimensions={0}, use_global_device_ids=true | all-gather | bytes 105600 | tf_op jit(solution)/shard_map/all_gather | solution.py:31
  1282.5 45.7 %all-gather.14 = f32[32,5,5,32]{3,2,1,0:T(8,128)S(1)} all-gather(f32[1,5,5,32]{3,2,1,0:T(8,128)S(1)} %copy.2822), channel_id=16, replica_groups=mesh['rows'=8,'cols'=4] {'rows','cols'}, dimensions={0}, use_global_device_ids=true | all-gather | bytes 105600 | tf_op jit(solution)/shard_map/all_gather | solution.py:31
  1328.2 38.4 %all-gather.15 = f32[32,5,5,32]{3,2,1,0:T(8,128)S(1)} all-gather(f32[1,5,5,32]{3,2,1,0:T(8,128)S(1)} %copy.2828), channel_id=17, replica_groups=mesh['rows'=8,'cols'=4] {'rows','cols'}, dimensions={0}, use_global_device_ids=true | all-gather | bytes 105600 | tf_op jit(solution)/shard_map/all_gather | solution.py:31
  1450.1 44.1 %all-gather.17 = f32[32,5,5,32]{3,2,1,0:T(8,128)S(1)} all-gather(f32[1,5,5,32]{3,2,1,0:T(8,128)S(1)} %copy.2852), channel_id=19, replica_groups=mesh['rows'=8,'cols'=4] {'rows','cols'}, dimensions={0}, use_global_device_ids=true | all-gather | bytes 105600 | tf_op jit(solution)/shard_map/all_gather | solution.py:31
  1494.2 38.4 %all-gather.16 = f32[32,5,5,32]{3,2,1,0:T(8,128)S(1)} all-gather(f32[1,5,5,32]{3,2,1,0:T(8,128)S(1)} %copy.2848), channel_id=18, replica_groups=mesh['rows'=8,'cols'=4] {'rows','cols'}, dimensions={0}, use_global_device_ids=true | all-gather | bytes 105600 | tf_op jit(solution)/shard_map/all_gather | solution.py:31
  1572.8 43.0 %all-gather.19 = f32[32,5,5,32]{3,2,1,0:T(8,128)S(1)} all-gather(f32[1,5,5,32]{3,2,1,0:T(8,128)S(1)} %copy.2874), channel_id=21, replica_groups=mesh['rows'=8,'cols'=4] {'rows','cols'}, dimensions={0}, use_global_device_ids=true | all-gather | bytes 105600 | tf_op jit(solution)/shard_map/all_gather | solution.py:31
  1615.8 38.4 %all-gather.18 = f32[32,5,5,32]{3,2,1,0:T(8,128)S(1)} all-gather(f32[1,5,5,32]{3,2,1,0:T(8,128)S(1)} %copy.2870), channel_id=20, replica_groups=mesh['rows'=8,'cols'=4] {'rows','cols'}, dimensions={0}, use_global_device_ids=true | all-gather | bytes 105600 | tf_op jit(solution)/shard_map/all_gather | solution.py:31
  1737.4 44.5 %all-gather.21 = f32[32,5,5,32]{3,2,1,0:T(8,128)S(1)} all-gather(f32[1,5,5,32]{3,2,1,0:T(8,128)S(1)} %copy.2909), channel_id=23, replica_groups=mesh['rows'=8,'cols'=4] {'rows','cols'}, dimensions={0}, use_global_device_ids=true | all-gather | bytes 105600 | tf_op jit(solution)/shard_map/all_gather | solution.py:31
  1781.9 38.4 %all-gather.20 = f32[32,5,5,32]{3,2,1,0:T(8,128)S(1)} all-gather(f32[1,5,5,32]{3,2,1,0:T(8,128)S(1)} %copy.2903), channel_id=22, replica_groups=mesh['rows'=8,'cols'=4] {'rows','cols'}, dimensions={0}, use_global_device_ids=true | all-gather | bytes 105600 | tf_op jit(solution)/shard_map/all_gather | solution.py:31
  1866.3 44.1 %all-gather.22 = f32[32,5,5,32]{3,2,1,0:T(8,128)S(1)} all-gather(f32[1,5,5,32]{3,2,1,0:T(8,128)S(1)} %copy.2929), channel_id=24, replica_groups=mesh['rows'=8,'cols'=4] {'rows','cols'}, dimensions={0}, use_global_device_ids=true | all-gather | bytes 105600 | tf_op jit(solution)/shard_map/all_gather | solution.py:31
  2001.0 43.8 %all-gather.25 = f32[32,5,5,32]{3,2,1,0:T(8,128)S(1)} all-gather(f32[1,5,5,32]{3,2,1,0:T(8,128)S(1)} %copy.2961), channel_id=27, replica_groups=mesh['rows'=8,'cols'=4] {'rows','cols'}, dimensions={0}, use_global_device_ids=true | all-gather | bytes 105600 | tf_op jit(solution)/shard_map/all_gather | solution.py:31
  2044.8 38.4 %all-gather.24 = f32[32,5,5,32]{3,2,1,0:T(8,128)S(1)} all-gather(f32[1,5,5,32]{3,2,1,0:T(8,128)S(1)} %copy.2955), channel_id=26, replica_groups=mesh['rows'=8,'cols'=4] {'rows','cols'}, dimensions={0}, use_global_device_ids=true | all-gather | bytes 105600 | tf_op jit(solution)/shard_map/all_gather | solution.py:31
  2138.6 42.6 %all-gather.26 = f32[32,5,5,32]{3,2,1,0:T(8,128)S(1)} all-gather(f32[1,5,5,32]{3,2,1,0:T(8,128)S(1)} %copy.2981), channel_id=28, replica_groups=mesh['rows'=8,'cols'=4] {'rows','cols'}, dimensions={0}, use_global_device_ids=true | all-gather | bytes 105600 | tf_op jit(solution)/shard_map/all_gather | solution.py:31
  2181.2 38.5 %all-gather.27 = f32[32,5,5,32]{3,2,1,0:T(8,128)S(1)} all-gather(f32[1,5,5,32]{3,2,1,0:T(8,128)S(1)} %copy.2987), channel_id=29, replica_groups=mesh['rows'=8,'cols'=4] {'rows','cols'}, dimensions={0}, use_global_device_ids=true | all-gather | bytes 105600 | tf_op jit(solution)/shard_map/all_gather | solution.py:31
  2329.5 54.1 %reduce-scatter.13.cloned.1.call-done = bf16[32,288]{1,0:T(8,128)(2,1)} async-done(((bf16[256,288]{1,0:T(8,128)(2,1)}), bf16[32,288]{1,0:T(8,128)(2,1)}) %reduce-scatter.13.cloned.1.call-update) | async-done | bytes 18448
  2385.9 61.9 %reduce-scatter.9.cloned.1.call-done = bf16[9,16,64]{2,0,1:T(8,128)(2,1)} async-done(((bf16[9,128,64]{2,0,1:T(8,128)(2,1)}), bf16[9,16,64]{2,0,1:T(8,128)(2,1)}) %reduce-scatter.9.cloned.1.call-update) | async-done | bytes 18448 | tf_op jit(solution)/shard_map/reduce_scatter | solution.py:452
  2449.3 110.7 %all-reduce.16.cloned.1.call-done = (bf16[4,9,128,32]{3,0,1,2:T(4,128)(2,1)}, bf16[2,9,256,64]{3,0,1,2:T(2,128)(2,1)}) async-done(((bf16[4,9,128,32]{3,0,1,2:T(4,128)(2,1)}, bf16[2,9,256,64]{3,0,1,2:T(2,128)(2,1)}), (bf16[4,9,128,32]{3,0,1,2:T(4,128)(2,1)}, bf16[2,9,256,64]{3,0,1,2:T(2,128)(2,1)})) %all-reduce.16.cloned.1.call-update) | async-done | bytes 884752
  2567.3 40.4 %all-reduce.7 = (f32[9,128,9]{1,2,0:T(8,128)S(1)}, f32[]{:T(128)}, f32[2,1152]{1,0:T(2,128)S(1)}) all-reduce(f32[9,128,9]{1,2,0:T(8,128)S(1)} %pad_maximum_fusion.55, f32[]{:T(128)S(6)} %add.2543, f32[2,1152]{1,0:T(2,128)S(1)} %pad_maximum_fusion.115), channel_id=1, replica_groups=mesh['rows'=8,'cols'=4] {'rows','cols'}, use_global_device_ids=true, to_apply=%region_88.89 | all-reduce | flops 12673 | bytes 101384 | tf_op jit(solution)/shard_map/psum | solution.py:401
  2626.2 40.0 %all-reduce.6 = (f32[10]{0:T(128)S(1)}, f32[10]{0:T(128)S(1)}, f32[]{:T(128)}) all-reduce(f32[10]{0:T(128)S(1)} %concatenate.522, f32[10]{0:T(128)S(1)} %concatenate.521, f32[]{:T(128)} %get-tuple-element.3738), channel_id=1, replica_groups=mesh['rows'=8,'cols'=4] {'rows','cols'}, use_global_device_ids=true, to_apply=%region_139.140 | all-reduce | flops 21 | bytes 168 | tf_op jit(solution)/shard_map/psum | solution.py:521
  (2442 shorter events, 1261.0 us)
Async XLA Ops:
  7.2 359.1 %all-gather.33.cloned.1.call-start = ((), (), s32[]{:S(2)}) async-start(), calls=%async_computation.4 | async-start | bytes 1474560 | tf_op jit(solution)/shard_map/all_gather | solution.py:294
  45.7 444.2 %all-gather.35.cloned.1.call-start = ((), (), s32[]{:S(2)}) async-start(), calls=%async_computation.5 | async-start | bytes 4460544 | tf_op jit(solution)/shard_map/all_gather | solution.py:301
  47.1 446.4 %all-gather.37.cloned.1.call-start = ((), (), s32[]{:S(2)}) async-start(), calls=%async_computation.6 | async-start | bytes 1310720 | tf_op jit(solution)/shard_map/all_gather | solution.py:298
  80.8 693.0 %all-gather.39.cloned.1.call-start = ((), (), s32[]{:S(2)}) async-start(), calls=%async_computation.7 | async-start | bytes 2949120 | tf_op jit(solution)/shard_map/all_gather | solution.py:295
  80.9 141.7 %collective-permute-start = (bf16[1,1,64,6]{2,1,3,0:T(2,128)(2,1)S(1)}, bf16[1,1,64,6]{2,1,3,0:T(2,128)(2,1)S(1)}, u32[]{:S(2)}, u32[]{:S(2)}) collective-permute-start(bf16[1,1,64,6]{2,1,3,0:T(2,128)(2,1)S(1)} %get-tuple-element.3754), channel_id=1, source_target_pairs={{0,4},{4,8},{8,12},{12,16},{16,20},{20,24},{24,28},{1,5},{5,9},{9,... | collective-permute-start | bytes 2312 | tf_op jit(solution)/shard_map/ppermute | solution.py:48
  83.7 138.9 %collective-permute-start.1 = (bf16[1,1,64,6]{2,1,3,0:T(2,128)(2,1)S(1)}, bf16[1,1,64,6]{2,1,3,0:T(2,128)(2,1)S(1)}, u32[]{:S(2)}, u32[]{:S(2)}) collective-permute-start(bf16[1,1,64,6]{2,1,3,0:T(2,128)(2,1)S(1)} %get-tuple-element.3755), channel_id=1, source_target_pairs={{4,0},{8,4},{12,8},{16,12},{20,16},{24,20},{28,24},{5,1},{9,5},{13... | collective-permute-start | bytes 2312 | tf_op jit(solution)/shard_map/ppermute | solution.py:51
  125.4 2131.3 %reduce-scatter.11.cloned.1.call-start = ((), (), s32[]{:S(2)}) async-start(), calls=%async_computation.10 | async-start | bytes 1310720 | tf_op jit(solution)/shard_map/reduce_scatter | solution.py:441
  344.5 21.3 collective-permute-start.7
  345.8 20.0 collective-permute-start.6
  499.1 12.0 collective-permute-start.8
  500.5 10.6 collective-permute-start.9
  753.5 15.0 collective-permute-start.16
  755.0 13.6 collective-permute-start.17
  768.6 21.8 collective-permute-start.19
  769.9 20.5 collective-permute-start.18
  1032.1 10.6 collective-permute-start.31
  1033.4 9.3 collective-permute-start.30
  1049.3 8.9 collective-permute-start.32
  1226.4 12.2 collective-permute-start.39
  1227.7 10.9 collective-permute-start.38
  1399.6 868.8 %reduce-scatter.7.cloned.1.call-start = ((), (), s32[]{:S(2)}) async-start(), calls=%async_computation.8 | async-start | bytes 1310720 | tf_op jit(solution)/shard_map/reduce_scatter | solution.py:438
  1420.4 8.4 collective-permute-start.48
  1549.6 9.7 collective-permute-start.55
  1550.9 8.4 collective-permute-start.54
  1672.5 600.0 %all-reduce.18.cloned.1.call-start = ((), (), s32[]{:S(2)}) async-start(), calls=%async_computation.14 | async-start | bytes 7077888
  1696.2 12.2 collective-permute-start.60
  1834.8 8.9 collective-permute-start.64
  1965.0 8.9 collective-permute-start.68
  2109.3 207.4 %all-reduce.14.cloned.1.call-start = ((), (), s32[]{:S(2)}) async-start(), calls=%async_computation.11 | async-start | bytes 327680 | tf_op jit(solution)/shard_map/psum | solution.py:401
  2121.7 261.9 %reduce-scatter.13.cloned.1.call-start = ((), (), s32[]{:S(2)}) async-start(), calls=%async_computation.12 | async-start | bytes 221184
  2265.5 182.4 %reduce-scatter.9.cloned.1.call-start = ((), (), s32[]{:S(2)}) async-start(), calls=%async_computation.9 | async-start | bytes 589824 | tf_op jit(solution)/shard_map/reduce_scatter | solution.py:452
  2270.7 289.2 %all-reduce.16.cloned.1.call-start = ((), (), s32[]{:S(2)}) async-start(), calls=%async_computation.13 | async-start | bytes 4718592
  (483 other events, 4329.8 us)
Sparse Core Ops, SparseCore 0:
  45.8 17.9 all-gather.32
  67.2 67.6 all-gather.34
  136.5 16.0 all-gather.36
  154.0 27.2 all-gather.38
  1399.8 25.5 reduce-scatter.10
  1672.6 25.5 reduce-scatter.6
  2109.4 77.9 all-reduce.17
  2193.6 123.0 all-reduce.13
  2320.5 63.0 reduce-scatter.12
  2386.8 60.9 reduce-scatter.8
  2451.9 108.0 all-reduce.15
where the time goes:
time: 2710 us; the launch traced here: 2690 us
  blocking collectives  1420 us (52%)
  local copies, waits for them, and re-layouts  333 us (12%)
  waiting for transfers between devices  300 us (11%)
  matrix products  278 us (10%)
  starting transfers between devices  155 us (6%)
  other arithmetic  153 us (6%)
  between operations  41.4 us (2%)
    all_gather x28, blocking collectives, entering(): gathered = jax.tree.map(lambda a: lax.all_gather(a, axis), part)  1150 us
    unnamed x14, waiting for transfers between devices  165 us
    dot_general x180, matrix products, conv_taps(): jnp.einsum('nhwc,cd->nhwd', tap_patch(padded, masks, tap, stride), weight...  137 us
    ppermute x40, starting transfers between devices, padded_2(): lax.ppermute(lax.slice_in_dim(block, block.shape[dim] - width, None, axis...  101 us
    unnamed x932, local copies, waits for them, and re-layouts  92.1 us
    reduce_scatter x1, waiting for transfers between devices, per_device(): lax.psum_scatter(by_cols[2].astype(jnp.bfloat16), 'rows', scatter_dimensi...  61.9 us
  transfers between devices with their start and end apart: 91, of which 19 were waited for; matrix products, arithmetic and copies ran while one was open for 20% of the time, Pallas kernels for 0%

commit v1 on v0

--- a/solution.py
+++ b/solution.py
@@ -2,7 +2,10 @@
 
 import jax
 import jax.numpy as jnp
+import numpy as np
 from jax import lax
+from jax.experimental import pallas as pl
+from jax.experimental.pallas import tpu as pltpu
 from jax.sharding import PartitionSpec as P
 
 SLOT = 64
@@ -585,7 +588,1052 @@
     )
 
 
+F32 = jnp.float32
+BF = jnp.bfloat16
+MESH = pl.DeviceIdType.MESH
+NORM_AT = (0, 128, 256, 384, 512, 768, 1024, 1152)
+FILM_AT = {1: 0, 3: 256, 5: 512}
+ROW_OF = (0, 1, -1, 2)
+COL_OF = (-1, 0, 1, 2)
+N_EXCHANGE = 20
+
+
+def phase_tables():
+    by_cell = np.zeros((9, 4, 4, 9), np.float32)
+    by_tile = np.zeros((4, 4, 4, 9), np.float32)
+    for out in range(4):
+        cp_out, rp_out = out // 2, out % 2
+        for cell in range(9):
+            for inp in range(4):
+                a = 2 * (cell // 3 - 1) + inp % 2 - rp_out + 1
+                b = 2 * (cell % 3 - 1) + inp // 2 - cp_out + 1
+                if 0 <= a <= 2 and 0 <= b <= 2:
+                    by_cell[cell, inp, out, 3 * a + b] = 1.0
+        for g in range(4):
+            for r in range(4):
+                a = ROW_OF[r] - rp_out + 1
+                b = COL_OF[g] - cp_out + 1
+                if 0 <= a <= 2 and 0 <= b <= 2:
+                    by_tile[g, r, out, 3 * a + b] = 1.0
+    return by_cell, by_tile
+
+
+def unet_kernel(
+    img_ref,
+    tgt_ref,
+    small_ref,
+    film_ref,
+    norm_ref,
+    low_ref,
+    high_ref,
+    down_ref,
+    up_ref,
+    wi_ref,
+    wit_ref,
+    wh_ref,
+    wht_ref,
+    dlow_ref,
+    dhigh_ref,
+    ddown_ref,
+    dup_ref,
+    dwi_ref,
+    dwh_ref,
+    fgrad_ref,
+    ngrad_ref,
+    loss_ref,
+    imgrad_ref,
+    full_ref,
+    half_ref,
+    work_ref,
+    grad_ref,
+    wide_ref,
+    thin_ref,
+    act_ref,
+    acth_ref,
+    turn_ref,
+    wc_ref,
+    wr_ref,
+    wu_ref,
+    wut_ref,
+    wd_ref,
+    coef_ref,
+    rows_ref,
+    patch_ref,
+    ext_ref,
+    send_ref,
+    recv_ref,
+    send_sem,
+    recv_sem,
+):
+    rr = lax.axis_index("rows")
+    cc = lax.axis_index("cols")
+    core = lax.rem(cc, 2)
+    partner = cc + 1 - 2 * core
+    halo = rr >= 2
+    split = jnp.logical_and(lax.rem(rr, 2) == 1, cc >= 2)
+
+    def flag(cond):
+        return jnp.where(cond, 1.0, 0.0).astype(F32)
+
+    f_halo = flag(halo)
+    f_core1 = flag(core == 1)
+    f_core0 = 1.0 - f_core1
+    f_top = f_halo * f_core1
+    f_bot = f_halo * f_core0
+    f_split = flag(split)
+    f_joined = 1.0 - f_split
+
+    place = lax.broadcasted_iota(jnp.int32, (32, 256), 0)
+    lo_mask = jnp.where(place == 0, 0.0, jnp.where(place == 16, f_joined, 1.0))
+    hi_mask = jnp.where(place == 31, 0.0, jnp.where(place == 15, f_joined, 1.0))
+
+    barrier = pltpu.get_barrier_semaphore()
+    pl.semaphore_signal(barrier, inc=1, device_id={"cols": partner}, device_id_type=MESH)
+    pl.semaphore_wait(barrier, 1)
+
+    def before(x):
+        return pltpu.roll(x, 1, 0) * lo_mask
+
+    def after(x):
+        return pltpu.roll(x, 31, 0) * hi_mask
+
+    def at(i):
+        return pl.ds(pl.multiple_of(i * 32, 32), 32)
+
+    def loop(body, init=0, count=16):
+        return lax.fori_loop(0, count, body, init)
+
+    def dot(a, b):
+        return jnp.dot(a, b, preferred_element_type=F32)
+
+    def dot_nt(a, b):
+        return lax.dot_general(a, b, (((1,), (1,)), ((), ())), preferred_element_type=F32)
+
+    def sigmoid(z):
+        return 0.5 * jnp.tanh(0.5 * z) + 0.5
+
+    def double(v):
+        return jnp.concatenate([v, v], axis=1)
+
+
+    def copy_of(e):
+        return pltpu.make_async_remote_copy(
+            src_ref=send_ref.at[e],
+            dst_ref=recv_ref.at[e],
+            send_sem=send_sem.at[e],
+            recv_sem=recv_sem.at[e],
+            device_id={"cols": partner},
+            device_id_type=MESH,
+        )
+
+    def send(e, row, stats=None):
+        send_ref[e, 0:32, :] = row
+        send_ref[e, 32:40, :] = jnp.zeros((8, 256), F32) if stats is None else stats
+        copy_of(e).start()
+
+    def arrive(e):
+        copy_of(e).wait()
+
+    def edge_full(ref):
+        low = f_core0 * ref[0, 480:512, 128:256] + f_core1 * ref[0, 0:32, 0:128]
+        high = f_core0 * ref[1, 480:512, 128:256] + f_core1 * ref[1, 0:32, 0:128]
+        return jnp.concatenate([low, high], axis=1)
+
+    def edge_cell(ref):
+        return f_core0 * ref[480:512, :] + f_core1 * ref[0:32, :]
+
+    def edge(ref, planes):
+        return edge_full(ref) if planes == 2 else edge_cell(ref.at[0])
+
+
+    def halves(x):
+        return x[0:8] + x[8:16], x[16:24] + x[24:32]
+
+    def gathered(sums, planes):
+        rows = []
+        for s in sums:
+            row = jnp.sum(s, axis=0, keepdims=True)
+            rows.append(double(row[:, 0:128] + row[:, 128:256]) if planes == 2 else row)
+        return jnp.concatenate(rows + [jnp.zeros((4, 256), F32)], axis=0)
+
+    zero8 = jnp.zeros((8, 256), F32)
+
+    def stats_of(x_ref, planes):
+        def body(i, carry):
+            s_l, s_r, q_l, q_r = carry
+            for p in range(planes):
+                x = x_ref[p, at(i), :]
+                a, b = halves(x)
+                c, d = halves(x * x)
+                s_l, s_r, q_l, q_r = s_l + a, s_r + b, q_l + c, q_r + d
+            return s_l, s_r, q_l, q_r
+
+        return gathered(loop(body, (zero8,) * 4), planes)
+
+    def over_slot(block, planes):
+        swapped = jnp.concatenate(
+            [block[1:2], block[0:1], block[3:4], block[2:3], block[4:8]], axis=0
+        )
+        x = block + f_joined * swapped
+        lane = lax.broadcasted_iota(jnp.int32, (8, 256), 1)
+        step = 1
+        while step < (4 if planes == 2 else 8):
+            up = pltpu.roll(x, 256 - step, 1)
+            down = pltpu.roll(x, step, 1)
+            x = x + jnp.where(lax.rem(lane, 2 * step) < step, up, down)
+            step *= 2
+        size = 16.0 if planes == 2 else 8.0
+        count = (16.0 + 16.0 * f_halo) * (16.0 + 16.0 * f_joined) * size
+        return x / count
+
+    def spread(two):
+        return jnp.concatenate(
+            [
+                jnp.broadcast_to(two[0:1], (16, 256)),
+                jnp.broadcast_to(two[1:2], (16, 256)),
+            ],
+            axis=0,
+        )
+
+    def norm_row(k, which):
+        width = NORM_AT[k + 1] - NORM_AT[k] if k < 6 else 128
+        row = norm_ref[which : which + 1, NORM_AT[k] : NORM_AT[k] + width]
+        return double(row) if width == 128 else row
+
+    def film_rows(k, which):
+        if k not in FILM_AT:
+            return jnp.zeros((2, 256), F32)
+        width = 256 if k == 5 else 128
+        base = FILM_AT[k] + which * width
+        two = film_ref[0:2, base : base + width]
+        return double(two) if width == 128 else two
+
+    def norm_ready(k, stats, e, planes):
+        total = over_slot(stats + f_halo * recv_ref[e, 32:40, :], planes)
+        mean = total[0:2]
+        var = total[2:4] - mean * mean
+        inverse = lax.rsqrt(var + EPS_NORM)
+        gain, bias = norm_row(k, 0), norm_row(k, 1)
+        factor = 1.0 + film_rows(k, 0)
+        slope = inverse * gain * factor
+        coef_ref[k, 0] = spread(slope)
+        coef_ref[k, 1] = spread((bias - mean * inverse * gain) * factor + film_rows(k, 1))
+        coef_ref[k, 2] = spread(mean)
+        coef_ref[k, 3] = spread(inverse)
+        rows_ref[k, 0:2, :] = mean
+        rows_ref[k, 2:4, :] = inverse
+
+    def activated(x, k):
+        z = x * coef_ref[k, 0] + coef_ref[k, 1]
+        return z * sigmoid(z)
+
+
+    def put_wide(i, even, odd):
+        for t, g in enumerate((before(odd), even, odd, after(even))):
+            b = g.astype(BF)
+            wide_ref[at(i + 1), 512 * t : 512 * t + 256] = b
+            wide_ref[at(i + 2), 512 * t + 256 : 512 * t + 384] = b[:, 128:256]
+            wide_ref[at(i), 512 * t + 384 : 512 * t + 512] = b[:, 0:128]
+
+    def put_wide_edge(row):
+        even, odd = row[:, 0:128], row[:, 128:256]
+        lo, hi = lo_mask[:, 0:128], hi_mask[:, 0:128]
+        for t, g in enumerate((pltpu.roll(odd, 1, 0) * lo, even, odd, pltpu.roll(even, 31, 0) * hi)):
+            wide_ref[32:64, 512 * t + 256 : 512 * t + 384] = (g * f_top).astype(BF)
+            wide_ref[512:544, 512 * t + 384 : 512 * t + 512] = (g * f_bot).astype(BF)
+
+    def put_thin(i, x):
+        for t, g in enumerate((before(x), x, after(x))):
+            thin_ref[at(i + 1), 256 * t : 256 * t + 256] = g.astype(BF)
+
+    def put_thin_edge(row):
+        for t, g in enumerate((before(row), row, after(row))):
+            thin_ref[0:32, 256 * t : 256 * t + 256] = (g * f_top).astype(BF)
+            thin_ref[544:576, 256 * t : 256 * t + 256] = (g * f_bot).astype(BF)
+
+    def keep_wide(slot):
+        act_ref[slot, 0] = wide_ref[32:544, 512:768]
+        act_ref[slot, 1] = wide_ref[32:544, 1024:1280]
+
+    def keep_thin(slot):
+        acth_ref[slot] = thin_ref[32:544, 256:512]
+
+    def turn_wide(slot):
+        turn_ref[0:256, :] = act_ref[slot, 0].T
+        turn_ref[256:512, :] = act_ref[slot, 1].T
+
+
+    def load_wc(index):
+        for b in range(3):
+            for r in range(4):
+                for rp in range(2):
+                    a = ROW_OF[r] - rp + 1
+                    if 0 <= a <= 2:
+                        wc_ref[
+                            b * 512 + r * 128 : b * 512 + r * 128 + 128, rp * 128 : rp * 128 + 128
+                        ] = low_ref[index, 3 * a + b]
+
+    def load_wr(index):
+        for b in range(3):
+            for r in range(4):
+                for rp in range(2):
+                    a = ROW_OF[r] - rp + 1
+                    if 0 <= a <= 2:
+                        wr_ref[
+                            rp * 128 : rp * 128 + 128, b * 512 + r * 128 : b * 512 + r * 128 + 128
+                        ] = low_ref[index, 8 - 3 * a - b]
+
+    def taps_of(parity, d):
+        if parity == 0:
+            return {-1: (0,), 0: (1, 2)}.get(d, ())
+        return {0: (0, 1), 1: (2,)}.get(d, ())
+
+    def load_up():
+        for cp in range(2):
+            for rp in range(2):
+                for di in (-1, 0, 1):
+                    for dj in (-1, 0, 1):
+                        taps = [3 * a + b for a in taps_of(rp, di) for b in taps_of(cp, dj)]
+                        if not taps:
+                            continue
+                        total = up_ref[taps[0]].astype(F32)
+                        for t in taps[1:]:
+                            total = total + up_ref[t].astype(F32)
+                        low = total.astype(BF)
+                        at_k = (dj + 1 - cp) * 256
+                        wu_ref[cp, di + 1, at_k : at_k + 256, rp * 128 : rp * 128 + 128] = low
+                        row = ROW_OF.index(rp - 2 * di)
+                        col = COL_OF.index(cp - 2 * dj)
+                        wut_ref[:, col * 512 + row * 128 : col * 512 + row * 128 + 128] = low
+
+    def load_down():
+        for b in range(3):
+            for r in range(3):
+                a = ROW_OF[r] + 1
+                wd_ref[b * 512 + r * 128 : b * 512 + r * 128 + 128, :] = down_ref[3 * a + b]
+
+
+    def conv_low(out, weight_nt=False):
+        for cp in range(2):
+            left = wide_ref[32:544, cp * 512 : cp * 512 + 1536]
+            out(cp, dot_nt(left, wr_ref[...]) if weight_nt else dot(left, wc_ref[...]))
+
+    def conv_high(index):
+        total = None
+        for a in range(3):
+            term = dot(
+                thin_ref[32 * a : 32 * a + 512, :],
+                high_ref[index, 3 * a : 3 * a + 3].reshape(768, 256),
+            )
+            total = term if total is None else total + term
+        return total
+
+    def conv_high_back(index):
+        total = None
+        for a in range(3):
+            for b in range(3):
+                term = dot_nt(
+                    thin_ref[32 * a : 32 * a + 512, b * 256 : b * 256 + 256],
+                    high_ref[index, 8 - 3 * a - b],
+                )
+                total = term if total is None else total + term
+        return total
+
+    def grad_low(index, slot):
+        turn_wide(slot)
+        for b in range(3):
+            block = dot(turn_ref[0:256, :], wide_ref[32:544, b * 512 : b * 512 + 512]) + dot(
+                turn_ref[256:512, :], wide_ref[32:544, b * 512 + 512 : b * 512 + 1024]
+            )
+            for a in range(3):
+                first = ROW_OF.index(a - 1) * 128
+                second = ROW_OF.index(a) * 128
+                dlow_ref[index, 8 - 3 * a - b] = (
+                    block[0:128, first : first + 128] + block[128:256, second : second + 128]
+                ).astype(dlow_ref.dtype)
+
+    def grad_high(index, slot):
+        turn_ref[0:256, :] = acth_ref[slot].T
+        for a in range(3):
+            block = dot(turn_ref[0:256, :], thin_ref[32 * a : 32 * a + 512, :])
+            for b in range(3):
+                dhigh_ref[index, 8 - 3 * a - b] = block[:, b * 256 : b * 256 + 256].astype(
+                    dhigh_ref.dtype
+                )
+
+
+    def put_patch(slot, source, row, lanes):
+        ext_ref[0:32, :] = row * f_top
+        ext_ref[544:576, :] = row * f_bot
+
+        def fill(i, carry):
+            ext_ref[at(i + 1), :] = source[at(i), :]
+            return carry
+
+        loop(fill)
+
+        def body(i, carry):
+            total = None
+            for di in (-1, 0, 1):
+                x = ext_ref[at(i + 1 + di), :]
+                for dj, g in enumerate((before(x), x, after(x))):
+                    shift = ((di + 1) * 3 + dj) * lanes
+                    term = pltpu.roll(g, shift, 1) if shift else g
+                    total = term if total is None else total + term
+            patch_ref[slot, at(i), :] = total.astype(BF)
+            return carry
+
+        loop(body)
+
+
+    def norm_back_start(k, x_ref, planes):
+        def body(i, carry):
+            s_l, s_r, q_l, q_r = carry
+            for p in range(planes):
+                x = x_ref[p, at(i), :]
+                z = x * coef_ref[k, 0] + coef_ref[k, 1]
+                s = sigmoid(z)
+                d = work_ref[p, at(i), :] * (s * (1.0 + z * (1.0 - s)))
+                work_ref[p, at(i), :] = d
+                a, b = halves(d)
+                c, e = halves(d * ((x - coef_ref[k, 2]) * coef_ref[k, 3]))
+                s_l, s_r, q_l, q_r = s_l + a, s_r + b, q_l + c, q_r + e
+            return s_l, s_r, q_l, q_r
+
+        return gathered(loop(body, (zero8,) * 4), planes)
+
+    def norm_back_ready(k, stats, e, planes):
+        gain, bias = norm_row(k, 0), norm_row(k, 1)
+        factor = 1.0 + film_rows(k, 0)
+        width = 128 if planes == 2 else 256
+        one, two = stats[0:2], stats[2:4]
+        dgain, dbias = factor * two, factor * one
+        o = NORM_AT[k]
+        ngrad_ref[0:1, o : o + width] = (dgain[0:1] + dgain[1:2])[:, 0:width]
+        ngrad_ref[1:2, o : o + width] = (dbias[0:1] + dbias[1:2])[:, 0:width]
+        if k in FILM_AT:
+            f = FILM_AT[k]
+            fgrad_ref[0:2, f : f + width] = (gain * two + bias * one)[:, 0:width]
+            fgrad_ref[0:2, f + width : f + 2 * width] = one[:, 0:width]
+        both = stats + f_halo * recv_ref[e, 32:40, :]
+        kk = gain * factor
+        scaled = jnp.concatenate([kk * both[0:2], kk * both[2:4], both[4:8]], axis=0)
+        total = over_slot(scaled, planes)
+        mean, inverse = rows_ref[k, 0:2, :], rows_ref[k, 2:4, :]
+        second = -inverse * inverse * total[2:4]
+        third = -inverse * total[0:2] - mean * second
+        coef_ref[k, 4] = spread(inverse * kk)
+        coef_ref[k, 5] = spread(second)
+        coef_ref[k, 6] = spread(third)
+
+    def back_value(k, d, x):
+        return d * coef_ref[k, 4] + x * coef_ref[k, 5] + coef_ref[k, 6]
+
+
+    def zero(i, carry):
+        wc_ref[at(i), :] = jnp.zeros((32, 256), BF)
+        return carry
+
+    loop(zero, count=48)
+    wr_ref[...] = jnp.zeros(wr_ref.shape, BF)
+    for cp in range(2):
+        for di in range(3):
+            wu_ref[cp, di] = jnp.zeros((512, 256), BF)
+    for b in range(3):
+        wd_ref[b * 512 + 384 : b * 512 + 512, :] = jnp.zeros((128, 256), BF)
+
+    send(0, edge_cell(img_ref))
+    load_wc(0)
+    load_up()
+    load_down()
+    arrive(0)
+    put_patch(0, img_ref, recv_ref[0, 0:32, :], 24)
+    for cp in range(2):
+        full_ref[0, cp] = dot(patch_ref[0], wi_ref[cp])
+
+    def fwd_norm_full(k, source, e):
+        stats = stats_of(source, 2)
+        send(e, edge_full(source), stats)
+        return stats
+
+    def fwd_apply_full(k, source, stats, e):
+        arrive(e)
+        norm_ready(k, stats, e, 2)
+
+        def body(i, carry):
+            put_wide(
+                i,
+                activated(source[0, at(i), :], k),
+                activated(source[1, at(i), :], k),
+            )
+            return carry
+
+        loop(body)
+        put_wide_edge(activated(recv_ref[e, 0:32, :], k))
+
+    for index in range(2):
+        h = full_ref.at[2 * index]
+        mid = full_ref.at[2 * index + 1]
+        out = full_ref.at[2 * index + 2]
+        k = 2 * index
+        stats = fwd_norm_full(k, h, 1 + k)
+        if index:
+            load_wc(2)
+        fwd_apply_full(k, h, stats, 1 + k)
+        keep_wide(k)
+
+        def put_mid(cp, value, mid=mid):
+            mid[cp] = value
+
+        conv_low(put_mid)
+        stats = fwd_norm_full(k + 1, mid, 2 + k)
+        load_wc(2 * index + 1)
+        fwd_apply_full(k + 1, mid, stats, 2 + k)
+        keep_wide(k + 1)
+
+        def put_out(cp, value, h=h, out=out):
+            out[cp] = h[cp] + value
+
+        conv_low(put_out)
+
+    skip = full_ref.at[4]
+    send(5, edge_full(skip))
+
+    def skip_body(i, carry):
+        put_wide(i, skip[0, at(i), :], skip[1, at(i), :])
+        return carry
+
+    loop(skip_body)
+    arrive(5)
+    put_wide_edge(recv_ref[5, 0:32, :])
+    keep_wide(4)
+    half_ref[0, 0] = dot(wide_ref[32:544, 0:1536], wd_ref[...])
+
+    def fwd_half(k, source, e):
+        stats = stats_of(source, 1)
+        send(e, edge_cell(source.at[0]), stats)
+        arrive(e)
+        norm_ready(k, stats, e, 1)
+
+        def body(i, carry):
+            put_thin(i, activated(source[0, at(i), :], k))
+            return carry
+
+        loop(body)
+        put_thin_edge(activated(recv_ref[e, 0:32, :], k))
+
+    fwd_half(4, half_ref.at[0], 6)
+    keep_thin(0)
+    half_ref[1, 0] = conv_high(0)
+    fwd_half(5, half_ref.at[1], 7)
+    keep_thin(1)
+    half_ref[2, 0] = half_ref[0, 0] + conv_high(1)
+    deep = half_ref.at[2]
+    send(8, edge_cell(deep.at[0]))
+
+    def deep_body(i, carry):
+        put_thin(i, deep[0, at(i), :])
+        return carry
+
+    loop(deep_body)
+    arrive(8)
+    put_thin_edge(recv_ref[8, 0:32, :])
+    keep_thin(2)
+    merged = full_ref.at[5]
+    for cp in range(2):
+        total = skip[cp]
+        for di in range(3):
+            total = total + dot(
+                thin_ref[32 * di : 32 * di + 512, cp * 256 : cp * 256 + 512], wu_ref[cp, di]
+            )
+        merged[cp] = total
+
+    stats = fwd_norm_full(6, merged, 9)
+    fwd_apply_full(6, merged, stats, 9)
+    keep_wide(5)
+    work_ref[0] = jnp.concatenate(
+        [dot(wide_ref[32:544, :], wh_ref[...]), jnp.zeros((512, 128), F32)], axis=1
+    )
+
+    live = spread(small_ref[0:2, :])
+    weight = small_ref[2:3, :]
+
+    def loss_body(i, carry):
+        diff = work_ref[0, at(i), :] - tgt_ref[at(i), :]
+        half = live * diff
+        work_ref[0, at(i), :] = (half * weight).astype(BF).astype(F32)
+        return carry + half * diff
+
+    lost = loop(loss_body, jnp.zeros((32, 256), F32))
+    loss_ref[...] = jnp.sum(lost.reshape(4, 8, 256), axis=0)
+
+
+    send(10, edge_cell(work_ref.at[0]))
+    arrive(10)
+    put_patch(1, work_ref.at[0], recv_ref[10, 0:32, :], 12)
+    for cp in range(2):
+        work_ref[cp] = dot(patch_ref[1], wht_ref[cp])
+    stats = norm_back_start(6, merged, 2)
+    send(11, edge_full(work_ref), stats)
+    turn_ref[0:256, :] = patch_ref[1].T
+    for cp in range(2):
+        dwh_ref[cp] = dot(turn_ref[0:256, :], act_ref[5, cp])
+    arrive(11)
+    norm_back_ready(6, stats, 11, 2)
+
+    def head_body(i, carry):
+        pair = []
+        for p in range(2):
+            g = back_value(6, work_ref[p, at(i), :], merged[p, at(i), :])
+            grad_ref[p, at(i), :] = g
+            pair.append(g)
+        put_wide(i, pair[0], pair[1])
+        return carry
+
+    loop(head_body)
+    put_wide_edge(back_value(6, recv_ref[11, 0:32, :], recv_ref[9, 0:32, :]))
+
+    hgrad = half_ref.at[3]
+    hgrad[0] = dot_nt(wide_ref[32:544, :], wut_ref[...])
+    send(12, edge_cell(hgrad.at[0]))
+    turn_ref[0:256, :] = acth_ref[2].T
+    for b in range(3):
+        cols = {0: (3, 2), 1: (1, 2), 2: (1, 0)}[b]
+        block = dot(turn_ref[0:256, :], wide_ref[32:544, cols[0] * 512 : cols[0] * 512 + 512]) + dot(
+            turn_ref[0:256, :], wide_ref[32:544, cols[1] * 512 : cols[1] * 512 + 512]
+        )
+        for a in range(3):
+            one, two = {0: (3, 1), 1: (0, 1), 2: (0, 2)}[a]
+            dup_ref[3 * a + b] = (
+                block[:, one * 128 : one * 128 + 128] + block[:, two * 128 : two * 128 + 128]
+            ).astype(dup_ref.dtype)
+
+    def deep_grad(i, carry):
+        put_thin(i, hgrad[0, at(i), :])
+        return carry
+
+    loop(deep_grad)
+    arrive(12)
+    put_thin_edge(recv_ref[12, 0:32, :])
+    work_ref[0] = conv_high_back(1)
+    stats = norm_back_start(5, half_ref.at[1], 1)
+    send(13, edge_cell(work_ref.at[0]), stats)
+    grad_high(1, 1)
+    arrive(13)
+    norm_back_ready(5, stats, 13, 1)
+
+    def mid_grad(i, carry):
+        put_thin(i, back_value(5, work_ref[0, at(i), :], half_ref[1, 0, at(i), :]))
+        return carry
+
+    loop(mid_grad)
+    put_thin_edge(back_value(5, recv_ref[13, 0:32, :], recv_ref[7, 0:32, :]))
+    work_ref[0] = conv_high_back(0)
+    stats = norm_back_start(4, half_ref.at[0], 1)
+    send(14, edge_cell(work_ref.at[0]), stats)
+    grad_high(0, 0)
+    arrive(14)
+    norm_back_ready(4, stats, 14, 1)
+
+    def first_grad(i, carry):
+        put_thin(
+            i, hgrad[0, at(i), :] + back_value(4, work_ref[0, at(i), :], half_ref[0, 0, at(i), :])
+        )
+        return carry
+
+    loop(first_grad)
+    put_thin_edge(
+        recv_ref[12, 0:32, :] + back_value(4, recv_ref[14, 0:32, :], recv_ref[6, 0:32, :])
+    )
+
+    for cp in range(2):
+        for rp in range(2):
+            total = None
+            for di in range(1 + rp):
+                for dj in range(1 + cp):
+                    a = 0 if di else 1 + rp
+                    b = 0 if dj else 1 + cp
+                    term = dot_nt(
+                        thin_ref[32 * (1 + di) : 32 * (1 + di) + 512, (1 + dj) * 256 : (2 + dj) * 256],
+                        down_ref[3 * a + b],
+                    )
+                    total = term if total is None else total + term
+            grad_ref[cp, :, rp * 128 : rp * 128 + 128] = (
+                grad_ref[cp, :, rp * 128 : rp * 128 + 128] + total
+            )
+    send(15, edge_full(grad_ref))
+    turn_wide(4)
+    for cp in range(2):
+        for rp in range(2):
+            for di in range(1 + rp):
+                for dj in range(1 + cp):
+                    a = 0 if di else 1 + rp
+                    b = 0 if dj else 1 + cp
+                    at_row = cp * 256 + rp * 128
+                    ddown_ref[3 * a + b] = dot(
+                        turn_ref[at_row : at_row + 128, :],
+                        thin_ref[32 * (1 + di) : 32 * (1 + di) + 512, (1 + dj) * 256 : (2 + dj) * 256],
+                    ).astype(ddown_ref.dtype)
+
+    def put_work(cp, value):
+        work_ref[cp] = value
+
+    edge_grad = None
+    for index in (1, 0):
+        h = full_ref.at[2 * index]
+        mid = full_ref.at[2 * index + 1]
+        k = 2 * index
+        e = 16 if index else 18
+        load_wr(k + 1)
+        if index:
+
+            def out_grad(i, carry):
+                put_wide(i, grad_ref[0, at(i), :], grad_ref[1, at(i), :])
+                return carry
+
+            loop(out_grad)
+            arrive(15)
+            edge_grad = recv_ref[15, 0:32, :]
+            put_wide_edge(edge_grad)
+        conv_low(put_work, True)
+        stats = norm_back_start(k + 1, mid, 2)
+        send(e, edge_full(work_ref), stats)
+        grad_low(k + 1, k + 1)
+        load_wr(k)
+        arrive(e)
+        norm_back_ready(k + 1, stats, e, 2)
+
+        def mid_body(i, carry, mid=mid, k=k):
+            put_wide(
+                i,
+                back_value(k + 1, work_ref[0, at(i), :], mid[0, at(i), :]),
+                back_value(k + 1, work_ref[1, at(i), :], mid[1, at(i), :]),
+            )
+            return carry
+
+        loop(mid_body)
+        put_wide_edge(back_value(k + 1, recv_ref[e, 0:32, :], recv_ref[k + 2, 0:32, :]))
+        conv_low(put_work, True)
+        stats = norm_back_start(k, h, 2)
+        send(e + 1, edge_full(work_ref), stats)
+        grad_low(k, k)
+        arrive(e + 1)
+        norm_back_ready(k, stats, e + 1, 2)
+
+        def in_body(i, carry, h=h, k=k):
+            pair = []
+            for p in range(2):
+                g = grad_ref[p, at(i), :] + back_value(k, work_ref[p, at(i), :], h[p, at(i), :])
+                grad_ref[p, at(i), :] = g
+                pair.append(g)
+            put_wide(i, pair[0], pair[1])
+            return carry
+
+        loop(in_body)
+        edge_grad = edge_grad + back_value(k, recv_ref[e + 1, 0:32, :], recv_ref[k + 1, 0:32, :])
+        put_wide_edge(edge_grad)
+
+    imgrad_ref[...] = dot(wide_ref[32:544, :], wit_ref[...])
+    turn_ref[0:256, :] = patch_ref[0].T
+    for cp in range(2):
+        dwi_ref[cp] = dot(turn_ref[0:256, :], wide_ref[32:544, 512 + cp * 512 : 768 + cp * 512])
+
+
+def unet(*operands):
+    outs = (
+        jax.ShapeDtypeStruct((4, 9, 128, 128), BF),
+        jax.ShapeDtypeStruct((2, 9, 256, 256), BF),
+        jax.ShapeDtypeStruct((9, 128, 256), BF),
+        jax.ShapeDtypeStruct((9, 256, 128), BF),
+        jax.ShapeDtypeStruct((2, 256, 256), F32),
+        jax.ShapeDtypeStruct((2, 256, 256), F32),
+        jax.ShapeDtypeStruct((2, 1024), F32),
+        jax.ShapeDtypeStruct((2, 1152), F32),
+        jax.ShapeDtypeStruct((8, 256), F32),
+        jax.ShapeDtypeStruct((512, 128), F32),
+    )
+    vmem = pl.BlockSpec(memory_space=pltpu.VMEM)
+    return pl.pallas_call(
+        unet_kernel,
+        out_shape=outs,
+        in_specs=[vmem] * len(operands),
+        out_specs=[vmem] * len(outs),
+        scratch_shapes=[
+            pltpu.VMEM((6, 2, 512, 256), F32),
+            pltpu.VMEM((4, 1, 512, 256), F32),
+            pltpu.VMEM((2, 512, 256), F32),
+            pltpu.VMEM((2, 512, 256), F32),
+            pltpu.VMEM((576, 2048), BF),
+            pltpu.VMEM((576, 768), BF),
+            pltpu.VMEM((6, 2, 512, 256), BF),
+            pltpu.VMEM((3, 512, 256), BF),
+            pltpu.VMEM((512, 512), BF),
+            pltpu.VMEM((1536, 256), BF),
+            pltpu.VMEM((256, 1536), BF),
+            pltpu.VMEM((2, 3, 512, 256), BF),
+            pltpu.VMEM((256, 2048), BF),
+            pltpu.VMEM((1536, 256), BF),
+            pltpu.VMEM((7, 7, 32, 256), F32),
+            pltpu.VMEM((7, 8, 256), F32),
+            pltpu.VMEM((2, 512, 256), BF),
+            pltpu.VMEM((576, 256), F32),
+            pltpu.VMEM((N_EXCHANGE, 40, 256), F32),
+            pltpu.VMEM((N_EXCHANGE, 40, 256), F32),
+            pltpu.SemaphoreType.DMA((N_EXCHANGE,)),
+            pltpu.SemaphoreType.DMA((N_EXCHANGE,)),
+        ],
+        compiler_params=pltpu.CompilerParams(
+            collective_id=1, has_side_effects=True, vmem_limit_bytes=58 * 1024 * 1024
+        ),
+        name="unet",
+    )(*operands)
+
+
+def strip_moves():
+    left, right = [], []
+    for r in range(8):
+        for c in range(4):
+            pair = ((r + 1) // 2) % 4
+            core = (r + 1) % 2
+            target = (pair * 2 + c // 2) * 4 + (c % 2) * 2 + core
+            right.append((r * 4 + c, target))
+            left.append((r * 4 + (c + 1) % 4, target))
+    return left, right
+
+
+def cells_of(block):
+    rows, cols, width = block.shape
+    x = block.reshape(rows // 2, 2, cols // 2, 2, width)
+    return jnp.transpose(x, (0, 2, 3, 1, 4)).reshape(rows // 2, cols // 2, 4 * width)
+
+
+def pixels_of(cells):
+    rows, cols, width = cells.shape
+    x = cells.reshape(rows, cols, 2, 2, width // 4)
+    return jnp.transpose(x, (0, 3, 1, 2, 4)).reshape(2 * rows, 2 * cols, width // 4)
+
+
+BOTH = ("rows", "cols")
+
+
+def flip_t(w):
+    return jnp.swapaxes(w[::-1], 1, 2)
+
+
+def per_device_strips(
+    image_pair,
+    noise_target,
+    timesteps,
+    text_pooled,
+    slot_live,
+    *params,
+):
+    weights, firsts, seconds = params[0::3], params[1::3], params[2::3]
+    edge_w, low_w, high_w, down_w, up_w, cond_w, film_w, norm_w = weights
+    rr, cc = lax.axis_index("rows"), lax.axis_index("cols")
+    by_cell, by_tile = phase_tables()
+    moves_left, moves_right = strip_moves()
+
+    block = jnp.concatenate(
+        [cells_of(image_pair[0].astype(F32)), cells_of(noise_target[0])], axis=-1
+    )
+    left = lax.ppermute(block[:, 16:], BOTH, moves_right)
+    right = lax.ppermute(block[:, :16], BOTH, moves_left)
+    strip = jnp.concatenate([left, right], axis=1).reshape(512, 36)
+    img = jnp.pad(strip[:, 0:24], ((0, 0), (0, 232)))
+    tgt = jnp.pad(strip[:, 24:36], ((0, 0), (0, 244)))
+
+    pair, core = rr // 2, lax.rem(cc, 2)
+    col = lax.rem(rr, 2) * 2 + cc // 2
+    slot_row = jnp.where(pair == 0, 4 * (1 - core), pair)
+    slot_left = slot_row * 5 + col + 1
+    slot_right = slot_row * 5 + jnp.where(col == 3, 0, col + 1)
+    slots = jnp.stack([slot_left, slot_right])
+
+    shards = [low_w, high_w, down_w, up_w]
+    flat = [w.astype(BF).reshape(-1, 128) for w in shards]
+    sizes = [f.shape[0] for f in flat]
+    every = lax.all_gather(jnp.concatenate(flat, axis=0), BOTH, axis=0, tiled=False)
+    starts = np.cumsum([0] + sizes)
+
+    def whole(k, shape):
+        part = every[:, starts[k] : starts[k + 1]].reshape((8, 4) + shape)
+        n = len(shape)
+        order = tuple(range(2, n)) + (0, n, 1, n + 1)
+        x = jnp.transpose(part, order)
+        return x.reshape(shape[:-2] + (8 * shape[-2], 4 * shape[-1]))
+
+    low = whole(0, low_w.shape)
+    high = whole(1, high_w.shape)
+    down = whole(2, down_w.shape)
+    up = whole(3, up_w.shape)
+
+    joined = jnp.concatenate([time_embed(timesteps).astype(BF), text_pooled], axis=-1)[0].reshape(25, -1)
+    pre_own = jnp.dot(joined, cond_w.astype(BF), preferred_element_type=F32)
+    pre = lax.all_gather(pre_own, BOTH, axis=1, tiled=True)
+    cond = jax.nn.silu(pre).astype(BF)
+    film_rows, film_cols = film_w.shape
+    cond_own = lax.dynamic_slice_in_dim(cond, rr * film_rows, film_rows, 1)
+    film_low = film_w.astype(BF)
+    film_part = jnp.dot(cond_own, film_low, preferred_element_type=F32)
+    film = lax.all_gather(lax.psum(film_part, "rows"), "cols", axis=1, tiled=True)
+    own_film = jnp.take(film, slots, axis=0)
+
+    live_slots = slot_live[0].astype(F32)
+    side = np.array([32, 64, 64, 64, 32], np.float32)
+    count = 3.0 * jnp.sum(live_slots * (side[:, None] * side[None, :]))
+    own_live = jnp.take(live_slots.reshape(25), slots)
+    small = jnp.concatenate([own_live, (2.0 / count)[None], jnp.zeros((5,), F32)])
+    small = jnp.broadcast_to(small[:, None], (8, 256))
+
+    edge_low = edge_w.astype(BF)
+    inconv = jnp.swapaxes(edge_low[:, :, 0:6], 1, 2)
+    head = edge_low[:, :, 6:9]
+    cell_tab = by_cell.astype(jnp.bfloat16)
+    tile_tab = by_tile.astype(jnp.bfloat16)
+
+    def by_cells(w):
+        x = jnp.einsum("oqpt,tcd->oqcpd", cell_tab, w)
+        x = x.reshape(-1, 2, 256)
+        return jnp.transpose(jnp.pad(x, ((0, 256 - x.shape[0]), (0, 0), (0, 0))), (1, 0, 2))
+
+    def by_tiles(w):
+        x = jnp.einsum("grpt,tcd->grcpd", tile_tab, w).reshape(2048, -1)
+        return jnp.pad(x, ((0, 0), (0, 128 - x.shape[1])))
+
+    outs = unet(
+        img,
+        tgt,
+        small,
+        own_film,
+        norm_w,
+        low,
+        high,
+        down,
+        up,
+        by_cells(inconv),
+        by_tiles(flip_t(inconv)),
+        by_tiles(head),
+        by_cells(flip_t(head)),
+    )
+    dlow, dhigh, ddown, dup, dwi, dwh, fgrad, ngrad, lost, imgrad = outs
+
+    back = (imgrad[:, 0:24] * (count)).reshape(16, 32, 24)
+    back_right = lax.ppermute(back[:, :16], BOTH, [(t, s) for s, t in moves_right])
+    back_left = lax.ppermute(back[:, 16:], BOTH, [(t, s) for s, t in moves_left])
+    image_grad = pixels_of(jnp.concatenate([back_left, back_right], axis=1))[None]
+
+    def fold(x, width):
+        x = jnp.transpose(x, (1, 0, 2))[: 36 * width].reshape(9, 4, width, 4, 128)
+        return jnp.einsum("oqpt,oqcpd->tcd", by_cell, x, precision=HIGH)
+
+    grad_in = fold(dwi, 6)
+    grad_head = fold(dwh, 3)[::-1]
+    edge_local = jnp.concatenate([jnp.swapaxes(grad_in, 1, 2), jnp.swapaxes(grad_head, 1, 2)], axis=2)
+    spot = (jnp.arange(25)[:, None] == slots[None, :]).astype(F32)
+    film_local = jnp.dot(spot, fgrad, precision=HIGH)
+    pieces = [film_local.reshape(-1), edge_local.reshape(-1), ngrad.reshape(-1), jnp.sum(lost).reshape(1)]
+    lens = [p.shape[0] for p in pieces]
+    total = lax.psum(jnp.concatenate(pieces), BOTH)
+    ends = np.cumsum([0] + lens)
+    film_sum = total[ends[0] : ends[1]].reshape(25, 1024)
+    edge_sum = total[ends[1] : ends[2]].reshape(9, 128, 9)
+    norm_sum = total[ends[2] : ends[3]].reshape(2, 1152)
+    loss_sum = total[ends[3]]
+
+    film_mine = lax.dynamic_slice_in_dim(film_sum, cc * film_cols, film_cols, 1)
+    film_own = lax.dot_general(
+        cond_own.astype(F32), film_mine, (((0,), (0,)), ((), ())), precision=HIGH
+    )
+    gc_part = lax.dot_general(
+        film_mine, film_low.astype(F32), (((1,), (1,)), ((), ())), precision=HIGH
+    )
+    gc = lax.psum_scatter(gc_part, "cols", scatter_dimension=1, tiled=True) * silu_grad(pre_own)
+    cond_grad = lax.dot_general(joined.astype(F32), gc, (((0,), (0,)), ((), ())), precision=HIGH)
+
+    def dealt(g, shape):
+        n = len(shape)
+        lead = shape[:-2]
+        x = g.reshape(lead + (8, shape[-2], 4, shape[-1]))
+        m = len(lead)
+        x = jnp.transpose(x, (m, m + 2) + tuple(range(m)) + (m + 1, m + 3))
+        return x.reshape(32, -1, 128)
+
+    packed = jnp.concatenate(
+        [dealt(g, w.shape) for g, w in zip((dlow, dhigh, ddown, dup), shards)], axis=1
+    )
+    mine = lax.psum_scatter(packed, BOTH, scatter_dimension=0, tiled=False).astype(F32)
+    own = [mine[starts[k] : starts[k + 1]].reshape(w.shape) for k, w in enumerate(shards)]
+    grads = (edge_sum, own[0], own[1], own[2], own[3], cond_grad, film_own, norm_sum)
+    results, clip_norm = lamb(weights, firsts, seconds, grads)
+    return tuple(results) + (loss_sum, count, clip_norm, image_grad)
+
+
+def lamb(weights, firsts, seconds, grads):
+    sharded = (1, 2, 3, 4, 5, 6)
+    stacked = (1, 2)
+    owned_sq = sum((jnp.sum(grads[k] * grads[k]) for k in sharded))
+    shared_sq = sum((jnp.sum(grads[k] * grads[k]) for k in range(8) if k not in sharded))
+    clip_norm = jnp.sqrt(lax.psum(owned_sq, BOTH) + shared_sq)
+    factor = jnp.minimum(1.0, CLIP_AT / clip_norm)
+    clipped, moments, updates = ([], [], [])
+    for k in range(8):
+        grad = grads[k] * factor
+        first_new = BETA_ONE * firsts[k] + (1.0 - BETA_ONE) * grad
+        second_new = BETA_TWO * seconds[k] + (1.0 - BETA_TWO) * grad * grad
+        first_hat = first_new / (1.0 - BETA_ONE**STEP)
+        second_hat = second_new / (1.0 - BETA_TWO**STEP)
+        clipped.append(grad)
+        moments.append(second_new)
+        updates.append(first_hat / (jnp.sqrt(second_hat) + EPS_ADAM) + DECAY * weights[k])
+
+    def matrix_squares(values, k):
+        if k in stacked:
+            return jnp.sum(values * values, axis=tuple(range(1, values.ndim)))
+        return jnp.sum(values * values).reshape(1)
+
+    sums = lax.psum(
+        jnp.stack(
+            [
+                jnp.concatenate([matrix_squares(weights[k], k) for k in sharded]),
+                jnp.concatenate([matrix_squares(updates[k], k) for k in sharded]),
+            ]
+        ),
+        BOTH,
+    )
+    ratios = jnp.sqrt(sums[0]) / jnp.sqrt(sums[1])
+    position = 0
+    results = []
+    for k in range(8):
+        if k in sharded:
+            span = weights[k].shape[0] if k in stacked else 1
+            ratio = ratios[position : position + span]
+            position += span
+            ratio = (
+                ratio.reshape((span,) + (1,) * (weights[k].ndim - 1)) if k in stacked else ratio[0]
+            )
+        elif k == 0:
+            part = (jnp.arange(9) < 6)[None, None, :]
+            other = jnp.logical_not(part)
+            weight_sq_two = weights[k] * weights[k]
+            update_sq_two = updates[k] * updates[k]
+            ratio_in = jnp.sqrt(jnp.sum(jnp.where(part, weight_sq_two, 0.0))) / jnp.sqrt(
+                jnp.sum(jnp.where(part, update_sq_two, 0.0))
+            )
+            ratio_out = jnp.sqrt(jnp.sum(jnp.where(other, weight_sq_two, 0.0))) / jnp.sqrt(
+                jnp.sum(jnp.where(other, update_sq_two, 0.0))
+            )
+            ratio = jnp.where(part, ratio_in, ratio_out)
+        else:
+            ratio = jnp.sqrt(jnp.sum(weights[k] * weights[k])) / jnp.sqrt(
+                jnp.sum(updates[k] * updates[k])
+            )
+        results.extend([clipped[k], moments[k], weights[k] - RATE * ratio * updates[k]])
+    return results, clip_norm
+
+
 def solution(mesh):
+    strips = mesh.shape["rows"] == 8 and mesh.shape["cols"] == 4
     placed = (
         P(None, "rows", "cols", None),
         P(None, "rows", "cols", None),
@@ -618,7 +1666,7 @@
         P(),
     )
     return jax.shard_map(
-        per_device,
+        per_device_strips if strips else per_device,
         mesh=mesh,
         in_specs=placed,
         out_specs=(

time: 2710 us -> 679 us (0.25)
  blocking collectives: 1420 us -> 162 us
  matrix products: 278 us -> 8.31 us
  local copies, waits for them, and re-layouts: 333 us -> 143 us
  starting transfers between devices: 155 us -> 16.7 us
  waiting for transfers between devices: 300 us -> 187 us
  other arithmetic: 153 us -> 55.1 us
  Pallas kernels: 0 us -> 69.5 us
    all_gather x35 -> x2, blocking collectives: 1340 us -> 49.1 us  [the longest x1 42.8 us: per_device_strips(): pre = lax.all_gather(pre_own, BOTH, axis=1, tiled=True)]
    dot_general x413 -> x12, matrix products: 278 us -> 8.31 us  [the longest x1 1.64 us: per_device_strips(): lax.dot_general(film_mine, film_low.astype(F32), (((1,), (1,)), ((), ()))...]
    unnamed x14 -> x4, waiting for transfers between devices: 165 us -> 0.07 us
    ppermute x80 -> x4, starting transfers between devices: 154 us -> 16.5 us  [the longest x1 6.64 us: per_device_strips(): right = lax.ppermute(block[:, :16], BOTH, moves_left)]
    unnamed x932 -> x82, local copies, waits for them, and re-layouts: 92.1 us -> 3.31 us
    reshape x1 -> x40, local copies, waits for them, and re-layouts: 2.57 us -> 83.9 us  [the longest x8 25.2 us: dealt(): x = g.reshape(lead + (8, shape[-2], 4, shape[-1]))]
    mul x50 -> x7, local copies, waits for them, and re-layouts: 76.7 us -> 0.96 us  [the longest x6 0.88 us: lamb(): grad = grads[k] * factor]
    pallas_call x0 -> x1, Pallas kernels: none -> 69.5 us  [unet(): pl.pallas_call(unet_kernel, out_shape=outs, in_specs=[vmem] * len(operand...]
  transfers between devices with their start and end apart: 91 -> 8, of which waited for: 19 -> 3; matrix products, arithmetic and copies ran while one was open for 20% -> 11% of each run, Pallas kernels for 0% -> 0%
where the time goes in v1:
time: 679 us; the launch traced here: 672 us
  waiting for transfers between devices  187 us (28%)
  blocking collectives  162 us (24%)
  local copies, waits for them, and re-layouts  143 us (21%)
  Pallas kernels  69.5 us (10%)
  other arithmetic  55.1 us (8%)
  between operations  30.2 us (4%)
  starting transfers between devices  16.7 us (2%)
  matrix products  8.31 us (1%)
    reduce_scatter x1, waiting for transfers between devices, per_device_strips(): lax.psum_scatter(packed, BOTH, scatter_dimension=0, tiled=False).astype(F32)  104 us
    psum x1, waiting for transfers between devices, per_device_strips(): total = lax.psum(jnp.concatenate(pieces), BOTH)  76.8 us
    pallas_call x1, Pallas kernels, unet(): pl.pallas_call(unet_kernel, out_shape=outs, in_specs=[vmem] * len(operand...  69.5 us
    all_gather x1, blocking collectives, per_device_strips(): pre = lax.all_gather(pre_own, BOTH, axis=1, tiled=True)  42.8 us
    psum x1, blocking collectives, lamb(): clip_norm = jnp.sqrt(lax.psum(owned_sq, BOTH) + shared_sq)  40 us
    psum x1, blocking collectives, lamb(): lax.psum(jnp.stack([jnp.concatenate([matrix_squares(weights[k], k) for k...  39.5 us
    psum x1, blocking collectives, per_device_strips(): lax.psum(film_part, 'rows')  33.3 us
    transpose x4, local copies, waits for them, and re-layouts, whole(): x = jnp.transpose(part, order)  27 us
  transfers between devices with their start and end apart: 8, of which 3 were waited for; matrix products, arithmetic and copies ran while one was open for 11% of the time, Pallas kernels for 0%

profile of v1, /device:TPU:0, one launch (start us, length us, event | category | flops | bytes accessed | tf_op | source)
XLA Modules:
  0.0 671.5 jit_solution(14591051965272806129)
XLA Ops:
  20.7 6.6 collective-permute-start.1
  30.6 42.8 %all_gather.12 = f32[25,512]{0,1:T(8,128)S(1)} all-gather(f32[25,16]{0,1:T(8,128)S(1)} %fusion.6), channel_id=1, replica_groups=mesh['rows'=8,'cols'=4] {'rows','cols'}, dimensions={1}, use_global_device_ids=true | all-gather | bytes 52800 | tf_op jit(solution)/shard_map/all_gather | solution.py:1473
  74.3 33.3 %psum.28 = f32[25,256]{1,0:T(8,128)S(1)} all-reduce(f32[25,256]{1,0:T(8,128)S(1)} %fusion.21), channel_id=1, replica_groups=mesh['rows'=8,'cols'=4] {'rows'}, use_global_device_ids=true, to_apply=%region_1.2 | all-reduce | flops 6400 | bytes 51200 | tf_op jit(solution)/shard_map/psum | solution.py:1479
  107.6 6.3 all_gather.13
  132.0 2.9 reshape.431.down_ref
  134.9 3.8 reshape.432
  138.8 4.3 copy.156
  143.0 4.0 reshape.433.up_ref
  147.1 4.2 reshape.428
  151.3 10.5 %copy.154 = bf16[2,9,8,32,4,64]{5,4,3,2,1,0:T(4,128)(2,1)} copy(bf16[2,9,8,32,4,64]{5,3,1,0,4,2:T(8,128)(2,1)} %bitcast.151) | data formatting | bytes 4718592 | tf_op jit(solution)/shard_map/transpose | solution.py:1463
  161.8 8.3 %reshape.429.high_ref = bf16[2,9,256,256]{3,2,1,0:T(8,128)(2,1)} reshape(bf16[2,9,8,32,4,64]{5,4,3,2,1,0:T(4,128)(2,1)} %copy.154) | data formatting | bytes 4718592 | tf_op jit(solution)/shard_map/reshape | solution.py:1464
  170.1 3.6 reshape.426
  173.7 10.5 %copy.153 = bf16[4,9,8,16,4,32]{5,4,3,2,1,0:T(4,128)(2,1)} copy(bf16[4,9,8,16,4,32]{5,3,1,0,4,2:T(8,128)(2,1)} %bitcast.152) | data formatting | bytes 2359296 | tf_op jit(solution)/shard_map/transpose | solution.py:1463
  184.2 6.4 reshape.427.low_ref
  191.3 69.5 %unet.1 = (bf16[4,9,128,128]{3,2,1,0:T(8,128)(2,1)}, bf16[2,9,256,256]{3,2,1,0:T(8,128)(2,1)}, bf16[9,128,256]{2,1,0:T(8,128)(2,1)}, bf16[9,256,128]{2,1,0:T(8,1...) custom-call(f32[512,256]{1,0:T(8,128)} %pad.24.img_ref, ...), custom_call_target="tpu_custom_call" | custom-call | tf_op jit(solution)/shard_map/unet/pallas_call | solution.py:1356
  272.7 3.7 reshape.450
  278.3 4.0 reshape.451
  282.4 3.5 reshape.444
  285.9 5.7 copy.206
  291.5 5.7 reshape.445
  297.2 4.0 reshape.446
  301.2 5.7 copy.205
  307.0 5.9 reshape.447
  312.9 76.8 %all-reduce.8.cloned.1.call-done = f32[38273]{0:T(1024)} async-done(((f32[38273]{0:T(1024)}), f32[38273]{0:T(1024)}) %all-reduce.8.cloned.1.call-update) | async-done | bytes 153108 | tf_op jit(solution)/shard_map/psum | solution.py:1537
  394.5 5.2 pad_maximum_fusion
  401.1 6.3 collective-permute-start.3
  407.4 3.1 collective-permute-start.2
  411.0 6.5 collective-permute-done.2
  425.3 104.0 %reduce-scatter.3.cloned.1.call-done = bf16[1,576,128]{2,1,0:T(8,128)(2,1)} async-done(((bf16[32,576,128]{2,1,0:T(8,128)(2,1)}), bf16[1,576,128]{2,1,0:T(8,128)(2,1)}) %reduce-scatter.3.cloned.1.call-update) | async-done | bytes 147472 | tf_op jit(solution)/shard_map/reduce_scatter | solution.py:1565
  537.4 40.0 %psum.30 = f32[]{:T(128)} all-reduce(f32[]{:T(128)S(6)} %add.231), channel_id=1, replica_groups=mesh['rows'=8,'cols'=4] {'rows','cols'}, use_global_device_ids=true, to_apply=%region_12.13 | all-reduce | flops 1 | bytes 8 | tf_op jit(solution)/shard_map/psum | solution.py:1577
  592.2 2.7 concatenate.72
  598.7 39.5 %psum.31 = f32[2,10]{1,0:T(2,128)S(1)} all-reduce(f32[2,10]{1,0:T(2,128)S(1)} %pad_maximum_fusion.7), channel_id=1, replica_groups=mesh['rows'=8,'cols'=4] {'rows','cols'}, use_global_device_ids=true, to_apply=%region_31.32 | all-reduce | flops 20 | bytes 160 | tf_op jit(solution)/shard_map/psum | solution.py:1595
  (235 shorter events, 101.9 us)
Async XLA Ops:
  7.2 116.1 %all-gather.3.cloned.1.call-start = ((), (), s32[]{:S(2)}) async-start(), calls=%async_computation.5 | async-start | bytes 4866048 | tf_op jit(solution)/shard_map/all_gather | solution.py:1456
  15.1 374.6 %all-reduce.8.cloned.1.call-start = ((), (), s32[]{:S(2)}) async-start(), calls=%async_computation.2 | async-start | bytes 311296 | tf_op jit(solution)/shard_map/psum | solution.py:1537
  16.2 58.0 %copy-start.13 = (f32[64,256]{1,0:T(8,128)S(1)}, f32[64,256]{1,0:T(8,128)}, u32[]{:S(2)}) copy-start(f32[64,256]{1,0:T(8,128)} %param.59) | copy-start | bytes 196612
  20.0 97.3 %copy-start.32 = (bf16[4,4,4,9,1]{3,2,4,1,0:T(4,128)(2,1)S(1)}, bf16[4,4,4,9,1]{3,2,4,1,0:T(4,128)(2,1)}, u32[]{:S(2)}) copy-start(bf16[4,4,4,9,1]{3,2,4,1,0:T(4,128)(2,1)} %constant.229) | copy-start | bytes 3460
  20.2 100.0 %collective-permute-start = (f32[16,16,36]{1,0,2:T(8,128)S(1)}, f32[16,16,36]{1,0,2:T(8,128)S(1)}, u32[]{:S(2)}, u32[]{:S(2)}) collective-permute-start(f32[16,16,36]{1,0,2:T(8,128)S(1)} %get-tuple-element.178), channel_id=1, source_target_pairs={{0,1},{1,3},{2,5},{3,7},{4,8},{5,10},{6,12},{7,14},{8,9},{9,11},{1... | collective-permute-start | bytes 110600 | tf_op jit(solution)/shard_map/ppermute | solution.py:1440
  20.7 99.5 %collective-permute-start.1 = (f32[16,16,36]{1,0,2:T(8,128)S(1)}, f32[16,16,36]{1,0,2:T(8,128)}, u32[]{:S(2)}, u32[]{:S(2)}) collective-permute-start(f32[16,16,36]{1,0,2:T(8,128)S(1)} %get-tuple-element.179), channel_id=1, source_target_pairs={{1,1},{2,3},{3,5},{0,7},{5,8},{6,10},{7,12},{4,14},{9,9},{10,11},{... | collective-permute-start | bytes 110600 | tf_op jit(solution)/shard_map/ppermute | solution.py:1441
  30.4 91.0 %copy-start.4 = (bf16[25,4224]{1,0:T(8,128)(2,1)}, bf16[25,4224]{1,0:T(8,128)(2,1)S(1)}, u32[]{:S(2)}) copy-start(bf16[25,4224]{1,0:T(8,128)(2,1)S(1)} %concatenate.67) | copy-start | bytes 633604
  30.6 86.0 %copy-start.30 = (f32[25,16]{0,1:T(8,128)}, f32[25,16]{0,1:T(8,128)S(1)}, u32[]{:S(2)}) copy-start(f32[25,16]{0,1:T(8,128)S(1)} %fusion.6) | copy-start | bytes 4804
  191.3 75.6 %copy-start.27 = (f32[9,4,4,9,1]{0,3,1,4,2:T(8,128)S(1)}, f32[9,4,4,9,1]{0,3,1,4,2:T(8,128)}, u32[]{:S(2)}) copy-start(f32[9,4,4,9,1]{0,3,1,4,2:T(8,128)} %constant.231) | copy-start | bytes 15556
  191.3 76.3 %copy-start.28 = (f32[9,4,4,9,1]{0,3,1,2,4:T(8,128)S(1)}, f32[9,4,4,9,1]{0,3,1,2,4:T(8,128)}, u32[]{:S(2)}) copy-start(f32[9,4,4,9,1]{0,3,1,2,4:T(8,128)} %constant.230) | copy-start | bytes 15556
  270.6 153.1 %reduce-scatter.5.cloned.1.call-start = ((), (), s32[]{:S(2)}) async-start(), calls=%async_computation.4 | async-start | bytes 40960 | tf_op jit(solution)/shard_map/reduce_scatter | solution.py:1551
  394.5 134.8 %reduce-scatter.3.cloned.1.call-start = ((), (), s32[]{:S(2)}) async-start(), calls=%async_computation.3 | async-start | bytes 4866048 | tf_op jit(solution)/shard_map/reduce_scatter | solution.py:1565
  399.8 23.9 %copy-start.5 = (bf16[25,4224]{1,0:T(8,128)(2,1)S(1)}, bf16[25,4224]{1,0:T(8,128)(2,1)}, u32[]{:S(2)}) copy-start(bf16[25,4224]{1,0:T(8,128)(2,1)} %copy-done.4) | copy-start | bytes 633604
  399.8 178.7 %copy-start.14 = (f32[64,256]{1,0:T(8,128)S(1)}, f32[64,256]{1,0:T(8,128)}, u32[]{:S(2)}) copy-start(f32[64,256]{1,0:T(8,128)} %param.59) | copy-start | bytes 196612
  399.9 181.1 %copy-start.17 = (f32[9,16,64]{2,1,0:T(8,128)S(1)}, f32[9,16,64]{2,1,0:T(8,128)}, u32[]{:S(2)}) copy-start(f32[9,16,64]{2,1,0:T(8,128)} %param.50) | copy-start | bytes 110596
  399.9 183.3 %copy-start.9 = (f32[9,32,32]{2,1,0:T(8,128)S(1)}, f32[9,32,32]{2,1,0:T(8,128)}, u32[]{:S(2)}) copy-start(f32[9,32,32]{2,1,0:T(8,128)} %param.53) | copy-start | bytes 110596
  400.7 184.8 %copy-start.7 = (f32[4224,16]{0,1:T(8,128)S(1)}, f32[4224,16]{0,1:T(8,128)}, u32[]{:S(2)}) copy-start(f32[4224,16]{0,1:T(8,128)} %param.56) | copy-start | bytes 811012
  401.1 9.9 %collective-permute-start.3 = (f32[16,16,24]{1,0,2:T(8,128)S(1)}, f32[16,16,24]{1,0,2:T(8,128)S(1)}, u32[]{:S(2)}, u32[]{:S(2)}) collective-permute-start(f32[16,16,24]{1,0,2:T(8,128)S(1)} %copy.193), channel_id=1, source_target_pairs={{1,0},{3,1},{5,2},{7,3},{8,4},{10,5},{12,6},{14,7},{9,8},{11,9},{1... | collective-permute-start | bytes 73736 | tf_op jit(solution)/shard_map/ppermute | solution.py:1522
  407.4 10.2 %collective-permute-start.2 = (f32[16,16,24]{1,0,2:T(8,128)S(1)}, f32[16,16,24]{1,0,2:T(8,128)S(1)}, u32[]{:S(2)}, u32[]{:S(2)}) collective-permute-start(f32[16,16,24]{1,0,2:T(8,128)S(1)} %copy.192), channel_id=1, source_target_pairs={{1,1},{3,2},{5,3},{7,0},{8,5},{10,6},{12,7},{14,4},{9,9},{11,10},{... | collective-permute-start | bytes 73736 | tf_op jit(solution)/shard_map/ppermute | solution.py:1523
  417.6 170.6 %copy-start.3 = (f32[4,9,16,32]{3,2,1,0:T(8,128)S(1)}, f32[4,9,16,32]{3,2,1,0:T(8,128)}, u32[]{:S(2)}) copy-start(f32[4,9,16,32]{3,2,1,0:T(8,128)} %param.44) | copy-start | bytes 221188
  418.3 171.9 %copy-start.2 = (f32[2,9,32,64]{3,2,1,0:T(8,128)S(1)}, f32[2,9,32,64]{3,2,1,0:T(8,128)}, u32[]{:S(2)}) copy-start(f32[2,9,32,64]{3,2,1,0:T(8,128)} %param.47) | copy-start | bytes 442372
  419.4 170.9 %copy-start.22 = (f32[2,9,32,64]{3,2,1,0:T(8,128)S(1)}, f32[2,9,32,64]{3,2,1,0:T(8,128)}, u32[]{:S(2)}) copy-start(f32[2,9,32,64]{3,2,1,0:T(8,128)} %param.48) | copy-start | bytes 442372
  530.3 61.9 %copy-start.36 = (f32[4]{0:T(128)S(1)}, f32[4]{0:T(128)}, u32[]{:S(2)}) copy-start(f32[4]{0:T(128)} %get-tuple-element.174) | copy-start | bytes 52
  530.3 61.9 %copy-start.37 = (f32[2]{0:T(128)S(1)}, f32[2]{0:T(128)}, u32[]{:S(2)}) copy-start(f32[2]{0:T(128)} %get-tuple-element.172) | copy-start | bytes 28
  530.3 110.5 %copy-start.29 = (f32[2,1152]{1,0:T(2,128)S(1)}, f32[2,1152]{1,0:T(2,128)}, u32[]{:S(2)}) copy-start(f32[2,1152]{1,0:T(2,128)} %norm_ref.1) | copy-start | bytes 27652
  530.3 110.5 %copy-start.34 = (f32[2,1152]{1,0:T(2,128)S(1)}, f32[2,1152]{1,0:T(2,128)}, u32[]{:S(2)}) copy-start(f32[2,1152]{1,0:T(2,128)} %param.63) | copy-start | bytes 27652
  530.3 110.5 %copy-start.35 = (f32[2,1152]{1,0:T(2,128)S(1)}, f32[2,1152]{1,0:T(2,128)}, u32[]{:S(2)}) copy-start(f32[2,1152]{1,0:T(2,128)} %param.64) | copy-start | bytes 27652
  578.2 67.4 %copy-start.21 = (f32[9,16,64]{2,1,0:T(8,128)}, f32[9,16,64]{2,1,0:T(8,128)S(1)}, u32[]{:S(2)}) copy-start(f32[9,16,64]{2,1,0:T(8,128)S(1)} %mul.661) | copy-start | bytes 110596
  578.3 67.3 %copy-start.19 = (f32[9,32,32]{2,1,0:T(8,128)}, f32[9,32,32]{2,1,0:T(8,128)S(1)}, u32[]{:S(2)}) copy-start(f32[9,32,32]{2,1,0:T(8,128)S(1)} %mul.675) | copy-start | bytes 110596
  578.3 67.3 %copy-start.16 = (f32[9,128,9]{1,2,0:T(8,128)S(1)}, f32[9,128,9]{1,2,0:T(8,128)}, u32[]{:S(2)}) copy-start(f32[9,128,9]{1,2,0:T(8,128)} %param.41) | copy-start | bytes 124420
  578.4 69.4 %copy-start.10 = (f32[2,9,32,64]{3,2,1,0:T(8,128)}, f32[2,9,32,64]{3,2,1,0:T(8,128)S(1)}, u32[]{:S(2)}) copy-start(f32[2,9,32,64]{3,2,1,0:T(8,128)S(1)} %mul.646) | copy-start | bytes 442372
  578.6 75.8 %copy-start.11 = (f32[4,9,16,32]{3,2,1,0:T(8,128)}, f32[4,9,16,32]{3,2,1,0:T(8,128)S(1)}, u32[]{:S(2)}) copy-start(f32[4,9,16,32]{3,2,1,0:T(8,128)S(1)} %mul.623) | copy-start | bytes 221188
  (14 other events, 166.8 us)
Sparse Core Ops, SparseCore 0:
  15.2 70.5 all-gather.2
  270.7 118.9 all-reduce.7
  394.6 21.3 reduce-scatter.4
  422.2 107.0 reduce-scatter.2

commit v2 on v1

--- a/solution.py
+++ b/solution.py
@@ -619,8 +619,7 @@
 
 
 def unet_kernel(
-    img_ref,
-    tgt_ref,
+    strip_ref,
     small_ref,
     film_ref,
     norm_ref,
@@ -636,12 +635,14 @@
     dhigh_ref,
     ddown_ref,
     dup_ref,
+    part_ref,
+    fgrad_ref,
+    imgrad_ref,
+    img_ref,
+    tgt_ref,
     dwi_ref,
     dwh_ref,
-    fgrad_ref,
     ngrad_ref,
-    loss_ref,
-    imgrad_ref,
     full_ref,
     half_ref,
     work_ref,
@@ -1042,6 +1043,18 @@
     for b in range(3):
         wd_ref[b * 512 + 384 : b * 512 + 512, :] = jnp.zeros((128, 256), BF)
 
+    lane = lax.broadcasted_iota(jnp.int32, (32, 128), 1)
+    none = jnp.zeros((32, 128), F32)
+
+    def open_strip(i, carry):
+        half = pl.ds(pl.multiple_of(i * 16, 16), 16)
+        x = jnp.concatenate([strip_ref[0, half, :], strip_ref[1, half, :]], axis=0)
+        img_ref[at(i), :] = jnp.concatenate([jnp.where(lane < 24, x, 0.0), none], axis=1)
+        x = jnp.where(lane < 12, pltpu.roll(x, 104, 1), 0.0)
+        tgt_ref[at(i), :] = jnp.concatenate([x, none], axis=1)
+        return carry
+
+    loop(open_strip)
     send(0, edge_cell(img_ref))
     load_wc(0)
     load_up()
@@ -1165,7 +1178,10 @@
         return carry + half * diff
 
     lost = loop(loss_body, jnp.zeros((32, 256), F32))
-    loss_ref[...] = jnp.sum(lost.reshape(4, 8, 256), axis=0)
+    lost = jnp.sum(lost, axis=0, keepdims=True)
+    part_ref[...] = jnp.zeros(part_ref.shape, F32)
+    part_ref[99:100, :] = lost[:, 0:128] + lost[:, 128:256]
+    fgrad_ref[...] = jnp.zeros(fgrad_ref.shape, F32)
 
 
     send(10, edge_cell(work_ref.at[0]))
@@ -1333,10 +1349,32 @@
         edge_grad = edge_grad + back_value(k, recv_ref[e + 1, 0:32, :], recv_ref[k + 1, 0:32, :])
         put_wide_edge(edge_grad)
 
-    imgrad_ref[...] = dot(wide_ref[32:544, :], wit_ref[...])
+    imgrad_ref[...] = dot(wide_ref[32:544, :], wit_ref[...]) * small_ref[3:4, 0:128]
     turn_ref[0:256, :] = patch_ref[0].T
     for cp in range(2):
         dwi_ref[cp] = dot(turn_ref[0:256, :], wide_ref[32:544, 512 + cp * 512 : 768 + cp * 512])
+
+    for a in range(3):
+        for b in range(3):
+            first, last = None, None
+            for cp in range(2):
+                for rp in range(2):
+                    rho, gamma = rp + a - 1, cp + b - 1
+                    cell = (rho // 2 + 1) * 3 + gamma // 2 + 1
+                    phase = (gamma % 2) * 2 + rho % 2
+                    row = cell * 24 + phase * 6
+                    term = dwi_ref[cp, row : row + 6, rp * 128 : rp * 128 + 128]
+                    first = term if first is None else first + term
+                    row = cell * 12 + phase * 3
+                    term = dwh_ref[cp, row : row + 3, rp * 128 : rp * 128 + 128]
+                    last = term if last is None else last + term
+            t = 3 * a + b
+            part_ref[9 * t : 9 * t + 6, :] = first
+            part_ref[9 * (8 - t) + 6 : 9 * (8 - t) + 9, :] = last
+    for which in range(2):
+        for j in range(9):
+            row = 81 + 9 * which + j
+            part_ref[row : row + 1, :] = ngrad_ref[which : which + 1, 128 * j : 128 * j + 128]
 
 
 def unet(*operands):
@@ -1345,11 +1383,8 @@
         jax.ShapeDtypeStruct((2, 9, 256, 256), BF),
         jax.ShapeDtypeStruct((9, 128, 256), BF),
         jax.ShapeDtypeStruct((9, 256, 128), BF),
-        jax.ShapeDtypeStruct((2, 256, 256), F32),
-        jax.ShapeDtypeStruct((2, 256, 256), F32),
-        jax.ShapeDtypeStruct((2, 1024), F32),
-        jax.ShapeDtypeStruct((2, 1152), F32),
-        jax.ShapeDtypeStruct((8, 256), F32),
+        jax.ShapeDtypeStruct((256, 128), F32),
+        jax.ShapeDtypeStruct((8, 1024), F32),
         jax.ShapeDtypeStruct((512, 128), F32),
     )
     vmem = pl.BlockSpec(memory_space=pltpu.VMEM)
@@ -1359,6 +1394,11 @@
         in_specs=[vmem] * len(operands),
         out_specs=[vmem] * len(outs),
         scratch_shapes=[
+            pltpu.VMEM((512, 256), F32),
+            pltpu.VMEM((512, 256), F32),
+            pltpu.VMEM((2, 256, 256), F32),
+            pltpu.VMEM((2, 256, 256), F32),
+            pltpu.VMEM((2, 1152), F32),
             pltpu.VMEM((6, 2, 512, 256), F32),
             pltpu.VMEM((4, 1, 512, 256), F32),
             pltpu.VMEM((2, 512, 256), F32),
@@ -1389,18 +1429,6 @@
     )(*operands)
 
 
-def strip_moves():
-    left, right = [], []
-    for r in range(8):
-        for c in range(4):
-            pair = ((r + 1) // 2) % 4
-            core = (r + 1) % 2
-            target = (pair * 2 + c // 2) * 4 + (c % 2) * 2 + core
-            right.append((r * 4 + c, target))
-            left.append((r * 4 + (c + 1) % 4, target))
-    return left, right
-
-
 def cells_of(block):
     rows, cols, width = block.shape
     x = block.reshape(rows // 2, 2, cols // 2, 2, width)
@@ -1413,11 +1441,948 @@
     return jnp.transpose(x, (0, 3, 1, 2, 4)).reshape(2 * rows, 2 * cols, width // 4)
 
 
-BOTH = ("rows", "cols")
-
-
-def flip_t(w):
-    return jnp.swapaxes(w[::-1], 1, 2)
+def place_of():
+    rr, cc = lax.axis_index("rows"), lax.axis_index("cols")
+    return rr, cc, rr // 2, lax.rem(rr, 2), cc // 2, lax.rem(cc, 2)
+
+
+def device_at(z, y, x, k):
+    return {"rows": z * 2 + y, "cols": x * 2 + k}
+
+
+def device_no(d):
+    return {"rows": d // 4, "cols": lax.rem(d, 4)}
+
+
+def meet_all(me, count=32):
+    barrier = pltpu.get_barrier_semaphore()
+
+    def hello(d, carry):
+        @pl.when(d != me)
+        def _():
+            pl.semaphore_signal(barrier, inc=1, device_id=device_no(d), device_id_type=MESH)
+
+        return carry
+
+    lax.fori_loop(0, count, hello, 0)
+    pl.semaphore_wait(barrier, count - 1)
+
+
+def strip_at(r, c):
+    pair = lax.rem((r + 1) // 2, 4)
+    return (pair * 2 + c // 2) * 4 + lax.rem(c, 2) * 2 + lax.rem(r + 1, 2)
+
+
+def strip_of(d):
+    rr, cc = d // 4, lax.rem(d, 4)
+    pair, core = rr // 2, lax.rem(cc, 2)
+    r = jnp.where(pair == 0, 7 * (1 - core), 2 * pair - 1 + core)
+    return r, lax.rem(rr, 2) * 2 + cc // 2
+
+
+def slots_of(d):
+    r, c = strip_of(d)
+    row = (r + 1) // 2
+    return row * 5 + c + 1, row * 5 + lax.rem(c + 1, 4)
+
+
+def lane_tables():
+    low = np.zeros((512, 512), np.float32)
+    high = np.zeros((512, 512), np.float32)
+    rest = np.zeros((512, 512), np.float32)
+    for lane in range(512):
+        c, q = lane // 128, lane % 128
+        low[lane, (q // 32) * 128 + c * 32 + q % 32] = 1.0
+        high[lane, (q // 64) * 256 + c * 64 + q % 64] = 1.0
+        to = c * 64 + q if q < 64 else (256 if q < 96 else 384) + c * 32 + q % 32
+        rest[lane, to] = 1.0
+    return np.stack([low, high, rest])
+
+
+def place_lanes(x, at, width=128):
+    n = x.shape[1]
+    one = (
+        lax.broadcasted_iota(jnp.int32, (n, width), 0) + at
+        == lax.broadcasted_iota(jnp.int32, (n, width), 1)
+    )
+    return jnp.dot(x, jnp.where(one, 1.0, 0.0).astype(x.dtype), preferred_element_type=F32)
+
+
+LOW_ROWS, HIGH_ROWS, ALL_ROWS = 144, 432, 576
+Z_ORDER = (0, 1, -1, 2, -2, 3, -3)
+
+
+def gather_kernel(
+    low_ref,
+    high_ref,
+    down_ref,
+    up_ref,
+    cond_ref,
+    film_ref,
+    joined_ref,
+    block_ref,
+    lanes_ref,
+    low_out,
+    high_out,
+    down_out,
+    up_out,
+    strip_out,
+    film_out,
+    pre_out,
+    cond_out,
+    all_ref,
+    strip_ref,
+    cbuf_ref,
+    csend_ref,
+    part_ref,
+    fsend_ref,
+    frecv_ref,
+    send_sem,
+    recv_sem,
+    strip_send,
+    strip_recv,
+    cond_send,
+    cond_recv,
+    film_send,
+    film_recv,
+):
+    rr, cc, z, y, x, k = place_of()
+    me = rr * 4 + cc
+
+    own = all_ref.at[z, y, x, k]
+    total = None
+    for j in range(4):
+        term = place_lanes(low_ref[j].reshape(144, 32).astype(BF), 32 * j)
+        total = term if total is None else total + term
+    own[0:144, :] = total.astype(BF)
+    own[144:432, :] = (
+        place_lanes(high_ref[0].reshape(288, 64).astype(BF), 0)
+        + place_lanes(high_ref[1].reshape(288, 64).astype(BF), 64)
+    ).astype(BF)
+    own[432:576, :] = (
+        place_lanes(down_ref[...].reshape(144, 64).astype(BF), 0)
+        + place_lanes(up_ref[:, 0:16, :].reshape(144, 32).astype(BF), 64)
+        + place_lanes(up_ref[:, 16:32, :].reshape(144, 32).astype(BF), 96)
+    ).astype(BF)
+
+    meet_all(me)
+
+    def shard(kind, zs, ys, xs, ks, device):
+        return pltpu.make_async_remote_copy(
+            src_ref=all_ref.at[zs, ys, xs, ks],
+            dst_ref=all_ref.at[zs, ys, xs, ks],
+            send_sem=send_sem.at[kind, zs, ys, xs],
+            recv_sem=recv_sem.at[zs, ys, xs, ks],
+            device_id=device,
+            device_id_type=MESH,
+        )
+
+    def to_up(zs):
+        return shard(0, zs, y, x, k, device_at(z + 1, y, x, k))
+
+    def to_down(zs):
+        return shard(1, zs, y, x, k, device_at(z - 1, y, x, k))
+
+    def to_x(zs, ys):
+        return shard(2, zs, ys, x, k, device_at(z, y, 1 - x, k))
+
+    def to_y(zs, xs):
+        return shard(3, zs, y, xs, k, device_at(z, 1 - y, x, k))
+
+    def to_core(zs, ys, xs):
+        return shard(4, zs, ys, xs, k, device_at(z, y, x, 1 - k))
+
+    def each_shard(act, wait, after_own):
+        for dz in Z_ORDER:
+            zs = z + dz
+            if dz == 1:
+                after_own()
+
+            @pl.when(jnp.logical_and(zs >= 0, zs <= 3))
+            def _(zs=zs, dz=dz):
+                if dz:
+                    wait(zs, y, x)
+                if dz <= 0:
+
+                    @pl.when(z < 3)
+                    def _():
+                        act(to_up(zs))
+
+                if dz >= 0:
+
+                    @pl.when(z > 0)
+                    def _():
+                        act(to_down(zs))
+
+                act(to_x(zs, y))
+                act(to_y(zs, x))
+                act(to_core(zs, y, x))
+
+        for dz in Z_ORDER:
+            zs = z + dz
+
+            @pl.when(jnp.logical_and(zs >= 0, zs <= 3))
+            def _(zs=zs):
+                wait(zs, y, 1 - x)
+
+                @pl.when(lax.rem(zs, 2) == 0)
+                def _():
+                    act(to_y(zs, 1 - x))
+
+                act(to_core(zs, y, 1 - x))
+                wait(zs, 1 - y, x)
+
+                @pl.when(lax.rem(zs, 2) == 1)
+                def _():
+                    act(to_x(zs, 1 - y))
+
+                act(to_core(zs, 1 - y, x))
+
+        for dz in Z_ORDER:
+            zs = z + dz
+
+            @pl.when(jnp.logical_and(zs >= 0, zs <= 3))
+            def _(zs=zs):
+                wait(zs, 1 - y, 1 - x)
+                act(to_core(zs, 1 - y, 1 - x))
+
+    to_left = strip_at(rr, cc)
+    to_right = strip_at(rr, lax.rem(cc + 3, 4))
+
+    def strip_copy(side, device):
+        return pltpu.make_async_remote_copy(
+            src_ref=block_ref.at[1 - side],
+            dst_ref=strip_ref.at[side],
+            send_sem=strip_send.at[side],
+            recv_sem=strip_recv.at[side],
+            device_id=device_no(device),
+            device_id_type=MESH,
+        )
+
+    strip_copy(0, to_left).start()
+
+    @pl.when(to_right != me)
+    def _():
+        strip_copy(1, to_right).start()
+
+    pre = lax.dot_general(
+        joined_ref[...],
+        cond_ref[...].astype(BF),
+        (((1,), (1,)), ((), ())),
+        preferred_element_type=F32,
+    )
+    pre_out[...] = pre
+    csend_ref[...] = jnp.concatenate([pre, jnp.zeros((32, 112), F32)], axis=1)
+
+    def cond_copy(c):
+        return pltpu.make_async_remote_copy(
+            src_ref=csend_ref,
+            dst_ref=cbuf_ref.at[cc],
+            send_sem=cond_send.at[c],
+            recv_sem=cond_recv.at[cc],
+            device_id={"rows": rr, "cols": c},
+            device_id_type=MESH,
+        )
+
+    def cond_arrives(c):
+        return pltpu.make_async_remote_copy(
+            src_ref=csend_ref,
+            dst_ref=cbuf_ref.at[c],
+            send_sem=cond_send.at[c],
+            recv_sem=cond_recv.at[c],
+            device_id={"rows": rr, "cols": c},
+            device_id_type=MESH,
+        )
+
+    for c in range(4):
+
+        @pl.when(cc != c)
+        def _(c=c):
+            cond_copy(c).start()
+
+    cbuf_ref[cc] = csend_ref[...]
+
+    def arrived(zs, ys, xs, ks=None):
+        ks = k if ks is None else ks
+        pltpu.make_async_remote_copy(
+            src_ref=all_ref.at[zs, ys, xs, ks],
+            dst_ref=all_ref.at[zs, ys, xs, ks],
+            send_sem=send_sem.at[0, zs, ys, xs],
+            recv_sem=recv_sem.at[zs, ys, xs, ks],
+            device_id=device_at(z, y, x, 1 - k),
+            device_id_type=MESH,
+        ).wait_recv()
+
+    def film_step():
+        for c in range(4):
+
+            @pl.when(cc != c)
+            def _(c=c):
+                cond_arrives(c).wait_recv()
+
+        whole = cbuf_ref[0]
+        for c in range(1, 4):
+            whole = whole + pltpu.roll(cbuf_ref[c], 16 * c, 1)
+        whole = whole[:, 0:64]
+        cond = (whole * (0.5 * jnp.tanh(0.5 * whole) + 0.5)).astype(BF)
+        cond_out[...] = cond.astype(F32)
+        part_ref[...] = jnp.dot(cond, film_ref[...].astype(BF), preferred_element_type=F32)
+
+        def deal(d, carry):
+            s_l, s_r = slots_of(d)
+            fsend_ref[d, 0:1, :] = part_ref[pl.ds(s_l, 1), :]
+            fsend_ref[d, 1:2, :] = part_ref[pl.ds(s_r, 1), :]
+
+            @pl.when(d != me)
+            def _():
+                film_copy(d).start()
+
+            return carry
+
+        fsend_ref[...] = jnp.zeros(fsend_ref.shape, F32)
+        lax.fori_loop(0, 32, deal, 0)
+        frecv_ref[me] = fsend_ref[me]
+
+    def film_copy(d):
+        return pltpu.make_async_remote_copy(
+            src_ref=fsend_ref.at[d],
+            dst_ref=frecv_ref.at[me],
+            send_sem=film_send.at[d],
+            recv_sem=film_recv.at[me],
+            device_id=device_no(d),
+            device_id_type=MESH,
+        )
+
+    def film_arrives(d):
+        return pltpu.make_async_remote_copy(
+            src_ref=fsend_ref.at[d],
+            dst_ref=frecv_ref.at[d],
+            send_sem=film_send.at[d],
+            recv_sem=film_recv.at[d],
+            device_id=device_no(d),
+            device_id_type=MESH,
+        )
+
+    each_shard(lambda copy: copy.start(), arrived, film_step)
+
+    for zs in range(4):
+        for ys in range(2):
+            for xs in range(2):
+                arrived(zs, ys, xs, 1 - k)
+
+    def row(r, carry):
+        zr, yr = r // 2, lax.rem(r, 2)
+
+        def joined(lo, hi):
+            return jnp.concatenate(
+                [all_ref[zr, yr, c // 2, c % 2, lo:hi, :] for c in range(4)], axis=1
+            )
+
+        low = jnp.dot(joined(0, 144), lanes_ref[0], preferred_element_type=F32).astype(BF)
+        at16 = pl.ds(pl.multiple_of(r * 16, 16), 16)
+        at32 = pl.ds(pl.multiple_of(r * 32, 32), 32)
+        for j in range(4):
+            low_out[j, :, at16, :] = low[:, j * 128 : j * 128 + 128].reshape(9, 16, 128)
+        high = jnp.dot(joined(144, 432), lanes_ref[1], preferred_element_type=F32).astype(BF)
+        for j in range(2):
+            high_out[j, :, at32, :] = high[:, j * 256 : j * 256 + 256].reshape(9, 32, 256)
+        rest = jnp.dot(joined(432, 576), lanes_ref[2], preferred_element_type=F32).astype(BF)
+        down_out[:, at16, :] = rest[:, 0:256].reshape(9, 16, 256)
+        up_out[:, at32, :] = jnp.concatenate(
+            [rest[:, 256:384].reshape(9, 16, 128), rest[:, 384:512].reshape(9, 16, 128)], axis=1
+        )
+        return carry
+
+    lax.fori_loop(0, 8, row, 0)
+
+    strip_copy(0, to_left).wait()
+
+    @pl.when(to_right != me)
+    def _():
+        strip_copy(1, to_right).wait()
+
+    @pl.when(to_right == me)
+    def _():
+        strip_ref[1] = block_ref[0]
+
+    strip_out[...] = strip_ref[...]
+
+    def film_wait(d, carry):
+        @pl.when(d != me)
+        def _():
+            film_arrives(d).wait_recv()
+
+        return carry
+
+    lax.fori_loop(0, 32, film_wait, 0)
+    for c in range(4):
+        total = frecv_ref[c]
+        for r in range(1, 8):
+            total = total + frecv_ref[4 * r + c]
+        film_out[:, c * 256 : c * 256 + 256] = total
+
+    def film_sent(d, carry):
+        @pl.when(d != me)
+        def _():
+            film_copy(d).wait_send()
+
+        return carry
+
+    lax.fori_loop(0, 32, film_sent, 0)
+    for c in range(4):
+
+        @pl.when(cc != c)
+        def _(c=c):
+            cond_copy(c).wait_send()
+
+    each_shard(lambda copy: copy.wait_send(), lambda *a: None, lambda: None)
+
+
+def gather(*operands):
+    outs = (
+        jax.ShapeDtypeStruct((4, 9, 128, 128), BF),
+        jax.ShapeDtypeStruct((2, 9, 256, 256), BF),
+        jax.ShapeDtypeStruct((9, 128, 256), BF),
+        jax.ShapeDtypeStruct((9, 256, 128), BF),
+        jax.ShapeDtypeStruct((2, 256, 128), F32),
+        jax.ShapeDtypeStruct((8, 1024), F32),
+        jax.ShapeDtypeStruct((32, 16), F32),
+        jax.ShapeDtypeStruct((32, 64), F32),
+    )
+    vmem = pl.BlockSpec(memory_space=pltpu.VMEM)
+    dma = pltpu.SemaphoreType.DMA
+    return pl.pallas_call(
+        gather_kernel,
+        out_shape=outs,
+        in_specs=[vmem] * len(operands),
+        out_specs=[vmem] * len(outs),
+        scratch_shapes=[
+            pltpu.VMEM((4, 2, 2, 2, ALL_ROWS, 128), BF),
+            pltpu.VMEM((2, 256, 128), F32),
+            pltpu.VMEM((4, 32, 128), F32),
+            pltpu.VMEM((32, 128), F32),
+            pltpu.VMEM((32, 256), F32),
+            pltpu.VMEM((32, 8, 256), F32),
+            pltpu.VMEM((32, 8, 256), F32),
+            dma((5, 4, 2, 2)),
+            dma((4, 2, 2, 2)),
+            dma((2,)),
+            dma((2,)),
+            dma((4,)),
+            dma((4,)),
+            dma((32,)),
+            dma((32,)),
+        ],
+        compiler_params=pltpu.CompilerParams(
+            collective_id=2, has_side_effects=True, vmem_limit_bytes=40 * 1024 * 1024
+        ),
+        name="gather",
+    )(*operands)
+
+
+PART_ROWS = 256
+NORM_ROW = 81
+LOSS_ROW = 99
+
+
+def lane_value(pairs):
+    lane = lax.broadcasted_iota(jnp.int32, (8, 128), 1)
+    total = jnp.zeros((8, 128), F32)
+    for at, value in pairs:
+        total = total + jnp.where(lane == at, value, 0.0)
+    return total
+
+
+def square_sum(x):
+    x = x * x
+    while x.ndim > 2:
+        x = jnp.sum(x, axis=0)
+    return jnp.sum(jnp.sum(x, axis=0, keepdims=True), axis=1, keepdims=True)
+
+
+def finish_kernel(*refs):
+    (
+        dlow_ref,
+        dhigh_ref,
+        ddown_ref,
+        dup_ref,
+        part_ref,
+        fgrad_ref,
+        imgrad_ref,
+        lanes_ref,
+        joined_ref,
+        pre_ref,
+        cond_ref,
+    ) = refs[:11]
+    params = refs[11:35]
+    outs = refs[35:59]
+    loss_out, clip_out, back_out = refs[59:62]
+    (
+        sb_ref,
+        rb_ref,
+        rx_ref,
+        ry_ref,
+        rz_ref,
+        m1_ref,
+        r1_ref,
+        m2_ref,
+        r2_ref,
+        m3_ref,
+        r3_ref,
+        gcs_ref,
+        gcr_ref,
+        film_ref,
+        total_ref,
+        back_ref,
+        core_send,
+        core_recv,
+        x_send,
+        x_recv,
+        y_send,
+        y_recv,
+        z_send,
+        z_recv,
+        m_send,
+        m_recv,
+        gc_send,
+        gc_recv,
+        back_send,
+        back_recv,
+    ) = refs[62:]
+    weights, firsts, seconds = params[0::3], params[1::3], params[2::3]
+    rr, cc, z, y, x, k = place_of()
+    me = rr * 4 + cc
+    meet_all(me)
+
+    def message(n, src, dst, d, source):
+        return pltpu.make_async_remote_copy(
+            src_ref=src,
+            dst_ref=dst.at[source],
+            send_sem=m_send.at[n, d],
+            recv_sem=m_recv.at[n, source],
+            device_id=device_no(d),
+            device_id_type=MESH,
+        )
+
+    def others(body):
+        def one(d, carry):
+            @pl.when(d != me)
+            def _():
+                body(d)
+
+            return carry
+
+        lax.fori_loop(0, 32, one, 0)
+
+    def fill(d, carry):
+        c = lax.rem(d, 4)
+        m1_ref[d, 0:2, 0:256] = fgrad_ref[0:2, pl.ds(pl.multiple_of(c * 256, 256), 256)]
+        m1_ref[d, :, 256:384] = part_ref[pl.ds(pl.multiple_of(d * 8, 8), 8), :]
+
+        @pl.when(d != me)
+        def _():
+            message(0, m1_ref.at[d], r1_ref, d, me).start()
+
+        return carry
+
+    m1_ref[...] = jnp.zeros(m1_ref.shape, F32)
+    lax.fori_loop(0, 32, fill, 0)
+    r1_ref[me] = m1_ref[me]
+
+    s_r, s_c = strip_of(me)
+    home_left = s_r * 4 + s_c
+    home_right = s_r * 4 + lax.rem(s_c + 1, 4)
+
+    def back_copy(side, device):
+        return pltpu.make_async_remote_copy(
+            src_ref=imgrad_ref.at[:, 16 * side : 16 * side + 16, :],
+            dst_ref=back_ref.at[1 - side],
+            send_sem=back_send.at[side],
+            recv_sem=back_recv.at[side],
+            device_id=device_no(device),
+            device_id_type=MESH,
+        )
+
+    back_copy(0, home_left).start()
+
+    @pl.when(home_right != me)
+    def _():
+        back_copy(1, home_right).start()
+
+    def back_lanes(v, which):
+        return lax.dot_general(
+            v, lanes_ref[which], (((1,), (1,)), ((), ())), preferred_element_type=F32
+        ).astype(BF)
+
+    def row(r, carry):
+        zr, yr = r // 2, lax.rem(r, 2)
+        at16 = pl.ds(pl.multiple_of(r * 16, 16), 16)
+        at32 = pl.ds(pl.multiple_of(r * 32, 32), 32)
+        b16 = pl.ds(pl.multiple_of(r * 32 + 16, 16), 16)
+        a16 = pl.ds(pl.multiple_of(r * 32, 16), 16)
+        low = back_lanes(
+            jnp.concatenate([dlow_ref[j, :, at16, :].reshape(144, 128) for j in range(4)], axis=1), 0
+        )
+        high = back_lanes(
+            jnp.concatenate([dhigh_ref[j, :, at32, :].reshape(288, 256) for j in range(2)], axis=1), 1
+        )
+        rest = back_lanes(
+            jnp.concatenate(
+                [
+                    ddown_ref[:, at16, :].reshape(144, 256),
+                    dup_ref[:, a16, :].reshape(144, 128),
+                    dup_ref[:, b16, :].reshape(144, 128),
+                ],
+                axis=1,
+            ),
+            2,
+        )
+        for c in range(4):
+            to = sb_ref.at[zr, yr, c // 2, c % 2]
+            to[0:144, :] = low[:, c * 128 : c * 128 + 128]
+            to[144:432, :] = high[:, c * 128 : c * 128 + 128]
+            to[432:576, :] = rest[:, c * 128 : c * 128 + 128]
+        return carry
+
+    def core_copy(zs):
+        return pltpu.make_async_remote_copy(
+            src_ref=sb_ref.at[zs, :, :, 1 - k],
+            dst_ref=rb_ref.at[zs],
+            send_sem=core_send.at[zs],
+            recv_sem=core_recv.at[zs],
+            device_id=device_at(z, y, x, 1 - k),
+            device_id_type=MESH,
+        )
+
+    for zs in range(4):
+        lax.fori_loop(2 * zs, 2 * zs + 2, row, 0)
+        core_copy(zs).start()
+
+    def add(to, a, b):
+        to[...] = (a[...].astype(F32) + b[...].astype(F32)).astype(BF)
+
+    def first_copy(zs):
+        by_x = zs % 2 == 0
+        return pltpu.make_async_remote_copy(
+            src_ref=rb_ref.at[zs, :, 1 - x] if by_x else rb_ref.at[zs, 1 - y],
+            dst_ref=rx_ref.at[zs],
+            send_sem=x_send.at[zs],
+            recv_sem=x_recv.at[zs],
+            device_id=device_at(z, y, 1 - x, k) if by_x else device_at(z, 1 - y, x, k),
+            device_id_type=MESH,
+        )
+
+    def second_copy(zs):
+        by_x = zs % 2 == 1
+        return pltpu.make_async_remote_copy(
+            src_ref=rb_ref.at[zs, y, 1 - x] if by_x else rb_ref.at[zs, 1 - y, x],
+            dst_ref=ry_ref.at[zs],
+            send_sem=y_send.at[zs],
+            recv_sem=y_recv.at[zs],
+            device_id=device_at(z, y, 1 - x, k) if by_x else device_at(z, 1 - y, x, k),
+            device_id_type=MESH,
+        )
+
+    for zs in range(4):
+        core_copy(zs).wait_recv()
+        for ys in range(2):
+            for xs in range(2):
+                to = rb_ref.at[zs, ys, xs]
+                add(to, to, sb_ref.at[zs, ys, xs, k])
+        first_copy(zs).start()
+
+    others(lambda d: message(0, m1_ref.at[d], r1_ref, d, d).wait_recv())
+    film_ref[...] = jnp.zeros(film_ref.shape, F32)
+
+    def collect(d, total):
+        s_l, s_rt = slots_of(d)
+        film_ref[pl.ds(s_l, 1), :] = film_ref[pl.ds(s_l, 1), :] + r1_ref[d, 0:1, 0:256]
+        film_ref[pl.ds(s_rt, 1), :] = film_ref[pl.ds(s_rt, 1), :] + r1_ref[d, 1:2, 0:256]
+        return total + r1_ref[d, :, 256:384]
+
+    m2_ref[0:8, :] = lax.fori_loop(0, 32, collect, jnp.zeros((8, 128), F32))
+    film_mine = film_ref[...]
+    film_w = weights[6][...].astype(BF).astype(F32)
+    gc_part = lax.dot_general(
+        film_mine, film_w, (((1,), (1,)), ((), ())), precision=HIGH, preferred_element_type=F32
+    )
+    wide = jnp.concatenate([gc_part, jnp.zeros((32, 64), F32)], axis=1)
+    for c in range(4):
+        gcs_ref[c] = pltpu.roll(wide, 128 - 16 * c, 1) if c else wide
+
+    def gc_copy(c, source):
+        return pltpu.make_async_remote_copy(
+            src_ref=gcs_ref.at[c],
+            dst_ref=gcr_ref.at[source],
+            send_sem=gc_send.at[c],
+            recv_sem=gc_recv.at[source],
+            device_id={"rows": rr, "cols": c},
+            device_id_type=MESH,
+        )
+
+    for c in range(4):
+
+        @pl.when(cc != c)
+        def _(c=c):
+            gc_copy(c, cc).start()
+
+        @pl.when(cc == c)
+        def _(c=c):
+            gcr_ref[c] = gcs_ref[c]
+
+    grads = [None] * 8
+    grads[6] = lax.dot_general(
+        cond_ref[...], film_mine, (((0,), (0,)), ((), ())), precision=HIGH, preferred_element_type=F32
+    )
+
+    for zs in range(4):
+        first_copy(zs).wait_recv()
+        for other in range(2):
+            to = rb_ref.at[zs, other, x] if zs % 2 == 0 else rb_ref.at[zs, y, other]
+            add(to, to, rx_ref.at[zs, other])
+        second_copy(zs).start()
+
+    for c in range(4):
+
+        @pl.when(cc != c)
+        def _(c=c):
+            gc_copy(c, c).wait_recv()
+
+    pre = pre_ref[...]
+    gc = gcr_ref[0] + gcr_ref[1] + gcr_ref[2] + gcr_ref[3]
+    gc = gc[:, 0:16] * silu_grad_tanh(pre)
+    grads[5] = lax.dot_general(
+        gc,
+        joined_ref[...].astype(F32),
+        (((0,), (0,)), ((), ())),
+        precision=HIGH,
+        preferred_element_type=F32,
+    )
+
+    def z_copy(zs):
+        return pltpu.make_async_remote_copy(
+            src_ref=rb_ref.at[zs, y, x],
+            dst_ref=rz_ref.at[z],
+            send_sem=z_send.at[zs],
+            recv_sem=z_recv.at[z],
+            device_id=device_at(zs, y, x, k),
+            device_id_type=MESH,
+        )
+
+    def z_arrives(zs):
+        return pltpu.make_async_remote_copy(
+            src_ref=rb_ref.at[zs, y, x],
+            dst_ref=rz_ref.at[zs],
+            send_sem=z_send.at[zs],
+            recv_sem=z_recv.at[zs],
+            device_id=device_at(zs, y, x, k),
+            device_id_type=MESH,
+        )
+
+    for zs in range(4):
+        second_copy(zs).wait_recv()
+        to = rb_ref.at[zs, y, x]
+        add(to, to, ry_ref.at[zs])
+
+        @pl.when(zs != z)
+        def _(zs=zs):
+            z_copy(zs).start()
+
+        @pl.when(zs == z)
+        def _(zs=zs):
+            rz_ref[zs] = rb_ref[zs, y, x]
+
+    for zs in range(4):
+
+        @pl.when(zs != z)
+        def _(zs=zs):
+            z_arrives(zs).wait_recv()
+
+    own = rz_ref[0].astype(F32)
+    for zs in range(1, 4):
+        own = own + rz_ref[zs].astype(F32)
+    grads[1] = jnp.stack([own[0:144, 32 * j : 32 * j + 32].reshape(9, 16, 32) for j in range(4)])
+    grads[2] = jnp.stack([own[144:432, 64 * j : 64 * j + 64].reshape(9, 32, 64) for j in range(2)])
+    grads[3] = own[432:576, 0:64].reshape(9, 16, 64)
+    grads[4] = jnp.concatenate(
+        [own[432:576, 64:96].reshape(9, 16, 32), own[432:576, 96:128].reshape(9, 16, 32)], axis=1
+    )
+
+    owned = square_sum(own)
+    for n in (5, 6):
+        owned = owned + square_sum(grads[n])
+    m2_ref[8:16, :] = jnp.broadcast_to(owned, (8, 128))
+    others(lambda d: message(1, m2_ref, r2_ref, d, me).start())
+    r2_ref[me] = m2_ref[...]
+    others(lambda d: message(1, m2_ref, r2_ref, d, d).wait_recv())
+
+    def take(d, total):
+        total_ref[pl.ds(pl.multiple_of(d * 8, 8), 8), :] = r2_ref[d, 0:8, :]
+        return total + r2_ref[d, 8:16, :]
+
+    squares = lax.fori_loop(0, 32, take, jnp.zeros((8, 128), F32))
+    shared = square_sum(total_ref[0:LOSS_ROW, :])
+    clip = jnp.sqrt(squares[0:1, 0:1] + shared)
+    factor = jnp.minimum(1.0, CLIP_AT / clip)
+    clip_out[...] = jnp.broadcast_to(clip, (1, 128))
+    loss_out[...] = jnp.broadcast_to(
+        jnp.sum(total_ref[LOSS_ROW : LOSS_ROW + 1, :], axis=1, keepdims=True), (1, 128)
+    )
+    grads[0] = jnp.stack([total_ref[9 * t : 9 * t + 9, :] for t in range(9)])
+    grads[7] = jnp.concatenate(
+        [
+            jnp.concatenate(
+                [total_ref[NORM_ROW + 9 * n + j : NORM_ROW + 9 * n + j + 1, :] for j in range(9)],
+                axis=1,
+            )
+            for n in range(2)
+        ],
+        axis=0,
+    )
+
+    updates = []
+    pairs = []
+    spot = 0
+    for n in range(8):
+        grad = grads[n] * factor.reshape((1,) * grads[n].ndim)
+        first_new = BETA_ONE * firsts[n][...] + (1.0 - BETA_ONE) * grad
+        second_new = BETA_TWO * seconds[n][...] + (1.0 - BETA_TWO) * grad * grad
+        first_hat = first_new / (1.0 - BETA_ONE**STEP)
+        second_hat = second_new / (1.0 - BETA_TWO**STEP)
+        update = first_hat / (jnp.sqrt(second_hat) + EPS_ADAM) + DECAY * weights[n][...]
+        outs[3 * n][...] = grad
+        outs[3 * n + 1][...] = second_new
+        outs[3 * n + 2][...] = update
+        if n in (1, 2):
+            for j in range(update.shape[0]):
+                pairs.append((spot, square_sum(weights[n][j])))
+                pairs.append((64 + spot, square_sum(update[j])))
+                spot += 1
+        elif 2 < n < 7:
+            pairs.append((spot, square_sum(weights[n][...])))
+            pairs.append((64 + spot, square_sum(update)))
+            spot += 1
+
+    m3_ref[...] = lane_value(pairs)
+    others(lambda d: message(2, m3_ref, r3_ref, d, me).start())
+    r3_ref[me] = m3_ref[...]
+
+    def step(n, ratio, at=None):
+        ratio = ratio * RATE
+        if at is None:
+            weight, out = weights[n][...], outs[3 * n + 2]
+            out[...] = weight - ratio.reshape((1,) * weight.ndim) * out[...]
+        else:
+            weight, out = weights[n][at], outs[3 * n + 2]
+            out[at] = weight - ratio.reshape((1,) * weight.ndim) * out[at]
+
+    def root_ratio(a, b):
+        return jnp.sqrt(a) / jnp.sqrt(b)
+
+    step(7, root_ratio(square_sum(weights[7][...]), square_sum(outs[23][...])))
+    edge_w, edge_u = weights[0][...], outs[2][...]
+    for lo, hi in ((0, 6), (6, 9)):
+        ratio = root_ratio(square_sum(edge_w[:, lo:hi, :]), square_sum(edge_u[:, lo:hi, :])) * RATE
+        outs[2][:, lo:hi, :] = edge_w[:, lo:hi, :] - ratio.reshape(1, 1, 1) * edge_u[:, lo:hi, :]
+
+    others(lambda d: message(2, m3_ref, r3_ref, d, d).wait_recv())
+    sums = lax.fori_loop(0, 32, lambda d, t: t + r3_ref[d], jnp.zeros((8, 128), F32))
+    spot = 0
+    for n in range(1, 7):
+        for j in range(weights[n].shape[0] if n in (1, 2) else 1):
+            ratio = root_ratio(sums[0:1, spot : spot + 1], sums[0:1, 64 + spot : 65 + spot])
+            step(n, ratio, j if n in (1, 2) else None)
+            spot += 1
+
+    back_copy(0, home_left).wait()
+
+    @pl.when(home_right != me)
+    def _():
+        back_copy(1, home_right).wait()
+
+    @pl.when(home_right == me)
+    def _():
+        back_ref[0] = imgrad_ref[:, 16:32, :]
+
+    back_out[...] = back_ref[...]
+
+    others(lambda d: message(0, m1_ref.at[d], r1_ref, d, me).wait_send())
+    others(lambda d: message(1, m2_ref, r2_ref, d, me).wait_send())
+    others(lambda d: message(2, m3_ref, r3_ref, d, me).wait_send())
+    for c in range(4):
+
+        @pl.when(cc != c)
+        def _(c=c):
+            gc_copy(c, cc).wait_send()
+
+    for zs in range(4):
+        core_copy(zs).wait_send()
+        first_copy(zs).wait_send()
+        second_copy(zs).wait_send()
+
+        @pl.when(zs != z)
+        def _(zs=zs):
+            z_copy(zs).wait_send()
+
+
+def silu_grad_tanh(v):
+    s = 0.5 * jnp.tanh(0.5 * v) + 0.5
+    return s * (1.0 + v * (1.0 - s))
+
+
+def finish(*operands):
+    outs = []
+    for n in range(8):
+        outs += [jax.ShapeDtypeStruct(operands[11 + 3 * n].shape, F32)] * 3
+    outs += [
+        jax.ShapeDtypeStruct((1, 128), F32),
+        jax.ShapeDtypeStruct((1, 128), F32),
+        jax.ShapeDtypeStruct((2, 16, 16, 128), F32),
+    ]
+    vmem = pl.BlockSpec(memory_space=pltpu.VMEM)
+    dma = pltpu.SemaphoreType.DMA
+    return pl.pallas_call(
+        finish_kernel,
+        out_shape=tuple(outs),
+        in_specs=[vmem] * len(operands),
+        out_specs=[vmem] * len(outs),
+        scratch_shapes=[
+            pltpu.VMEM((4, 2, 2, 2, ALL_ROWS, 128), BF),
+            pltpu.VMEM((4, 2, 2, ALL_ROWS, 128), BF),
+            pltpu.VMEM((4, 2, ALL_ROWS, 128), BF),
+            pltpu.VMEM((4, ALL_ROWS, 128), BF),
+            pltpu.VMEM((4, ALL_ROWS, 128), BF),
+            pltpu.VMEM((32, 8, 384), F32),
+            pltpu.VMEM((32, 8, 384), F32),
+            pltpu.VMEM((16, 128), F32),
+            pltpu.VMEM((32, 16, 128), F32),
+            pltpu.VMEM((8, 128), F32),
+            pltpu.VMEM((32, 8, 128), F32),
+            pltpu.VMEM((4, 32, 128), F32),
+            pltpu.VMEM((4, 32, 128), F32),
+            pltpu.VMEM((32, 256), F32),
+            pltpu.VMEM((256, 128), F32),
+            pltpu.VMEM((2, 16, 16, 128), F32),
+            dma((4,)),
+            dma((4,)),
+            dma((4,)),
+            dma((4,)),
+            dma((4,)),
+            dma((4,)),
+            dma((4,)),
+            dma((4,)),
+            dma((3, 32)),
+            dma((3, 32)),
+            dma((4,)),
+            dma((4,)),
+            dma((2,)),
+            dma((2,)),
+        ],
+        compiler_params=pltpu.CompilerParams(
+            collective_id=3, has_side_effects=True, vmem_limit_bytes=56 * 1024 * 1024
+        ),
+        name="finish",
+    )(*operands)
 
 
 def per_device_strips(
@@ -1428,62 +2393,28 @@
     slot_live,
     *params,
 ):
-    weights, firsts, seconds = params[0::3], params[1::3], params[2::3]
-    edge_w, low_w, high_w, down_w, up_w, cond_w, film_w, norm_w = weights
-    rr, cc = lax.axis_index("rows"), lax.axis_index("cols")
+    edge_w, low_w, high_w, down_w, up_w, cond_w, film_w, norm_w = params[0::3]
+    me = lax.axis_index("rows") * 4 + lax.axis_index("cols")
     by_cell, by_tile = phase_tables()
-    moves_left, moves_right = strip_moves()
+    lanes = jnp.asarray(lane_tables(), BF)
 
     block = jnp.concatenate(
         [cells_of(image_pair[0].astype(F32)), cells_of(noise_target[0])], axis=-1
     )
-    left = lax.ppermute(block[:, 16:], BOTH, moves_right)
-    right = lax.ppermute(block[:, :16], BOTH, moves_left)
-    strip = jnp.concatenate([left, right], axis=1).reshape(512, 36)
-    img = jnp.pad(strip[:, 0:24], ((0, 0), (0, 232)))
-    tgt = jnp.pad(strip[:, 24:36], ((0, 0), (0, 244)))
-
-    pair, core = rr // 2, lax.rem(cc, 2)
-    col = lax.rem(rr, 2) * 2 + cc // 2
-    slot_row = jnp.where(pair == 0, 4 * (1 - core), pair)
-    slot_left = slot_row * 5 + col + 1
-    slot_right = slot_row * 5 + jnp.where(col == 3, 0, col + 1)
-    slots = jnp.stack([slot_left, slot_right])
-
-    shards = [low_w, high_w, down_w, up_w]
-    flat = [w.astype(BF).reshape(-1, 128) for w in shards]
-    sizes = [f.shape[0] for f in flat]
-    every = lax.all_gather(jnp.concatenate(flat, axis=0), BOTH, axis=0, tiled=False)
-    starts = np.cumsum([0] + sizes)
-
-    def whole(k, shape):
-        part = every[:, starts[k] : starts[k + 1]].reshape((8, 4) + shape)
-        n = len(shape)
-        order = tuple(range(2, n)) + (0, n, 1, n + 1)
-        x = jnp.transpose(part, order)
-        return x.reshape(shape[:-2] + (8 * shape[-2], 4 * shape[-1]))
-
-    low = whole(0, low_w.shape)
-    high = whole(1, high_w.shape)
-    down = whole(2, down_w.shape)
-    up = whole(3, up_w.shape)
-
-    joined = jnp.concatenate([time_embed(timesteps).astype(BF), text_pooled], axis=-1)[0].reshape(25, -1)
-    pre_own = jnp.dot(joined, cond_w.astype(BF), preferred_element_type=F32)
-    pre = lax.all_gather(pre_own, BOTH, axis=1, tiled=True)
-    cond = jax.nn.silu(pre).astype(BF)
-    film_rows, film_cols = film_w.shape
-    cond_own = lax.dynamic_slice_in_dim(cond, rr * film_rows, film_rows, 1)
-    film_low = film_w.astype(BF)
-    film_part = jnp.dot(cond_own, film_low, preferred_element_type=F32)
-    film = lax.all_gather(lax.psum(film_part, "rows"), "cols", axis=1, tiled=True)
-    own_film = jnp.take(film, slots, axis=0)
+    block = jnp.pad(block, ((0, 0), (0, 0), (0, 92)))
+    block = jnp.stack([block[:, 0:16], block[:, 16:32]]).reshape(2, 256, 128)
+    joined = jnp.concatenate([time_embed(timesteps).astype(BF), text_pooled], axis=-1)[0]
+    joined = jnp.pad(joined.reshape(25, -1), ((0, 7), (0, 0)))
+    low, high, down, up, strip, own_film, pre, cond = gather(
+        low_w, high_w, down_w, up_w, cond_w.T, film_w, joined, block, lanes
+    )
 
     live_slots = slot_live[0].astype(F32)
     side = np.array([32, 64, 64, 64, 32], np.float32)
     count = 3.0 * jnp.sum(live_slots * (side[:, None] * side[None, :]))
+    slots = jnp.stack(slots_of(me))
     own_live = jnp.take(live_slots.reshape(25), slots)
-    small = jnp.concatenate([own_live, (2.0 / count)[None], jnp.zeros((5,), F32)])
+    small = jnp.concatenate([own_live, (2.0 / count)[None], count[None], jnp.zeros((4,), F32)])
     small = jnp.broadcast_to(small[:, None], (8, 256))
 
     edge_low = edge_w.astype(BF)
@@ -1501,9 +2432,11 @@
         x = jnp.einsum("grpt,tcd->grcpd", tile_tab, w).reshape(2048, -1)
         return jnp.pad(x, ((0, 0), (0, 128 - x.shape[1])))
 
-    outs = unet(
-        img,
-        tgt,
+    def flip_t(w):
+        return jnp.swapaxes(w[::-1], 1, 2)
+
+    dlow, dhigh, ddown, dup, part, fgrad, imgrad = unet(
+        strip,
         small,
         own_film,
         norm_w,
@@ -1516,120 +2449,18 @@
         by_tiles(head),
         by_cells(flip_t(head)),
     )
-    dlow, dhigh, ddown, dup, dwi, dwh, fgrad, ngrad, lost, imgrad = outs
-
-    back = (imgrad[:, 0:24] * (count)).reshape(16, 32, 24)
-    back_right = lax.ppermute(back[:, :16], BOTH, [(t, s) for s, t in moves_right])
-    back_left = lax.ppermute(back[:, 16:], BOTH, [(t, s) for s, t in moves_left])
-    image_grad = pixels_of(jnp.concatenate([back_left, back_right], axis=1))[None]
-
-    def fold(x, width):
-        x = jnp.transpose(x, (1, 0, 2))[: 36 * width].reshape(9, 4, width, 4, 128)
-        return jnp.einsum("oqpt,oqcpd->tcd", by_cell, x, precision=HIGH)
-
-    grad_in = fold(dwi, 6)
-    grad_head = fold(dwh, 3)[::-1]
-    edge_local = jnp.concatenate([jnp.swapaxes(grad_in, 1, 2), jnp.swapaxes(grad_head, 1, 2)], axis=2)
-    spot = (jnp.arange(25)[:, None] == slots[None, :]).astype(F32)
-    film_local = jnp.dot(spot, fgrad, precision=HIGH)
-    pieces = [film_local.reshape(-1), edge_local.reshape(-1), ngrad.reshape(-1), jnp.sum(lost).reshape(1)]
-    lens = [p.shape[0] for p in pieces]
-    total = lax.psum(jnp.concatenate(pieces), BOTH)
-    ends = np.cumsum([0] + lens)
-    film_sum = total[ends[0] : ends[1]].reshape(25, 1024)
-    edge_sum = total[ends[1] : ends[2]].reshape(9, 128, 9)
-    norm_sum = total[ends[2] : ends[3]].reshape(2, 1152)
-    loss_sum = total[ends[3]]
-
-    film_mine = lax.dynamic_slice_in_dim(film_sum, cc * film_cols, film_cols, 1)
-    film_own = lax.dot_general(
-        cond_own.astype(F32), film_mine, (((0,), (0,)), ((), ())), precision=HIGH
-    )
-    gc_part = lax.dot_general(
-        film_mine, film_low.astype(F32), (((1,), (1,)), ((), ())), precision=HIGH
-    )
-    gc = lax.psum_scatter(gc_part, "cols", scatter_dimension=1, tiled=True) * silu_grad(pre_own)
-    cond_grad = lax.dot_general(joined.astype(F32), gc, (((0,), (0,)), ((), ())), precision=HIGH)
-
-    def dealt(g, shape):
-        n = len(shape)
-        lead = shape[:-2]
-        x = g.reshape(lead + (8, shape[-2], 4, shape[-1]))
-        m = len(lead)
-        x = jnp.transpose(x, (m, m + 2) + tuple(range(m)) + (m + 1, m + 3))
-        return x.reshape(32, -1, 128)
-
-    packed = jnp.concatenate(
-        [dealt(g, w.shape) for g, w in zip((dlow, dhigh, ddown, dup), shards)], axis=1
-    )
-    mine = lax.psum_scatter(packed, BOTH, scatter_dimension=0, tiled=False).astype(F32)
-    own = [mine[starts[k] : starts[k + 1]].reshape(w.shape) for k, w in enumerate(shards)]
-    grads = (edge_sum, own[0], own[1], own[2], own[3], cond_grad, film_own, norm_sum)
-    results, clip_norm = lamb(weights, firsts, seconds, grads)
-    return tuple(results) + (loss_sum, count, clip_norm, image_grad)
-
-
-def lamb(weights, firsts, seconds, grads):
-    sharded = (1, 2, 3, 4, 5, 6)
-    stacked = (1, 2)
-    owned_sq = sum((jnp.sum(grads[k] * grads[k]) for k in sharded))
-    shared_sq = sum((jnp.sum(grads[k] * grads[k]) for k in range(8) if k not in sharded))
-    clip_norm = jnp.sqrt(lax.psum(owned_sq, BOTH) + shared_sq)
-    factor = jnp.minimum(1.0, CLIP_AT / clip_norm)
-    clipped, moments, updates = ([], [], [])
-    for k in range(8):
-        grad = grads[k] * factor
-        first_new = BETA_ONE * firsts[k] + (1.0 - BETA_ONE) * grad
-        second_new = BETA_TWO * seconds[k] + (1.0 - BETA_TWO) * grad * grad
-        first_hat = first_new / (1.0 - BETA_ONE**STEP)
-        second_hat = second_new / (1.0 - BETA_TWO**STEP)
-        clipped.append(grad)
-        moments.append(second_new)
-        updates.append(first_hat / (jnp.sqrt(second_hat) + EPS_ADAM) + DECAY * weights[k])
-
-    def matrix_squares(values, k):
-        if k in stacked:
-            return jnp.sum(values * values, axis=tuple(range(1, values.ndim)))
-        return jnp.sum(values * values).reshape(1)
-
-    sums = lax.psum(
-        jnp.stack(
-            [
-                jnp.concatenate([matrix_squares(weights[k], k) for k in sharded]),
-                jnp.concatenate([matrix_squares(updates[k], k) for k in sharded]),
-            ]
-        ),
-        BOTH,
-    )
-    ratios = jnp.sqrt(sums[0]) / jnp.sqrt(sums[1])
-    position = 0
-    results = []
-    for k in range(8):
-        if k in sharded:
-            span = weights[k].shape[0] if k in stacked else 1
-            ratio = ratios[position : position + span]
-            position += span
-            ratio = (
-                ratio.reshape((span,) + (1,) * (weights[k].ndim - 1)) if k in stacked else ratio[0]
-            )
-        elif k == 0:
-            part = (jnp.arange(9) < 6)[None, None, :]
-            other = jnp.logical_not(part)
-            weight_sq_two = weights[k] * weights[k]
-            update_sq_two = updates[k] * updates[k]
-            ratio_in = jnp.sqrt(jnp.sum(jnp.where(part, weight_sq_two, 0.0))) / jnp.sqrt(
-                jnp.sum(jnp.where(part, update_sq_two, 0.0))
-            )
-            ratio_out = jnp.sqrt(jnp.sum(jnp.where(other, weight_sq_two, 0.0))) / jnp.sqrt(
-                jnp.sum(jnp.where(other, update_sq_two, 0.0))
-            )
-            ratio = jnp.where(part, ratio_in, ratio_out)
-        else:
-            ratio = jnp.sqrt(jnp.sum(weights[k] * weights[k])) / jnp.sqrt(
-                jnp.sum(updates[k] * updates[k])
-            )
-        results.extend([clipped[k], moments[k], weights[k] - RATE * ratio * updates[k]])
-    return results, clip_norm
+
+    def view(n, a):
+        return jnp.swapaxes(a, 1, 2) if n == 0 else a.T if n == 5 else a
+
+    state = [view(n // 3, a) for n, a in enumerate(params)]
+    results = finish(
+        dlow, dhigh, ddown, dup, part, fgrad, imgrad.reshape(16, 32, 128), lanes, joined, pre, cond, *state
+    )
+    new = [view(n // 3, a) for n, a in enumerate(results[:24])]
+    loss, clip, back = results[24:]
+    back = jnp.concatenate([back[0], back[1]], axis=1)[:, :, 0:24]
+    return tuple(new) + (loss[0, 0], count, clip[0, 0], pixels_of(back)[None])
 
 
 def solution(mesh):

time: 679 us -> 246 us (0.36)
  waiting for transfers between devices: 187 us -> 0 us
  blocking collectives: 162 us -> 0 us
  Pallas kernels: 69.5 us -> 195 us
  local copies, waits for them, and re-layouts: 143 us -> 40.2 us
  other arithmetic: 55.1 us -> 2.53 us
  between operations: 30.2 us -> 5.42 us
  starting transfers between devices: 16.7 us -> 0 us
    pallas_call x0 -> x2, Pallas kernels: none -> 123 us  [the longest x1 74.2 us: finish(): pl.pallas_call(finish_kernel, out_shape=tuple(outs), in_specs=[vmem] * le...]
    psum x3 -> x0, blocking collectives: 113 us -> none  [the longest x1 40 us: lamb(): clip_norm = jnp.sqrt(lax.psum(owned_sq, BOTH) + shared_sq)]
    reduce_scatter x2 -> x0, waiting for transfers between devices: 104 us -> none  [the longest x1 104 us: per_device_strips(): lax.psum_scatter(packed, BOTH, scatter_dimension=0, tiled=False).astype(F32)]
    reshape x30 -> x0, local copies, waits for them, and re-layouts: 81.2 us -> none  [the longest x8 25.2 us: dealt(): x = g.reshape(lead + (8, shape[-2], 4, shape[-1]))]
    psum x1 -> x0, waiting for transfers between devices: 76.8 us -> none  [per_device_strips(): total = lax.psum(jnp.concatenate(pieces), BOTH)]
    all_gather x2 -> x0, blocking collectives: 49.1 us -> none  [the longest x1 42.8 us: per_device_strips(): pre = lax.all_gather(pre_own, BOTH, axis=1, tiled=True)]
    reduce_sum x18 -> x0, other arithmetic: 29.7 us -> none  [the longest x6 12.8 us: matrix_squares(): return jnp.sum(values * values).reshape(1)]
    transpose x4 -> x0, local copies, waits for them, and re-layouts: 27 us -> none  [whole(): x = jnp.transpose(part, order)]
  transfers between devices with their start and end apart: 8 -> 0, of which waited for: 3 -> 0; matrix products, arithmetic and copies ran while one was open for 11% -> 0% of each run, Pallas kernels for 0% -> 0%
where the time goes in v2:
time: 246 us; the launch traced here: 245 us
  Pallas kernels  195 us (79%)
  local copies, waits for them, and re-layouts  40.2 us (16%)
  between operations  5.42 us (2%)
  other arithmetic  2.53 us (1%)
    pallas_call x1, Pallas kernels, finish(): pl.pallas_call(finish_kernel, out_shape=tuple(outs), in_specs=[vmem] * le...  74.2 us
    pallas_call x1, Pallas kernels, unet(): pl.pallas_call(unet_kernel, out_shape=outs, in_specs=[vmem] * len(operand...  72 us
    pallas_call x1, Pallas kernels, gather(): pl.pallas_call(gather_kernel, out_shape=outs, in_specs=[vmem] * len(opera...  48.6 us
    unnamed x118, local copies, waits for them, and re-layouts  24.6 us
    slice x3, local copies, waits for them, and re-layouts, per_device_strips(): block = jnp.stack([block[:, 0:16], block[:, 16:32]]).reshape(2, 256, 128)  5.03 us

profile of v2, /device:TPU:0, one launch (start us, length us, event | category | flops | bytes accessed | tf_op | source)
XLA Modules:
  0.0 245.1 jit_solution(78907405360334848)
XLA Ops:
  0.9 0.7 convert_reduce_fusion.1
  1.7 1.3 convert_reduce_fusion
  5.4 0.9 copy.93
  6.4 0.8 convolution_bitcast_fusion.3
  7.3 0.9 convolution_bitcast_fusion.2
  9.4 0.8 pad_bitcast_fusion
  10.5 0.9 pad.27.wit_ref
  11.8 0.9 pad.28.wh_ref
  13.6 1.6 reshape_squeeze.4
  15.3 0.7 copy.71
  16.0 1.7 fusion.9
  17.8 1.8 copy.72
  19.5 1.6 copy.73
  21.2 48.6 %gather.8 = (bf16[4,9,128,128]{3,2,1,0:T(8,128)(2,1)S(1)}, bf16[2,9,256,256]{3,2,1,0:T(8,128)(2,1)S(1)}, bf16[9,128,256]{2,1,0:T(8,128)(2,1)S(1)}, bf16[9,256,12...) custom-call(f32[4,9,16,32]{3,2,1,0:T(8,128)S(1)} %copy-done.3, ...), custom_call_target="tpu_custom_call" | custom-call | tf_op jit(solution)/shard_map/gather/pallas_call | solution.py:1854
  69.8 1.4 copy-done.2
  71.3 1.0 copy-done.5
  72.3 0.9 copy-done.7
  73.1 0.8 copy-done.8
  74.0 0.7 copy-done.12
  76.5 72.0 %unet.1 = (bf16[4,9,128,128]{3,2,1,0:T(8,128)(2,1)}, bf16[2,9,256,256]{3,2,1,0:T(8,128)(2,1)}, bf16[9,128,256]{2,1,0:T(8,128)(2,1)}, bf16[9,256,128]{2,1,0:T(8,1...) custom-call(f32[2,256,128]{2,1,0:T(8,128)} %copy-done.12, ...), custom_call_target="tpu_custom_call" | custom-call | tf_op jit(solution)/shard_map/unet/pallas_call | solution.py:1391
  148.5 74.2 %finish.1 = (f32[9,9,128]{2,1,0:T(8,128)}, f32[9,9,128]{2,1,0:T(8,128)}, f32[9,9,128]{2,1,0:T(8,128)}, f32[4,9,16,32]{3,2,1,0:T(8,128)}, f32[4,9,16,32]{3,2,1,0:...) custom-call(bf16[4,9,128,128]{3,2,1,0:T(8,128)(2,1)} %get-tuple-elem, ...), custom_call_target="tpu_custom_call" | custom-call | tf_op jit(solution)/shard_map/finish/pallas_call | solution.py:2344
  222.7 1.0 slice_bitcast_fusion.1
  224.6 1.0 copy.85
  227.5 0.7 copy.123
  228.3 0.7 copy.124
  229.0 0.7 copy.125
  229.7 0.7 copy.126
  230.4 0.7 copy.127
  231.1 0.7 copy.128
  235.8 0.7 copy.135
  236.5 0.7 copy.136
  237.2 0.7 copy.137
  (141 shorter events, 17.0 us)
Async XLA Ops:
  0.7 7.6 %copy-start.26 = (bf16[9,4,4,9,1]{3,0,4,2,1:T(8,128)(2,1)S(1)}, bf16[9,4,4,9,1]{3,0,4,2,1:T(8,128)(2,1)}, u32[]{:S(2)}) copy-start(bf16[9,4,4,9,1]{3,0,4,2,1:T(8,128)(2,1)} %constant.116) | copy-start | bytes 7780
  0.7 7.9 %copy-start.16 = (bf16[1,5,5,4096]{3,2,1,0:T(8,128)(2,1)S(1)}, bf16[1,5,5,4096]{3,2,1,0:T(8,128)(2,1)}, u32[]{:S(2)}) copy-start(bf16[1,5,5,4096]{3,2,1,0:T(8,128)(2,1)} %param.38) | copy-start | bytes 614404
  8.9 12.3 %copy-start.1 = (bf16[32,4224]{1,0:T(8,128)(2,1)}, bf16[32,4224]{1,0:T(8,128)(2,1)S(1)}, u32[]{:S(2)}) copy-start(bf16[32,4224]{1,0:T(8,128)(2,1)S(1)} %pad.24.joined_ref.refs_8_) | copy-start | bytes 811012
  17.7 3.4 %copy-start.3 = (f32[4,9,16,32]{3,2,1,0:T(8,128)S(1)}, f32[4,9,16,32]{3,2,1,0:T(8,128)}, u32[]{:S(2)}) copy-start(f32[4,9,16,32]{3,2,1,0:T(8,128)} %refs_14_.1) | copy-start | bytes 221188
  17.7 3.5 %copy-start.4 = (f32[2,9,32,64]{3,2,1,0:T(8,128)S(1)}, f32[2,9,32,64]{3,2,1,0:T(8,128)}, u32[]{:S(2)}) copy-start(f32[2,9,32,64]{3,2,1,0:T(8,128)} %refs_17_.1) | copy-start | bytes 442372
  17.7 3.5 %copy-start.6 = (f32[4224,16]{0,1:T(8,128)S(1)}, f32[4224,16]{0,1:T(8,128)}, u32[]{:S(2)}) copy-start(f32[4224,16]{0,1:T(8,128)} %param.55) | copy-start | bytes 811012
  17.7 3.5 %copy-start.9 = (f32[9,32,32]{2,1,0:T(8,128)S(1)}, f32[9,32,32]{2,1,0:T(8,128)}, u32[]{:S(2)}) copy-start(f32[9,32,32]{2,1,0:T(8,128)} %refs_23_.1) | copy-start | bytes 110596
  17.7 3.5 %copy-start.10 = (f32[9,16,64]{2,1,0:T(8,128)S(1)}, f32[9,16,64]{2,1,0:T(8,128)}, u32[]{:S(2)}) copy-start(f32[9,16,64]{2,1,0:T(8,128)} %refs_20_.1) | copy-start | bytes 110596
  17.7 3.5 %copy-start.11 = (f32[64,256]{1,0:T(8,128)S(1)}, f32[64,256]{1,0:T(8,128)}, u32[]{:S(2)}) copy-start(f32[64,256]{1,0:T(8,128)} %refs_29_.1) | copy-start | bytes 196612
  223.7 3.8 %copy-start.22 = (f32[4,9,16,32]{3,2,1,0:T(8,128)S(1)}, f32[4,9,16,32]{3,2,1,0:T(8,128)}, u32[]{:S(2)}) copy-start(f32[4,9,16,32]{3,2,1,0:T(8,128)} %get-tuple-element.181) | copy-start | bytes 221188
  223.9 4.3 %copy-start.21 = (f32[4,9,16,32]{3,2,1,0:T(8,128)S(1)}, f32[4,9,16,32]{3,2,1,0:T(8,128)}, u32[]{:S(2)}) copy-start(f32[4,9,16,32]{3,2,1,0:T(8,128)} %get-tuple-element.182) | copy-start | bytes 221188
  224.6 4.4 %copy-start.20 = (f32[4,9,16,32]{3,2,1,0:T(8,128)S(1)}, f32[4,9,16,32]{3,2,1,0:T(8,128)}, u32[]{:S(2)}) copy-start(f32[4,9,16,32]{3,2,1,0:T(8,128)} %get-tuple-element.183) | copy-start | bytes 221188
  224.6 5.1 %copy-start.19 = (f32[2,9,32,64]{3,2,1,0:T(8,128)S(1)}, f32[2,9,32,64]{3,2,1,0:T(8,128)}, u32[]{:S(2)}) copy-start(f32[2,9,32,64]{3,2,1,0:T(8,128)} %get-tuple-element.184) | copy-start | bytes 442372
  225.6 4.8 %copy-start.18 = (f32[2,9,32,64]{3,2,1,0:T(8,128)S(1)}, f32[2,9,32,64]{3,2,1,0:T(8,128)}, u32[]{:S(2)}) copy-start(f32[2,9,32,64]{3,2,1,0:T(8,128)} %get-tuple-element.185) | copy-start | bytes 442372
  226.9 4.3 %copy-start.17 = (f32[2,9,32,64]{3,2,1,0:T(8,128)S(1)}, f32[2,9,32,64]{3,2,1,0:T(8,128)}, u32[]{:S(2)}) copy-start(f32[2,9,32,64]{3,2,1,0:T(8,128)} %get-tuple-element.186) | copy-start | bytes 442372
  228.2 3.6 %copy-start.32 = (f32[9,16,64]{2,1,0:T(8,128)S(1)}, f32[9,16,64]{2,1,0:T(8,128)}, u32[]{:S(2)}) copy-start(f32[9,16,64]{2,1,0:T(8,128)} %get-tuple-element.187) | copy-start | bytes 110596
  228.3 4.3 %copy-start.31 = (f32[9,16,64]{2,1,0:T(8,128)S(1)}, f32[9,16,64]{2,1,0:T(8,128)}, u32[]{:S(2)}) copy-start(f32[9,16,64]{2,1,0:T(8,128)} %get-tuple-element.188) | copy-start | bytes 110596
  228.3 4.9 %copy-start.30 = (f32[9,16,64]{2,1,0:T(8,128)S(1)}, f32[9,16,64]{2,1,0:T(8,128)}, u32[]{:S(2)}) copy-start(f32[9,16,64]{2,1,0:T(8,128)} %get-tuple-element.189) | copy-start | bytes 110596
  228.3 5.5 %copy-start.29 = (f32[9,32,32]{2,1,0:T(8,128)S(1)}, f32[9,32,32]{2,1,0:T(8,128)}, u32[]{:S(2)}) copy-start(f32[9,32,32]{2,1,0:T(8,128)} %get-tuple-element.190) | copy-start | bytes 110596
  229.0 5.5 %copy-start.28 = (f32[9,32,32]{2,1,0:T(8,128)S(1)}, f32[9,32,32]{2,1,0:T(8,128)}, u32[]{:S(2)}) copy-start(f32[9,32,32]{2,1,0:T(8,128)} %get-tuple-element.191) | copy-start | bytes 110596
  229.0 6.1 %copy-start.27 = (f32[9,32,32]{2,1,0:T(8,128)S(1)}, f32[9,32,32]{2,1,0:T(8,128)}, u32[]{:S(2)}) copy-start(f32[9,32,32]{2,1,0:T(8,128)} %get-tuple-element.192) | copy-start | bytes 110596
  229.7 6.1 %copy-start.25 = (f32[16,4224]{1,0:T(8,128)S(1)}, f32[16,4224]{1,0:T(8,128)}, u32[]{:S(2)}) copy-start(f32[16,4224]{1,0:T(8,128)} %get-tuple-element.100) | copy-start | bytes 811012
  230.4 6.1 %copy-start.24 = (f32[16,4224]{1,0:T(8,128)S(1)}, f32[16,4224]{1,0:T(8,128)}, u32[]{:S(2)}) copy-start(f32[16,4224]{1,0:T(8,128)} %get-tuple-element.101) | copy-start | bytes 811012
  231.1 6.1 %copy-start.23 = (f32[16,4224]{1,0:T(8,128)S(1)}, f32[16,4224]{1,0:T(8,128)}, u32[]{:S(2)}) copy-start(f32[16,4224]{1,0:T(8,128)} %get-tuple-element.102) | copy-start | bytes 811012
  231.9 6.1 %copy-start.38 = (f32[64,256]{1,0:T(8,128)S(1)}, f32[64,256]{1,0:T(8,128)}, u32[]{:S(2)}) copy-start(f32[64,256]{1,0:T(8,128)} %get-tuple-element.196) | copy-start | bytes 196612
  231.9 6.7 %copy-start.37 = (f32[64,256]{1,0:T(8,128)S(1)}, f32[64,256]{1,0:T(8,128)}, u32[]{:S(2)}) copy-start(f32[64,256]{1,0:T(8,128)} %get-tuple-element.197) | copy-start | bytes 196612
  231.9 7.3 %copy-start.36 = (f32[64,256]{1,0:T(8,128)S(1)}, f32[64,256]{1,0:T(8,128)}, u32[]{:S(2)}) copy-start(f32[64,256]{1,0:T(8,128)} %get-tuple-element.198) | copy-start | bytes 196612
  232.5 7.3 %copy-start.43 = (f32[2,1152]{1,0:T(2,128)S(1)}, f32[2,1152]{1,0:T(2,128)}, u32[]{:S(2)}) copy-start(f32[2,1152]{1,0:T(2,128)} %get-tuple-element.199) | copy-start | bytes 27652
  232.5 7.9 %copy-start.42 = (f32[2,1152]{1,0:T(2,128)S(1)}, f32[2,1152]{1,0:T(2,128)}, u32[]{:S(2)}) copy-start(f32[2,1152]{1,0:T(2,128)} %get-tuple-element.200) | copy-start | bytes 27652
  233.2 7.9 %copy-start.41 = (f32[2,1152]{1,0:T(2,128)S(1)}, f32[2,1152]{1,0:T(2,128)}, u32[]{:S(2)}) copy-start(f32[2,1152]{1,0:T(2,128)} %get-tuple-element.201) | copy-start | bytes 27652
  233.2 8.5 %copy-start.45 = (f32[1,128]{1,0:T(1,128)S(1)}, f32[1,128]{1,0:T(1,128)}, u32[]{:S(2)}) copy-start(f32[1,128]{1,0:T(1,128)} %get-tuple-element.109) | copy-start | bytes 1540
  233.2 8.5 %copy-start.44 = (f32[1,128]{1,0:T(1,128)S(1)}, f32[1,128]{1,0:T(1,128)}, u32[]{:S(2)}) copy-start(f32[1,128]{1,0:T(1,128)} %get-tuple-element.110) | copy-start | bytes 1540
  (14 other events, 22.0 us)

commit v3 on v1

--- a/solution.py
+++ b/solution.py
@@ -598,77 +598,204 @@
 N_EXCHANGE = 20
 
 
-def phase_tables():
-    by_cell = np.zeros((9, 4, 4, 9), np.float32)
-    by_tile = np.zeros((4, 4, 4, 9), np.float32)
-    for out in range(4):
-        cp_out, rp_out = out // 2, out % 2
-        for cell in range(9):
-            for inp in range(4):
-                a = 2 * (cell // 3 - 1) + inp % 2 - rp_out + 1
-                b = 2 * (cell % 3 - 1) + inp // 2 - cp_out + 1
-                if 0 <= a <= 2 and 0 <= b <= 2:
-                    by_cell[cell, inp, out, 3 * a + b] = 1.0
-        for g in range(4):
-            for r in range(4):
-                a = ROW_OF[r] - rp_out + 1
-                b = COL_OF[g] - cp_out + 1
-                if 0 <= a <= 2 and 0 <= b <= 2:
-                    by_tile[g, r, out, 3 * a + b] = 1.0
-    return by_cell, by_tile
-
-
-def unet_kernel(
-    img_ref,
-    tgt_ref,
-    small_ref,
-    film_ref,
-    norm_ref,
-    low_ref,
-    high_ref,
-    down_ref,
-    up_ref,
-    wi_ref,
-    wit_ref,
-    wh_ref,
-    wht_ref,
-    dlow_ref,
-    dhigh_ref,
-    ddown_ref,
-    dup_ref,
-    dwi_ref,
-    dwh_ref,
-    fgrad_ref,
-    ngrad_ref,
-    loss_ref,
-    imgrad_ref,
-    full_ref,
-    half_ref,
-    work_ref,
-    grad_ref,
-    wide_ref,
-    thin_ref,
-    act_ref,
-    acth_ref,
-    turn_ref,
-    wc_ref,
-    wr_ref,
-    wu_ref,
-    wut_ref,
-    wd_ref,
-    coef_ref,
-    rows_ref,
-    patch_ref,
-    ext_ref,
-    send_ref,
-    recv_ref,
-    send_sem,
-    recv_sem,
-):
-    rr = lax.axis_index("rows")
-    cc = lax.axis_index("cols")
-    core = lax.rem(cc, 2)
-    partner = cc + 1 - 2 * core
+def place_of():
+    rr, cc = lax.axis_index("rows"), lax.axis_index("cols")
+    return rr, cc, rr // 2, lax.rem(rr, 2), cc // 2, lax.rem(cc, 2)
+
+
+def device_at(z, y, x, k):
+    return {"rows": z * 2 + y, "cols": x * 2 + k}
+
+
+def device_no(d):
+    return {"rows": d // 4, "cols": lax.rem(d, 4)}
+
+
+def meet_all(me, count=32):
+    barrier = pltpu.get_barrier_semaphore()
+
+    def hello(d, carry):
+        @pl.when(d != me)
+        def _():
+            pl.semaphore_signal(barrier, inc=1, device_id=device_no(d), device_id_type=MESH)
+
+        return carry
+
+    lax.fori_loop(0, count, hello, 0)
+    pl.semaphore_wait(barrier, count - 1)
+
+
+def strip_at(r, c):
+    pair = lax.rem((r + 1) // 2, 4)
+    return (pair * 2 + c // 2) * 4 + lax.rem(c, 2) * 2 + lax.rem(r + 1, 2)
+
+
+def strip_of(d):
+    rr, cc = d // 4, lax.rem(d, 4)
+    pair, core = rr // 2, lax.rem(cc, 2)
+    r = jnp.where(pair == 0, 7 * (1 - core), 2 * pair - 1 + core)
+    return r, lax.rem(rr, 2) * 2 + cc // 2
+
+
+def slots_of(d):
+    r, c = strip_of(d)
+    row = (r + 1) // 2
+    return row * 5 + c + 1, row * 5 + lax.rem(c + 1, 4)
+
+
+def lane_tables():
+    low = np.zeros((512, 512), np.float32)
+    high = np.zeros((512, 512), np.float32)
+    rest = np.zeros((512, 512), np.float32)
+    for lane in range(512):
+        c, q = lane // 128, lane % 128
+        low[lane, (q // 32) * 128 + c * 32 + q % 32] = 1.0
+        high[lane, (q // 64) * 256 + c * 64 + q % 64] = 1.0
+        to = c * 64 + q if q < 64 else (256 if q < 96 else 384) + c * 32 + q % 32
+        rest[lane, to] = 1.0
+    return np.stack([low, rest, high])
+
+
+def place_lanes(x, at, width=128):
+    n = x.shape[1]
+    one = (
+        lax.broadcasted_iota(jnp.int32, (n, width), 0) + at
+        == lax.broadcasted_iota(jnp.int32, (n, width), 1)
+    )
+    return jnp.dot(x, jnp.where(one, 1.0, 0.0).astype(x.dtype), preferred_element_type=F32)
+
+
+ALL_ROWS = 576
+LOW, REST, HIGH_PART = range(3)
+ROWS_OF = ((0, 144), (144, 288), (288, 576))
+Z_ORDER = (0, 1, -1, 2, -2, 3, -3)
+
+
+NORM_ROW = 81
+LOSS_ROW = 99
+
+
+def lane_value(pairs):
+    lane = lax.broadcasted_iota(jnp.int32, (8, 128), 1)
+    total = jnp.zeros((8, 128), F32)
+    for at, value in pairs:
+        total = total + jnp.where(lane == at, value, 0.0)
+    return total
+
+
+def square_sum(x):
+    x = x * x
+    while x.ndim > 2:
+        x = jnp.sum(x, axis=0)
+    return jnp.sum(jnp.sum(x, axis=0, keepdims=True), axis=1, keepdims=True)
+
+
+def silu_grad_tanh(v):
+    s = 0.5 * jnp.tanh(0.5 * v) + 0.5
+    return s * (1.0 + v * (1.0 - s))
+
+
+def step_kernel(*refs):
+    live_ref, temb_ref, text_ref, block_ref, lanes_ref = refs[:5]
+    params, outs = refs[5:29], refs[29:53]
+    loss_out, count_out, clip_out, back_out = refs[53:57]
+    (
+        low_ref,
+        high_ref,
+        down_ref,
+        up_ref,
+        full_ref,
+        half_ref,
+        work_ref,
+        grad_ref,
+        wide_ref,
+        thin_ref,
+        act_ref,
+        acth_ref,
+        turn_ref,
+        wc_ref,
+        wr_ref,
+        wu_ref,
+        wut_ref,
+        wd_ref,
+        coef_ref,
+        rows_ref,
+        patch_ref,
+        ext_ref,
+        send_ref,
+        recv_ref,
+        img_ref,
+        tgt_ref,
+        dwi_ref,
+        dwh_ref,
+        ngrad_ref,
+        fgrad_ref,
+        part_ref,
+        imgrad_ref,
+        wi_ref,
+        wht_ref,
+        wit_ref,
+        wh_ref,
+        tmp_ref,
+        all_ref,
+        strip_ref,
+        cbuf_ref,
+        csend_ref,
+        cpart_ref,
+        fsend_ref,
+        frecv_ref,
+        film_ref,
+        joined_ref,
+        condv_ref,
+        rb_ref,
+        rx_ref,
+        ry_ref,
+        rz_ref,
+        own_ref,
+        m1_ref,
+        r1_ref,
+        m2_ref,
+        r2_ref,
+        m3_ref,
+        r3_ref,
+        gcs_ref,
+        gcr_ref,
+        fsum_ref,
+        total_ref,
+        back_ref,
+        send_sem,
+        recv_sem,
+        g_send,
+        g_recv,
+        strip_send,
+        strip_recv,
+        cond_send,
+        cond_recv,
+        film_send,
+        film_recv,
+        core_send,
+        core_recv,
+        x_send,
+        x_recv,
+        y_send,
+        y_recv,
+        z_send,
+        z_recv,
+        m_send,
+        m_recv,
+        gc_send,
+        gc_recv,
+        back_send,
+        back_recv,
+    ) = refs[57:]
+    weights, firsts, seconds = params[0::3], params[1::3], params[2::3]
+    edge_ref, norm_ref = weights[0], weights[7]
+    dlow_ref, dhigh_ref, ddown_ref, dup_ref = low_ref, high_ref, down_ref, up_ref
+    sb_ref = all_ref
+    rr, cc, z, y, x, co = place_of()
+    me = rr * 4 + cc
+    core = co
+    partner = 1 - co + 2 * x
     halo = rr >= 2
     split = jnp.logical_and(lax.rem(rr, 2) == 1, cc >= 2)
 
@@ -686,10 +813,6 @@
     place = lax.broadcasted_iota(jnp.int32, (32, 256), 0)
     lo_mask = jnp.where(place == 0, 0.0, jnp.where(place == 16, f_joined, 1.0))
     hi_mask = jnp.where(place == 31, 0.0, jnp.where(place == 15, f_joined, 1.0))
-
-    barrier = pltpu.get_barrier_semaphore()
-    pl.semaphore_signal(barrier, inc=1, device_id={"cols": partner}, device_id_type=MESH)
-    pl.semaphore_wait(barrier, 1)
 
     def before(x):
         return pltpu.roll(x, 1, 0) * lo_mask
@@ -1030,6 +1153,463 @@
         return d * coef_ref[k, 4] + x * coef_ref[k, 5] + coef_ref[k, 6]
 
 
+    def shard(kind, part, zs, ys, xs, ks, device):
+        rows = slice(*ROWS_OF[part])
+        return pltpu.make_async_remote_copy(
+            src_ref=all_ref.at[zs, ys, xs, ks, rows],
+            dst_ref=all_ref.at[zs, ys, xs, ks, rows],
+            send_sem=g_send.at[part, kind, zs, ys, xs],
+            recv_sem=g_recv.at[part, zs, ys, xs, ks],
+            device_id=device,
+            device_id_type=MESH,
+        )
+
+    def to_up(part, zs):
+        return shard(0, part, zs, y, x, co, device_at(z + 1, y, x, co))
+
+    def to_down(part, zs):
+        return shard(1, part, zs, y, x, co, device_at(z - 1, y, x, co))
+
+    def to_x(part, zs, ys):
+        return shard(2, part, zs, ys, x, co, device_at(z, y, 1 - x, co))
+
+    def to_y(part, zs, xs):
+        return shard(3, part, zs, y, xs, co, device_at(z, 1 - y, x, co))
+
+    def to_core(part, zs, ys, xs):
+        return shard(4, part, zs, ys, xs, co, device_at(z, y, x, 1 - co))
+
+    def arrived(part, zs, ys, xs, ks=co):
+        shard(4, part, zs, ys, xs, ks, device_at(z, y, x, 1 - co)).wait_recv()
+
+    def start(copy):
+        copy.start()
+
+    def in_line(dz, act):
+        zs = z + dz
+
+        @pl.when(jnp.logical_and(zs >= 0, zs <= 3))
+        def _():
+            act(zs)
+
+    def gather_z(part, dzs, act=start, wait=arrived):
+        for dz in dzs:
+
+            def one(zs, dz=dz):
+                if dz:
+                    wait(part, zs, y, x)
+                if dz <= 0:
+
+                    @pl.when(z < 3)
+                    def _():
+                        act(to_up(part, zs))
+
+                if dz >= 0:
+
+                    @pl.when(z > 0)
+                    def _():
+                        act(to_down(part, zs))
+
+                act(to_x(part, zs, y))
+                act(to_y(part, zs, x))
+                act(to_core(part, zs, y, x))
+
+            in_line(dz, one)
+
+    def gather_xy(part, act=start, wait=arrived):
+        for dz in Z_ORDER:
+
+            def one(zs):
+                wait(part, zs, y, 1 - x)
+
+                @pl.when(lax.rem(zs, 2) == 0)
+                def _():
+                    act(to_y(part, zs, 1 - x))
+
+                act(to_core(part, zs, y, 1 - x))
+                wait(part, zs, 1 - y, x)
+
+                @pl.when(lax.rem(zs, 2) == 1)
+                def _():
+                    act(to_x(part, zs, 1 - y))
+
+                act(to_core(part, zs, 1 - y, x))
+
+            in_line(dz, one)
+
+    def gather_last(part, act=start, wait=arrived):
+        for dz in Z_ORDER:
+
+            def one(zs):
+                wait(part, zs, 1 - y, 1 - x)
+                act(to_core(part, zs, 1 - y, 1 - x))
+
+            in_line(dz, one)
+
+    def gather_sent(part):
+        def sent(copy):
+            copy.wait_send()
+
+        def none(*a):
+            return None
+
+        gather_z(part, Z_ORDER, sent, none)
+        gather_xy(part, sent, none)
+        gather_last(part, sent, none)
+
+    def row_places(r):
+        def rows(at_row, size):
+            return pl.ds(pl.multiple_of(at_row, 16), size)
+
+        return rows(r * 16, 16), rows(r * 32, 32), rows(r * 32, 16), rows(r * 32 + 16, 16)
+
+    def gather_place(part):
+        for zs in range(4):
+            for ys in range(2):
+                for xs in range(2):
+                    arrived(part, zs, ys, xs, 1 - co)
+        rows = slice(*ROWS_OF[part])
+
+        def row(r, carry):
+            zr, yr = r // 2, lax.rem(r, 2)
+            at16, at32, a16, b16 = row_places(r)
+            packed = jnp.concatenate(
+                [all_ref[zr, yr, c // 2, c % 2, rows, :] for c in range(4)], axis=1
+            )
+            v = jnp.dot(packed, lanes_ref[part], preferred_element_type=F32).astype(BF)
+            if part == LOW:
+                for j in range(4):
+                    low_ref[j, :, at16, :] = v[:, j * 128 : j * 128 + 128].reshape(9, 16, 128)
+            elif part == HIGH_PART:
+                for j in range(2):
+                    high_ref[j, :, at32, :] = v[:, j * 256 : j * 256 + 256].reshape(9, 32, 256)
+            else:
+                down_ref[:, at16, :] = v[:, 0:256].reshape(9, 16, 256)
+                up_ref[:, a16, :] = v[:, 256:384].reshape(9, 16, 128)
+                up_ref[:, b16, :] = v[:, 384:512].reshape(9, 16, 128)
+            return carry
+
+        lax.fori_loop(0, 8, row, 0)
+
+    def pack_own(part):
+        rows = slice(*ROWS_OF[part])
+        own = all_ref.at[z, y, x, co]
+        if part == LOW:
+            total = None
+            for j in range(4):
+                term = place_lanes(weights[1][j].reshape(144, 32).astype(BF), 32 * j)
+                total = term if total is None else total + term
+        elif part == HIGH_PART:
+            total = place_lanes(weights[2][0].reshape(288, 64).astype(BF), 0) + place_lanes(
+                weights[2][1].reshape(288, 64).astype(BF), 64
+            )
+        else:
+            total = (
+                place_lanes(weights[3][...].reshape(144, 64).astype(BF), 0)
+                + place_lanes(weights[4][:, 0:16, :].reshape(144, 32).astype(BF), 64)
+                + place_lanes(weights[4][:, 16:32, :].reshape(144, 32).astype(BF), 96)
+            )
+        own[rows, :] = total.astype(BF)
+
+    to_left = strip_at(rr, cc)
+    to_right = strip_at(rr, lax.rem(cc + 3, 4))
+
+    def strip_copy(side, device):
+        return pltpu.make_async_remote_copy(
+            src_ref=block_ref.at[1 - side],
+            dst_ref=strip_ref.at[side],
+            send_sem=strip_send.at[side],
+            recv_sem=strip_recv.at[side],
+            device_id=device_no(device),
+            device_id_type=MESH,
+        )
+
+
+    def others(body):
+        def one(d, carry):
+            @pl.when(d != me)
+            def _():
+                body(d)
+
+            return carry
+
+        lax.fori_loop(0, 32, one, 0)
+
+    def row_mates(body):
+        for c in range(4):
+
+            @pl.when(cc != c)
+            def _(c=c):
+                body(c)
+
+    def cond_copy(c, source):
+        return pltpu.make_async_remote_copy(
+            src_ref=csend_ref,
+            dst_ref=cbuf_ref.at[source],
+            send_sem=cond_send.at[c],
+            recv_sem=cond_recv.at[source],
+            device_id={"rows": rr, "cols": c},
+            device_id_type=MESH,
+        )
+
+    def film_copy(d, source):
+        return pltpu.make_async_remote_copy(
+            src_ref=fsend_ref.at[d],
+            dst_ref=frecv_ref.at[source],
+            send_sem=film_send.at[d],
+            recv_sem=film_recv.at[source],
+            device_id=device_no(d),
+            device_id_type=MESH,
+        )
+
+    def cond_start():
+        joined_ref[24:32, :] = jnp.zeros((8, joined_ref.shape[1]), F32)
+        for a in range(5):
+            joined_ref[5 * a : 5 * a + 5, 0:128] = temb_ref[a].astype(F32)
+            joined_ref[5 * a : 5 * a + 5, 128:] = text_ref[a].astype(F32)
+        own = dot_nt(joined_ref[...].astype(BF), weights[5][...].astype(BF))
+        csend_ref[...] = jnp.concatenate([own, jnp.zeros((32, 112), F32)], axis=1)
+        row_mates(lambda c: cond_copy(c, cc).start())
+        cbuf_ref[cc] = csend_ref[...]
+
+    def film_start():
+        row_mates(lambda c: cond_copy(c, c).wait_recv())
+        whole = cbuf_ref[0]
+        for c in range(1, 4):
+            whole = whole + pltpu.roll(cbuf_ref[c], 16 * c, 1)
+        whole = whole[:, 0:64]
+        cond = (whole * sigmoid(whole)).astype(BF)
+        condv_ref[...] = cond.astype(F32)
+        cpart_ref[...] = dot(cond, weights[6][...].astype(BF))
+        fsend_ref[...] = jnp.zeros(fsend_ref.shape, F32)
+
+        def deal(d, carry):
+            s_l, s_r = slots_of(d)
+            fsend_ref[d, 0:1, :] = cpart_ref[pl.ds(s_l, 1), :]
+            fsend_ref[d, 1:2, :] = cpart_ref[pl.ds(s_r, 1), :]
+
+            @pl.when(d != me)
+            def _():
+                film_copy(d, me).start()
+
+            return carry
+
+        lax.fori_loop(0, 32, deal, 0)
+        frecv_ref[me] = fsend_ref[me]
+
+    def film_ready():
+        others(lambda d: film_copy(d, d).wait_recv())
+        for c in range(4):
+            total = frecv_ref[c]
+            for r in range(1, 8):
+                total = total + frecv_ref[4 * r + c]
+            film_ref[:, c * 256 : c * 256 + 256] = total
+
+
+    def edge_terms():
+        for a in range(3):
+            for b in range(3):
+                for cp in range(2):
+                    for rp in range(2):
+                        rho, gamma = rp + a - 1, cp + b - 1
+                        cell = (rho // 2 + 1) * 3 + gamma // 2 + 1
+                        phase = (gamma % 2) * 2 + rho % 2
+                        tile = COL_OF.index(gamma) * 512 + ROW_OF.index(rho) * 128
+                        yield 3 * a + b, cp, rp, cell, phase, tile
+
+    def load_edges():
+        dwi_ref[...] = jnp.zeros(dwi_ref.shape, F32)
+        dwh_ref[...] = jnp.zeros(dwh_ref.shape, F32)
+        for t, cp, rp, cell, phase, _ in edge_terms():
+            lanes = slice(rp * 128, rp * 128 + 128)
+            row = cell * 24 + phase * 6
+            dwi_ref[cp, row : row + 6, lanes] = edge_ref[t, 0:6, :]
+            row = cell * 12 + phase * 3
+            dwh_ref[cp, row : row + 3, lanes] = edge_ref[8 - t, 6:9, :]
+        wi_ref[...] = dwi_ref[...].astype(BF)
+        wht_ref[...] = dwh_ref[...].astype(BF)
+        for ref, taps, lo, size in ((wh_ref, 1, 6, 3), (wit_ref, -1, 0, 6)):
+            ref[...] = jnp.zeros(ref.shape, BF)
+            tmp_ref[...] = jnp.zeros(tmp_ref.shape, F32)
+            for t, cp, rp, _, _, tile in edge_terms():
+                row = (cp * 2 + rp) * size
+                tap = t if taps > 0 else 8 - t
+                tmp_ref[row : row + size, tile : tile + 128] = edge_ref[tap, lo : lo + size, :]
+            ref[0:32, :] = tmp_ref[...].astype(BF)
+
+
+    def add(to, b):
+        to[...] = (to[...].astype(F32) + b[...].astype(F32)).astype(BF)
+
+    def deal_pack(part, r_lo, r_hi):
+        rows = slice(*ROWS_OF[part])
+
+        def row(r, carry):
+            zr, yr = r // 2, lax.rem(r, 2)
+            at16, at32, a16, b16 = row_places(r)
+            if part == LOW:
+                pieces = [dlow_ref[j, :, at16, :].reshape(144, 128) for j in range(4)]
+            elif part == HIGH_PART:
+                pieces = [dhigh_ref[j, :, at32, :].reshape(288, 256) for j in range(2)]
+            else:
+                pieces = [
+                    ddown_ref[:, at16, :].reshape(144, 256),
+                    dup_ref[:, a16, :].reshape(144, 128),
+                    dup_ref[:, b16, :].reshape(144, 128),
+                ]
+            v = dot_nt(jnp.concatenate(pieces, axis=1), lanes_ref[part]).astype(BF)
+            for c in range(4):
+                sb_ref[zr, yr, c // 2, c % 2, rows, :] = v[:, c * 128 : c * 128 + 128]
+            return carry
+
+        lax.fori_loop(r_lo, r_hi, row, 0)
+
+    def core_copy(part, zs):
+        rows = slice(*ROWS_OF[part])
+        return pltpu.make_async_remote_copy(
+            src_ref=sb_ref.at[zs, :, :, 1 - co, rows],
+            dst_ref=rb_ref.at[zs, :, :, rows],
+            send_sem=core_send.at[part, zs],
+            recv_sem=core_recv.at[part, zs],
+            device_id=device_at(z, y, x, 1 - co),
+            device_id_type=MESH,
+        )
+
+    def first_copy(part, zs):
+        rows = slice(*ROWS_OF[part])
+        by_x = zs % 2 == 0
+        return pltpu.make_async_remote_copy(
+            src_ref=rb_ref.at[zs, :, 1 - x, rows] if by_x else rb_ref.at[zs, 1 - y, :, rows],
+            dst_ref=rx_ref.at[zs, :, rows],
+            send_sem=x_send.at[part, zs],
+            recv_sem=x_recv.at[part, zs],
+            device_id=device_at(z, y, 1 - x, co) if by_x else device_at(z, 1 - y, x, co),
+            device_id_type=MESH,
+        )
+
+    def second_copy(part, zs):
+        rows = slice(*ROWS_OF[part])
+        by_x = zs % 2 == 1
+        return pltpu.make_async_remote_copy(
+            src_ref=rb_ref.at[zs, y, 1 - x, rows] if by_x else rb_ref.at[zs, 1 - y, x, rows],
+            dst_ref=ry_ref.at[zs, rows],
+            send_sem=y_send.at[part, zs],
+            recv_sem=y_recv.at[part, zs],
+            device_id=device_at(z, y, 1 - x, co) if by_x else device_at(z, 1 - y, x, co),
+            device_id_type=MESH,
+        )
+
+    def z_copy(part, zs, source):
+        rows = slice(*ROWS_OF[part])
+        return pltpu.make_async_remote_copy(
+            src_ref=rb_ref.at[zs, y, x, rows],
+            dst_ref=rz_ref.at[source, rows],
+            send_sem=z_send.at[part, zs],
+            recv_sem=z_recv.at[part, source],
+            device_id=device_at(zs, y, x, co),
+            device_id_type=MESH,
+        )
+
+    def deal_core(part):
+        for zs in range(4):
+            deal_pack(part, 2 * zs, 2 * zs + 2)
+            core_copy(part, zs).start()
+
+    def deal_first(part):
+        rows = slice(*ROWS_OF[part])
+        for zs in range(4):
+            core_copy(part, zs).wait_recv()
+            for ys in range(2):
+                for xs in range(2):
+                    add(rb_ref.at[zs, ys, xs, rows], sb_ref.at[zs, ys, xs, co, rows])
+            first_copy(part, zs).start()
+
+    def deal_second(part):
+        rows = slice(*ROWS_OF[part])
+        for zs in range(4):
+            first_copy(part, zs).wait_recv()
+            for other in range(2):
+                to = rb_ref.at[zs, other, x, rows] if zs % 2 == 0 else rb_ref.at[zs, y, other, rows]
+                add(to, rx_ref.at[zs, other, rows])
+            second_copy(part, zs).start()
+
+    def deal_z(part):
+        rows = slice(*ROWS_OF[part])
+        for zs in range(4):
+            second_copy(part, zs).wait_recv()
+            add(rb_ref.at[zs, y, x, rows], ry_ref.at[zs, rows])
+
+            @pl.when(zs != z)
+            def _(zs=zs):
+                z_copy(part, zs, z).start()
+
+            @pl.when(zs == z)
+            def _(zs=zs):
+                rz_ref[zs, rows, :] = rb_ref[zs, y, x, rows, :]
+
+    def deal_end(part):
+        rows = slice(*ROWS_OF[part])
+        for zs in range(4):
+
+            @pl.when(zs != z)
+            def _(zs=zs):
+                z_copy(part, zs, zs).wait_recv()
+
+        own = rz_ref[0, rows, :].astype(F32)
+        for zs in range(1, 4):
+            own = own + rz_ref[zs, rows, :].astype(F32)
+        own_ref[rows, :] = own
+
+    def deal_sent(part):
+        for zs in range(4):
+            core_copy(part, zs).wait_send()
+            first_copy(part, zs).wait_send()
+            second_copy(part, zs).wait_send()
+
+            @pl.when(zs != z)
+            def _(zs=zs):
+                z_copy(part, zs, z).wait_send()
+
+
+    pack_own(LOW)
+    meet_all(me)
+    gather_z(LOW, (0,))
+    strip_copy(0, to_left).start()
+
+    @pl.when(to_right != me)
+    def _():
+        strip_copy(1, to_right).start()
+
+    cond_start()
+    gather_z(LOW, (1, -1))
+    pack_own(REST)
+    pack_own(HIGH_PART)
+    gather_z(LOW, (2, -2))
+    gather_z(LOW, (3, -3))
+    gather_xy(LOW)
+    gather_z(REST, (0,))
+    gather_z(HIGH_PART, (0,))
+    load_edges()
+    film_start()
+    gather_last(LOW)
+
+    live_all = live_ref[...].astype(F32)
+    slot_r = lax.broadcasted_iota(jnp.int32, (5, 5), 0)
+    slot_c = lax.broadcasted_iota(jnp.int32, (5, 5), 1)
+
+    def side(s):
+        return jnp.where(jnp.logical_or(s == 0, s == 4), 32.0, 64.0)
+
+    def all_sum(v):
+        return jnp.sum(jnp.sum(v, axis=0, keepdims=True), axis=1, keepdims=True)
+
+    count = 3.0 * all_sum(live_all * side(slot_r) * side(slot_c))
+    count_out[...] = jnp.broadcast_to(count, (1, 128))
+    my_l, my_r = slots_of(me)
+    slot_id = slot_r * 5 + slot_c
+    live_l = all_sum(jnp.where(slot_id == my_l, live_all, 0.0))
+    live_r = all_sum(jnp.where(slot_id == my_r, live_all, 0.0))
+
     def zero(i, carry):
         wc_ref[at(i), :] = jnp.zeros((32, 256), BF)
         return carry
@@ -1042,10 +1622,31 @@
     for b in range(3):
         wd_ref[b * 512 + 384 : b * 512 + 512, :] = jnp.zeros((128, 256), BF)
 
+
+    strip_copy(0, to_left).wait()
+
+    @pl.when(to_right != me)
+    def _():
+        strip_copy(1, to_right).wait()
+
+    @pl.when(to_right == me)
+    def _():
+        strip_ref[1] = block_ref[0]
+
+
+    lane = lax.broadcasted_iota(jnp.int32, (32, 128), 1)
+    none = jnp.zeros((32, 128), F32)
+
+    def open_strip(i, carry):
+        half = pl.ds(pl.multiple_of(i * 16, 16), 16)
+        x = jnp.concatenate([strip_ref[0, half, :], strip_ref[1, half, :]], axis=0)
+        img_ref[at(i), :] = jnp.concatenate([jnp.where(lane < 24, x, 0.0), none], axis=1)
+        x = jnp.where(lane < 12, pltpu.roll(x, 104, 1), 0.0)
+        tgt_ref[at(i), :] = jnp.concatenate([x, none], axis=1)
+        return carry
+
+    loop(open_strip)
     send(0, edge_cell(img_ref))
-    load_wc(0)
-    load_up()
-    load_down()
     arrive(0)
     put_patch(0, img_ref, recv_ref[0, 0:32, :], 24)
     for cp in range(2):
@@ -1078,7 +1679,12 @@
         k = 2 * index
         stats = fwd_norm_full(k, h, 1 + k)
         if index:
+            gather_xy(REST)
+            gather_xy(HIGH_PART)
             load_wc(2)
+        else:
+            gather_place(LOW)
+            load_wc(0)
         fwd_apply_full(k, h, stats, 1 + k)
         keep_wide(k)
 
@@ -1086,8 +1692,18 @@
             mid[cp] = value
 
         conv_low(put_mid)
+        if not index:
+            gather_z(REST, (1, -1))
+            gather_z(HIGH_PART, (1, -1))
         stats = fwd_norm_full(k + 1, mid, 2 + k)
         load_wc(2 * index + 1)
+        if index:
+            gather_last(REST)
+            gather_last(HIGH_PART)
+        else:
+            gather_z(REST, (2, -2))
+            gather_z(HIGH_PART, (2, -2))
+            film_ready()
         fwd_apply_full(k + 1, mid, stats, 2 + k)
         keep_wide(k + 1)
 
@@ -1095,9 +1711,14 @@
             out[cp] = h[cp] + value
 
         conv_low(put_out)
+        if not index:
+            gather_z(REST, (3, -3))
+            gather_z(HIGH_PART, (3, -3))
 
     skip = full_ref.at[4]
     send(5, edge_full(skip))
+    gather_place(REST)
+    load_down()
 
     def skip_body(i, carry):
         put_wide(i, skip[0, at(i), :], skip[1, at(i), :])
@@ -1124,12 +1745,14 @@
 
     fwd_half(4, half_ref.at[0], 6)
     keep_thin(0)
+    gather_place(HIGH_PART)
     half_ref[1, 0] = conv_high(0)
     fwd_half(5, half_ref.at[1], 7)
     keep_thin(1)
     half_ref[2, 0] = half_ref[0, 0] + conv_high(1)
     deep = half_ref.at[2]
     send(8, edge_cell(deep.at[0]))
+    load_up()
 
     def deep_body(i, carry):
         put_thin(i, deep[0, at(i), :])
@@ -1152,11 +1775,11 @@
     fwd_apply_full(6, merged, stats, 9)
     keep_wide(5)
     work_ref[0] = jnp.concatenate(
-        [dot(wide_ref[32:544, :], wh_ref[...]), jnp.zeros((512, 128), F32)], axis=1
-    )
-
-    live = spread(small_ref[0:2, :])
-    weight = small_ref[2:3, :]
+        [dot_nt(wide_ref[32:544, :], wh_ref[...]), jnp.zeros((512, 128), F32)], axis=1
+    )
+
+    live = spread(jnp.broadcast_to(jnp.concatenate([live_l, live_r], axis=0), (2, 256)))
+    weight = 2.0 / count
 
     def loss_body(i, carry):
         diff = work_ref[0, at(i), :] - tgt_ref[at(i), :]
@@ -1165,7 +1788,10 @@
         return carry + half * diff
 
     lost = loop(loss_body, jnp.zeros((32, 256), F32))
-    loss_ref[...] = jnp.sum(lost.reshape(4, 8, 256), axis=0)
+    lost = jnp.sum(lost, axis=0, keepdims=True)
+    part_ref[...] = jnp.zeros(part_ref.shape, F32)
+    part_ref[99:100, :] = lost[:, 0:128] + lost[:, 128:256]
+    fgrad_ref[...] = jnp.zeros(fgrad_ref.shape, F32)
 
 
     send(10, edge_cell(work_ref.at[0]))
@@ -1245,6 +1871,10 @@
     put_thin_edge(
         recv_ref[12, 0:32, :] + back_value(4, recv_ref[14, 0:32, :], recv_ref[6, 0:32, :])
     )
+
+    for part in range(3):
+        gather_sent(part)
+    deal_core(HIGH_PART)
 
     for cp in range(2):
         for rp in range(2):
@@ -1275,6 +1905,9 @@
                         thin_ref[32 * (1 + di) : 32 * (1 + di) + 512, (1 + dj) * 256 : (2 + dj) * 256],
                     ).astype(ddown_ref.dtype)
 
+    deal_first(HIGH_PART)
+    deal_core(REST)
+
     def put_work(cp, value):
         work_ref[cp] = value
 
@@ -1299,6 +1932,12 @@
         stats = norm_back_start(k + 1, mid, 2)
         send(e, edge_full(work_ref), stats)
         grad_low(k + 1, k + 1)
+        if index:
+            deal_second(HIGH_PART)
+            deal_first(REST)
+        else:
+            deal_end(HIGH_PART)
+            deal_z(REST)
         load_wr(k)
         arrive(e)
         norm_back_ready(k + 1, stats, e, 2)
@@ -1317,6 +1956,12 @@
         stats = norm_back_start(k, h, 2)
         send(e + 1, edge_full(work_ref), stats)
         grad_low(k, k)
+        if index:
+            deal_z(HIGH_PART)
+            deal_second(REST)
+        else:
+            deal_end(REST)
+            deal_core(LOW)
         arrive(e + 1)
         norm_back_ready(k, stats, e + 1, 2)
 
@@ -1333,91 +1978,377 @@
         edge_grad = edge_grad + back_value(k, recv_ref[e + 1, 0:32, :], recv_ref[k + 1, 0:32, :])
         put_wide_edge(edge_grad)
 
-    imgrad_ref[...] = dot(wide_ref[32:544, :], wit_ref[...])
+    deal_first(LOW)
     turn_ref[0:256, :] = patch_ref[0].T
     for cp in range(2):
         dwi_ref[cp] = dot(turn_ref[0:256, :], wide_ref[32:544, 512 + cp * 512 : 768 + cp * 512])
 
-
-def unet(*operands):
-    outs = (
-        jax.ShapeDtypeStruct((4, 9, 128, 128), BF),
-        jax.ShapeDtypeStruct((2, 9, 256, 256), BF),
-        jax.ShapeDtypeStruct((9, 128, 256), BF),
-        jax.ShapeDtypeStruct((9, 256, 128), BF),
-        jax.ShapeDtypeStruct((2, 256, 256), F32),
-        jax.ShapeDtypeStruct((2, 256, 256), F32),
-        jax.ShapeDtypeStruct((2, 1024), F32),
-        jax.ShapeDtypeStruct((2, 1152), F32),
-        jax.ShapeDtypeStruct((8, 256), F32),
-        jax.ShapeDtypeStruct((512, 128), F32),
-    )
+    for a in range(3):
+        for b in range(3):
+            first, last = None, None
+            for cp in range(2):
+                for rp in range(2):
+                    rho, gamma = rp + a - 1, cp + b - 1
+                    cell = (rho // 2 + 1) * 3 + gamma // 2 + 1
+                    phase = (gamma % 2) * 2 + rho % 2
+                    row = cell * 24 + phase * 6
+                    term = dwi_ref[cp, row : row + 6, rp * 128 : rp * 128 + 128]
+                    first = term if first is None else first + term
+                    row = cell * 12 + phase * 3
+                    term = dwh_ref[cp, row : row + 3, rp * 128 : rp * 128 + 128]
+                    last = term if last is None else last + term
+            t = 3 * a + b
+            part_ref[9 * t : 9 * t + 6, :] = first
+            part_ref[9 * (8 - t) + 6 : 9 * (8 - t) + 9, :] = last
+    for which in range(2):
+        for j in range(9):
+            row = 81 + 9 * which + j
+            part_ref[row : row + 1, :] = ngrad_ref[which : which + 1, 128 * j : 128 * j + 128]
+
+
+    def message(n, src, dst, d, source):
+        return pltpu.make_async_remote_copy(
+            src_ref=src,
+            dst_ref=dst.at[source],
+            send_sem=m_send.at[n, d],
+            recv_sem=m_recv.at[n, source],
+            device_id=device_no(d),
+            device_id_type=MESH,
+        )
+
+    def fill(d, carry):
+        c = lax.rem(d, 4)
+        m1_ref[d, 0:2, 0:256] = fgrad_ref[0:2, pl.ds(pl.multiple_of(c * 256, 256), 256)]
+        m1_ref[d, :, 256:384] = part_ref[pl.ds(pl.multiple_of(d * 8, 8), 8), :]
+
+        @pl.when(d != me)
+        def _():
+            message(0, m1_ref.at[d], r1_ref, d, me).start()
+
+        return carry
+
+    m1_ref[...] = jnp.zeros(m1_ref.shape, F32)
+    lax.fori_loop(0, 32, fill, 0)
+    r1_ref[me] = m1_ref[me]
+
+    deal_second(LOW)
+    imgrad = dot_nt(wide_ref[32:544, :], wit_ref[...]) * count
+    imgrad_ref[...] = imgrad.reshape(16, 32, 128)
+
+    s_r, s_c = strip_of(me)
+    home_left = s_r * 4 + s_c
+    home_right = s_r * 4 + lax.rem(s_c + 1, 4)
+
+    def back_copy(side, device):
+        return pltpu.make_async_remote_copy(
+            src_ref=imgrad_ref.at[:, 16 * side : 16 * side + 16, :],
+            dst_ref=back_ref.at[1 - side],
+            send_sem=back_send.at[side],
+            recv_sem=back_recv.at[side],
+            device_id=device_no(device),
+            device_id_type=MESH,
+        )
+
+    back_copy(0, home_left).start()
+
+    @pl.when(home_right != me)
+    def _():
+        back_copy(1, home_right).start()
+
+    others(lambda d: message(0, m1_ref.at[d], r1_ref, d, d).wait_recv())
+    fsum_ref[...] = jnp.zeros(fsum_ref.shape, F32)
+
+    def collect(d, total):
+        s_l, s_rt = slots_of(d)
+        fsum_ref[pl.ds(s_l, 1), :] = fsum_ref[pl.ds(s_l, 1), :] + r1_ref[d, 0:1, 0:256]
+        fsum_ref[pl.ds(s_rt, 1), :] = fsum_ref[pl.ds(s_rt, 1), :] + r1_ref[d, 1:2, 0:256]
+        return total + r1_ref[d, :, 256:384]
+
+    m2_ref[0:8, :] = lax.fori_loop(0, 32, collect, jnp.zeros((8, 128), F32))
+    film_mine = fsum_ref[...]
+    film_w = weights[6][...].astype(BF).astype(F32)
+    gc_part = lax.dot_general(
+        film_mine, film_w, (((1,), (1,)), ((), ())), precision=HIGH, preferred_element_type=F32
+    )
+    wide = jnp.concatenate([gc_part, jnp.zeros((32, 64), F32)], axis=1)
+    for c in range(4):
+        gcs_ref[c] = pltpu.roll(wide, 128 - 16 * c, 1) if c else wide
+
+    def gc_copy(c, source):
+        return pltpu.make_async_remote_copy(
+            src_ref=gcs_ref.at[c],
+            dst_ref=gcr_ref.at[source],
+            send_sem=gc_send.at[c],
+            recv_sem=gc_recv.at[source],
+            device_id={"rows": rr, "cols": c},
+            device_id_type=MESH,
+        )
+
+    for c in range(4):
+
+        @pl.when(cc != c)
+        def _(c=c):
+            gc_copy(c, cc).start()
+
+        @pl.when(cc == c)
+        def _(c=c):
+            gcr_ref[c] = gcs_ref[c]
+
+    grads = [None] * 8
+    grads[6] = lax.dot_general(
+        condv_ref[...], film_mine, (((0,), (0,)), ((), ())), precision=HIGH, preferred_element_type=F32
+    )
+
+    deal_z(LOW)
+
+    for c in range(4):
+
+        @pl.when(cc != c)
+        def _(c=c):
+            gc_copy(c, c).wait_recv()
+
+    pre = csend_ref[:, 0:16]
+    gc = gcr_ref[0] + gcr_ref[1] + gcr_ref[2] + gcr_ref[3]
+    gc = gc[:, 0:16] * silu_grad_tanh(pre)
+    grads[5] = lax.dot_general(
+        gc,
+        joined_ref[...],
+        (((0,), (0,)), ((), ())),
+        precision=HIGH,
+        preferred_element_type=F32,
+    )
+
+    deal_end(LOW)
+    own = own_ref[...]
+    grads[1] = jnp.stack([own[0:144, 32 * j : 32 * j + 32].reshape(9, 16, 32) for j in range(4)])
+    grads[2] = jnp.stack([own[288:576, 64 * j : 64 * j + 64].reshape(9, 32, 64) for j in range(2)])
+    grads[3] = own[144:288, 0:64].reshape(9, 16, 64)
+    grads[4] = jnp.concatenate(
+        [own[144:288, 64:96].reshape(9, 16, 32), own[144:288, 96:128].reshape(9, 16, 32)], axis=1
+    )
+
+    owned = square_sum(own)
+    for n in (5, 6):
+        owned = owned + square_sum(grads[n])
+    m2_ref[8:16, :] = jnp.broadcast_to(owned, (8, 128))
+    others(lambda d: message(1, m2_ref, r2_ref, d, me).start())
+    r2_ref[me] = m2_ref[...]
+    others(lambda d: message(1, m2_ref, r2_ref, d, d).wait_recv())
+
+    def take(d, total):
+        total_ref[pl.ds(pl.multiple_of(d * 8, 8), 8), :] = r2_ref[d, 0:8, :]
+        return total + r2_ref[d, 8:16, :]
+
+    squares = lax.fori_loop(0, 32, take, jnp.zeros((8, 128), F32))
+    shared = square_sum(total_ref[0:LOSS_ROW, :])
+    clip = jnp.sqrt(squares[0:1, 0:1] + shared)
+    factor = jnp.minimum(1.0, CLIP_AT / clip)
+    clip_out[...] = jnp.broadcast_to(clip, (1, 128))
+    loss_out[...] = jnp.broadcast_to(
+        jnp.sum(total_ref[LOSS_ROW : LOSS_ROW + 1, :], axis=1, keepdims=True), (1, 128)
+    )
+    grads[0] = jnp.stack([total_ref[9 * t : 9 * t + 9, :] for t in range(9)])
+    grads[7] = jnp.concatenate(
+        [
+            jnp.concatenate(
+                [total_ref[NORM_ROW + 9 * n + j : NORM_ROW + 9 * n + j + 1, :] for j in range(9)],
+                axis=1,
+            )
+            for n in range(2)
+        ],
+        axis=0,
+    )
+
+    updates = []
+    pairs = []
+    spot = 0
+    for n in range(8):
+        grad = grads[n] * factor.reshape((1,) * grads[n].ndim)
+        first_new = BETA_ONE * firsts[n][...] + (1.0 - BETA_ONE) * grad
+        second_new = BETA_TWO * seconds[n][...] + (1.0 - BETA_TWO) * grad * grad
+        first_hat = first_new / (1.0 - BETA_ONE**STEP)
+        second_hat = second_new / (1.0 - BETA_TWO**STEP)
+        update = first_hat / (jnp.sqrt(second_hat) + EPS_ADAM) + DECAY * weights[n][...]
+        outs[3 * n][...] = grad
+        outs[3 * n + 1][...] = second_new
+        outs[3 * n + 2][...] = update
+        if n in (1, 2):
+            for j in range(update.shape[0]):
+                pairs.append((spot, square_sum(weights[n][j])))
+                pairs.append((64 + spot, square_sum(update[j])))
+                spot += 1
+        elif 2 < n < 7:
+            pairs.append((spot, square_sum(weights[n][...])))
+            pairs.append((64 + spot, square_sum(update)))
+            spot += 1
+
+    m3_ref[...] = lane_value(pairs)
+    others(lambda d: message(2, m3_ref, r3_ref, d, me).start())
+    r3_ref[me] = m3_ref[...]
+
+    def step(n, ratio, at=None):
+        ratio = ratio * RATE
+        if at is None:
+            weight, out = weights[n][...], outs[3 * n + 2]
+            out[...] = weight - ratio.reshape((1,) * weight.ndim) * out[...]
+        else:
+            weight, out = weights[n][at], outs[3 * n + 2]
+            out[at] = weight - ratio.reshape((1,) * weight.ndim) * out[at]
+
+    def root_ratio(a, b):
+        return jnp.sqrt(a) / jnp.sqrt(b)
+
+    step(7, root_ratio(square_sum(weights[7][...]), square_sum(outs[23][...])))
+    edge_w, edge_u = weights[0][...], outs[2][...]
+    for lo, hi in ((0, 6), (6, 9)):
+        ratio = root_ratio(square_sum(edge_w[:, lo:hi, :]), square_sum(edge_u[:, lo:hi, :])) * RATE
+        outs[2][:, lo:hi, :] = edge_w[:, lo:hi, :] - ratio.reshape(1, 1, 1) * edge_u[:, lo:hi, :]
+
+    others(lambda d: message(2, m3_ref, r3_ref, d, d).wait_recv())
+    sums = lax.fori_loop(0, 32, lambda d, t: t + r3_ref[d], jnp.zeros((8, 128), F32))
+    spot = 0
+    for n in range(1, 7):
+        for j in range(weights[n].shape[0] if n in (1, 2) else 1):
+            ratio = root_ratio(sums[0:1, spot : spot + 1], sums[0:1, 64 + spot : 65 + spot])
+            step(n, ratio, j if n in (1, 2) else None)
+            spot += 1
+
+    back_copy(0, home_left).wait()
+
+    @pl.when(home_right != me)
+    def _():
+        back_copy(1, home_right).wait()
+
+    @pl.when(home_right == me)
+    def _():
+        back_ref[0] = imgrad_ref[:, 16:32, :]
+
+    back_out[...] = back_ref[...]
+
+    for part in range(3):
+        deal_sent(part)
+    others(lambda d: film_copy(d, me).wait_send())
+    row_mates(lambda c: cond_copy(c, cc).wait_send())
+    row_mates(lambda c: gc_copy(c, cc).wait_send())
+    for n, src in ((1, m2_ref), (2, m3_ref)):
+        others(lambda d, n=n, src=src: message(n, src, r2_ref if n == 1 else r3_ref, d, me).wait_send())
+    others(lambda d: message(0, m1_ref.at[d], r1_ref, d, me).wait_send())
+
+
+def step(*operands):
+    outs = []
+    for n in range(8):
+        outs += [jax.ShapeDtypeStruct(operands[5 + 3 * n].shape, F32)] * 3
+    outs += [jax.ShapeDtypeStruct((1, 128), F32)] * 3
+    outs += [jax.ShapeDtypeStruct((2, 16, 16, 128), F32)]
     vmem = pl.BlockSpec(memory_space=pltpu.VMEM)
+    dma = pltpu.SemaphoreType.DMA
+
+    def half(*shape):
+        return pltpu.VMEM(shape, BF)
+
+    def full(*shape):
+        return pltpu.VMEM(shape, F32)
+
     return pl.pallas_call(
-        unet_kernel,
-        out_shape=outs,
+        step_kernel,
+        out_shape=tuple(outs),
         in_specs=[vmem] * len(operands),
         out_specs=[vmem] * len(outs),
         scratch_shapes=[
-            pltpu.VMEM((6, 2, 512, 256), F32),
-            pltpu.VMEM((4, 1, 512, 256), F32),
-            pltpu.VMEM((2, 512, 256), F32),
-            pltpu.VMEM((2, 512, 256), F32),
-            pltpu.VMEM((576, 2048), BF),
-            pltpu.VMEM((576, 768), BF),
-            pltpu.VMEM((6, 2, 512, 256), BF),
-            pltpu.VMEM((3, 512, 256), BF),
-            pltpu.VMEM((512, 512), BF),
-            pltpu.VMEM((1536, 256), BF),
-            pltpu.VMEM((256, 1536), BF),
-            pltpu.VMEM((2, 3, 512, 256), BF),
-            pltpu.VMEM((256, 2048), BF),
-            pltpu.VMEM((1536, 256), BF),
-            pltpu.VMEM((7, 7, 32, 256), F32),
-            pltpu.VMEM((7, 8, 256), F32),
-            pltpu.VMEM((2, 512, 256), BF),
-            pltpu.VMEM((576, 256), F32),
-            pltpu.VMEM((N_EXCHANGE, 40, 256), F32),
-            pltpu.VMEM((N_EXCHANGE, 40, 256), F32),
-            pltpu.SemaphoreType.DMA((N_EXCHANGE,)),
-            pltpu.SemaphoreType.DMA((N_EXCHANGE,)),
+            half(4, 9, 128, 128),
+            half(2, 9, 256, 256),
+            half(9, 128, 256),
+            half(9, 256, 128),
+            full(6, 2, 512, 256),
+            full(4, 1, 512, 256),
+            full(2, 512, 256),
+            full(2, 512, 256),
+            half(576, 2048),
+            half(576, 768),
+            half(6, 2, 512, 256),
+            half(3, 512, 256),
+            half(512, 512),
+            half(1536, 256),
+            half(256, 1536),
+            half(2, 3, 512, 256),
+            half(256, 2048),
+            half(1536, 256),
+            full(7, 7, 32, 256),
+            full(7, 8, 256),
+            half(2, 512, 256),
+            full(576, 256),
+            full(N_EXCHANGE, 40, 256),
+            full(N_EXCHANGE, 40, 256),
+            full(512, 256),
+            full(512, 256),
+            full(2, 256, 256),
+            full(2, 256, 256),
+            full(2, 1152),
+            full(8, 1024),
+            full(256, 128),
+            full(16, 32, 128),
+            half(2, 256, 256),
+            half(2, 256, 256),
+            half(128, 2048),
+            half(128, 2048),
+            full(32, 2048),
+            half(4, 2, 2, 2, ALL_ROWS, 128),
+            full(2, 256, 128),
+            full(4, 32, 128),
+            full(32, 128),
+            full(32, 256),
+            full(32, 8, 256),
+            full(32, 8, 256),
+            full(8, 1024),
+            full(32, 4224),
+            full(32, 64),
+            half(4, 2, 2, ALL_ROWS, 128),
+            half(4, 2, ALL_ROWS, 128),
+            half(4, ALL_ROWS, 128),
+            half(4, ALL_ROWS, 128),
+            full(ALL_ROWS, 128),
+            full(32, 8, 384),
+            full(32, 8, 384),
+            full(16, 128),
+            full(32, 16, 128),
+            full(8, 128),
+            full(32, 8, 128),
+            full(4, 32, 128),
+            full(4, 32, 128),
+            full(32, 256),
+            full(256, 128),
+            full(2, 16, 16, 128),
+            dma((N_EXCHANGE,)),
+            dma((N_EXCHANGE,)),
+            dma((3, 5, 4, 2, 2)),
+            dma((3, 4, 2, 2, 2)),
+            dma((2,)),
+            dma((2,)),
+            dma((4,)),
+            dma((4,)),
+            dma((32,)),
+            dma((32,)),
+            dma((3, 4)),
+            dma((3, 4)),
+            dma((3, 4)),
+            dma((3, 4)),
+            dma((3, 4)),
+            dma((3, 4)),
+            dma((3, 4)),
+            dma((3, 4)),
+            dma((3, 32)),
+            dma((3, 32)),
+            dma((4,)),
+            dma((4,)),
+            dma((2,)),
+            dma((2,)),
         ],
         compiler_params=pltpu.CompilerParams(
-            collective_id=1, has_side_effects=True, vmem_limit_bytes=58 * 1024 * 1024
+            collective_id=1, has_side_effects=True, vmem_limit_bytes=62 * 1024 * 1024
         ),
-        name="unet",
+        name="step",
     )(*operands)
-
-
-def strip_moves():
-    left, right = [], []
-    for r in range(8):
-        for c in range(4):
-            pair = ((r + 1) // 2) % 4
-            core = (r + 1) % 2
-            target = (pair * 2 + c // 2) * 4 + (c % 2) * 2 + core
-            right.append((r * 4 + c, target))
-            left.append((r * 4 + (c + 1) % 4, target))
-    return left, right
-
-
-def cells_of(block):
-    rows, cols, width = block.shape
-    x = block.reshape(rows // 2, 2, cols // 2, 2, width)
-    return jnp.transpose(x, (0, 2, 3, 1, 4)).reshape(rows // 2, cols // 2, 4 * width)
-
-
-def pixels_of(cells):
-    rows, cols, width = cells.shape
-    x = cells.reshape(rows, cols, 2, 2, width // 4)
-    return jnp.transpose(x, (0, 3, 1, 2, 4)).reshape(2 * rows, 2 * cols, width // 4)
-
-
-BOTH = ("rows", "cols")
-
-
-def flip_t(w):
-    return jnp.swapaxes(w[::-1], 1, 2)
 
 
 def per_device_strips(
@@ -1428,208 +2359,36 @@
     slot_live,
     *params,
 ):
-    weights, firsts, seconds = params[0::3], params[1::3], params[2::3]
-    edge_w, low_w, high_w, down_w, up_w, cond_w, film_w, norm_w = weights
-    rr, cc = lax.axis_index("rows"), lax.axis_index("cols")
-    by_cell, by_tile = phase_tables()
-    moves_left, moves_right = strip_moves()
-
     block = jnp.concatenate(
         [cells_of(image_pair[0].astype(F32)), cells_of(noise_target[0])], axis=-1
     )
-    left = lax.ppermute(block[:, 16:], BOTH, moves_right)
-    right = lax.ppermute(block[:, :16], BOTH, moves_left)
-    strip = jnp.concatenate([left, right], axis=1).reshape(512, 36)
-    img = jnp.pad(strip[:, 0:24], ((0, 0), (0, 232)))
-    tgt = jnp.pad(strip[:, 24:36], ((0, 0), (0, 244)))
-
-    pair, core = rr // 2, lax.rem(cc, 2)
-    col = lax.rem(rr, 2) * 2 + cc // 2
-    slot_row = jnp.where(pair == 0, 4 * (1 - core), pair)
-    slot_left = slot_row * 5 + col + 1
-    slot_right = slot_row * 5 + jnp.where(col == 3, 0, col + 1)
-    slots = jnp.stack([slot_left, slot_right])
-
-    shards = [low_w, high_w, down_w, up_w]
-    flat = [w.astype(BF).reshape(-1, 128) for w in shards]
-    sizes = [f.shape[0] for f in flat]
-    every = lax.all_gather(jnp.concatenate(flat, axis=0), BOTH, axis=0, tiled=False)
-    starts = np.cumsum([0] + sizes)
-
-    def whole(k, shape):
-        part = every[:, starts[k] : starts[k + 1]].reshape((8, 4) + shape)
-        n = len(shape)
-        order = tuple(range(2, n)) + (0, n, 1, n + 1)
-        x = jnp.transpose(part, order)
-        return x.reshape(shape[:-2] + (8 * shape[-2], 4 * shape[-1]))
-
-    low = whole(0, low_w.shape)
-    high = whole(1, high_w.shape)
-    down = whole(2, down_w.shape)
-    up = whole(3, up_w.shape)
-
-    joined = jnp.concatenate([time_embed(timesteps).astype(BF), text_pooled], axis=-1)[0].reshape(25, -1)
-    pre_own = jnp.dot(joined, cond_w.astype(BF), preferred_element_type=F32)
-    pre = lax.all_gather(pre_own, BOTH, axis=1, tiled=True)
-    cond = jax.nn.silu(pre).astype(BF)
-    film_rows, film_cols = film_w.shape
-    cond_own = lax.dynamic_slice_in_dim(cond, rr * film_rows, film_rows, 1)
-    film_low = film_w.astype(BF)
-    film_part = jnp.dot(cond_own, film_low, preferred_element_type=F32)
-    film = lax.all_gather(lax.psum(film_part, "rows"), "cols", axis=1, tiled=True)
-    own_film = jnp.take(film, slots, axis=0)
-
-    live_slots = slot_live[0].astype(F32)
-    side = np.array([32, 64, 64, 64, 32], np.float32)
-    count = 3.0 * jnp.sum(live_slots * (side[:, None] * side[None, :]))
-    own_live = jnp.take(live_slots.reshape(25), slots)
-    small = jnp.concatenate([own_live, (2.0 / count)[None], jnp.zeros((5,), F32)])
-    small = jnp.broadcast_to(small[:, None], (8, 256))
-
-    edge_low = edge_w.astype(BF)
-    inconv = jnp.swapaxes(edge_low[:, :, 0:6], 1, 2)
-    head = edge_low[:, :, 6:9]
-    cell_tab = by_cell.astype(jnp.bfloat16)
-    tile_tab = by_tile.astype(jnp.bfloat16)
-
-    def by_cells(w):
-        x = jnp.einsum("oqpt,tcd->oqcpd", cell_tab, w)
-        x = x.reshape(-1, 2, 256)
-        return jnp.transpose(jnp.pad(x, ((0, 256 - x.shape[0]), (0, 0), (0, 0))), (1, 0, 2))
-
-    def by_tiles(w):
-        x = jnp.einsum("grpt,tcd->grcpd", tile_tab, w).reshape(2048, -1)
-        return jnp.pad(x, ((0, 0), (0, 128 - x.shape[1])))
-
-    outs = unet(
-        img,
-        tgt,
-        small,
-        own_film,
-        norm_w,
-        low,
-        high,
-        down,
-        up,
-        by_cells(inconv),
-        by_tiles(flip_t(inconv)),
-        by_tiles(head),
-        by_cells(flip_t(head)),
-    )
-    dlow, dhigh, ddown, dup, dwi, dwh, fgrad, ngrad, lost, imgrad = outs
-
-    back = (imgrad[:, 0:24] * (count)).reshape(16, 32, 24)
-    back_right = lax.ppermute(back[:, :16], BOTH, [(t, s) for s, t in moves_right])
-    back_left = lax.ppermute(back[:, 16:], BOTH, [(t, s) for s, t in moves_left])
-    image_grad = pixels_of(jnp.concatenate([back_left, back_right], axis=1))[None]
-
-    def fold(x, width):
-        x = jnp.transpose(x, (1, 0, 2))[: 36 * width].reshape(9, 4, width, 4, 128)
-        return jnp.einsum("oqpt,oqcpd->tcd", by_cell, x, precision=HIGH)
-
-    grad_in = fold(dwi, 6)
-    grad_head = fold(dwh, 3)[::-1]
-    edge_local = jnp.concatenate([jnp.swapaxes(grad_in, 1, 2), jnp.swapaxes(grad_head, 1, 2)], axis=2)
-    spot = (jnp.arange(25)[:, None] == slots[None, :]).astype(F32)
-    film_local = jnp.dot(spot, fgrad, precision=HIGH)
-    pieces = [film_local.reshape(-1), edge_local.reshape(-1), ngrad.reshape(-1), jnp.sum(lost).reshape(1)]
-    lens = [p.shape[0] for p in pieces]
-    total = lax.psum(jnp.concatenate(pieces), BOTH)
-    ends = np.cumsum([0] + lens)
-    film_sum = total[ends[0] : ends[1]].reshape(25, 1024)
-    edge_sum = total[ends[1] : ends[2]].reshape(9, 128, 9)
-    norm_sum = total[ends[2] : ends[3]].reshape(2, 1152)
-    loss_sum = total[ends[3]]
-
-    film_mine = lax.dynamic_slice_in_dim(film_sum, cc * film_cols, film_cols, 1)
-    film_own = lax.dot_general(
-        cond_own.astype(F32), film_mine, (((0,), (0,)), ((), ())), precision=HIGH
-    )
-    gc_part = lax.dot_general(
-        film_mine, film_low.astype(F32), (((1,), (1,)), ((), ())), precision=HIGH
-    )
-    gc = lax.psum_scatter(gc_part, "cols", scatter_dimension=1, tiled=True) * silu_grad(pre_own)
-    cond_grad = lax.dot_general(joined.astype(F32), gc, (((0,), (0,)), ((), ())), precision=HIGH)
-
-    def dealt(g, shape):
-        n = len(shape)
-        lead = shape[:-2]
-        x = g.reshape(lead + (8, shape[-2], 4, shape[-1]))
-        m = len(lead)
-        x = jnp.transpose(x, (m, m + 2) + tuple(range(m)) + (m + 1, m + 3))
-        return x.reshape(32, -1, 128)
-
-    packed = jnp.concatenate(
-        [dealt(g, w.shape) for g, w in zip((dlow, dhigh, ddown, dup), shards)], axis=1
-    )
-    mine = lax.psum_scatter(packed, BOTH, scatter_dimension=0, tiled=False).astype(F32)
-    own = [mine[starts[k] : starts[k + 1]].reshape(w.shape) for k, w in enumerate(shards)]
-    grads = (edge_sum, own[0], own[1], own[2], own[3], cond_grad, film_own, norm_sum)
-    results, clip_norm = lamb(weights, firsts, seconds, grads)
-    return tuple(results) + (loss_sum, count, clip_norm, image_grad)
-
-
-def lamb(weights, firsts, seconds, grads):
-    sharded = (1, 2, 3, 4, 5, 6)
-    stacked = (1, 2)
-    owned_sq = sum((jnp.sum(grads[k] * grads[k]) for k in sharded))
-    shared_sq = sum((jnp.sum(grads[k] * grads[k]) for k in range(8) if k not in sharded))
-    clip_norm = jnp.sqrt(lax.psum(owned_sq, BOTH) + shared_sq)
-    factor = jnp.minimum(1.0, CLIP_AT / clip_norm)
-    clipped, moments, updates = ([], [], [])
-    for k in range(8):
-        grad = grads[k] * factor
-        first_new = BETA_ONE * firsts[k] + (1.0 - BETA_ONE) * grad
-        second_new = BETA_TWO * seconds[k] + (1.0 - BETA_TWO) * grad * grad
-        first_hat = first_new / (1.0 - BETA_ONE**STEP)
-        second_hat = second_new / (1.0 - BETA_TWO**STEP)
-        clipped.append(grad)
-        moments.append(second_new)
-        updates.append(first_hat / (jnp.sqrt(second_hat) + EPS_ADAM) + DECAY * weights[k])
-
-    def matrix_squares(values, k):
-        if k in stacked:
-            return jnp.sum(values * values, axis=tuple(range(1, values.ndim)))
-        return jnp.sum(values * values).reshape(1)
-
-    sums = lax.psum(
-        jnp.stack(
-            [
-                jnp.concatenate([matrix_squares(weights[k], k) for k in sharded]),
-                jnp.concatenate([matrix_squares(updates[k], k) for k in sharded]),
-            ]
-        ),
-        BOTH,
-    )
-    ratios = jnp.sqrt(sums[0]) / jnp.sqrt(sums[1])
-    position = 0
-    results = []
-    for k in range(8):
-        if k in sharded:
-            span = weights[k].shape[0] if k in stacked else 1
-            ratio = ratios[position : position + span]
-            position += span
-            ratio = (
-                ratio.reshape((span,) + (1,) * (weights[k].ndim - 1)) if k in stacked else ratio[0]
-            )
-        elif k == 0:
-            part = (jnp.arange(9) < 6)[None, None, :]
-            other = jnp.logical_not(part)
-            weight_sq_two = weights[k] * weights[k]
-            update_sq_two = updates[k] * updates[k]
-            ratio_in = jnp.sqrt(jnp.sum(jnp.where(part, weight_sq_two, 0.0))) / jnp.sqrt(
-                jnp.sum(jnp.where(part, update_sq_two, 0.0))
-            )
-            ratio_out = jnp.sqrt(jnp.sum(jnp.where(other, weight_sq_two, 0.0))) / jnp.sqrt(
-                jnp.sum(jnp.where(other, update_sq_two, 0.0))
-            )
-            ratio = jnp.where(part, ratio_in, ratio_out)
-        else:
-            ratio = jnp.sqrt(jnp.sum(weights[k] * weights[k])) / jnp.sqrt(
-                jnp.sum(updates[k] * updates[k])
-            )
-        results.extend([clipped[k], moments[k], weights[k] - RATE * ratio * updates[k]])
-    return results, clip_norm
+    block = jnp.pad(block, ((0, 0), (0, 0), (0, 92)))
+    block = jnp.stack([block[:, 0:16], block[:, 16:32]]).reshape(2, 256, 128)
+    lanes = jnp.asarray(lane_tables(), BF)
+
+    def view(n, a):
+        return jnp.swapaxes(a, 1, 2) if n == 0 else a.T if n == 5 else a
+
+    state = [view(n // 3, a) for n, a in enumerate(params)]
+    results = step(
+        slot_live[0], time_embed(timesteps)[0].astype(BF), text_pooled[0], block, lanes, *state
+    )
+    new = [view(n // 3, a) for n, a in enumerate(results[:24])]
+    loss, count, clip, back = results[24:]
+    back = jnp.concatenate([back[0], back[1]], axis=1)[:, :, 0:24]
+    return tuple(new) + (loss[0, 0], count[0, 0], clip[0, 0], pixels_of(back)[None])
+
+
+def cells_of(block):
+    rows, cols, width = block.shape
+    x = block.reshape(rows // 2, 2, cols // 2, 2, width)
+    return jnp.transpose(x, (0, 2, 3, 1, 4)).reshape(rows // 2, cols // 2, 4 * width)
+
+
+def pixels_of(cells):
+    rows, cols, width = cells.shape
+    x = cells.reshape(rows, cols, 2, 2, width // 4)
+    return jnp.transpose(x, (0, 3, 1, 2, 4)).reshape(2 * rows, 2 * cols, width // 4)
 
 
 def solution(mesh):

time: 679 us -> 196 us (0.29); the launches traced: 672 us -> 196 us
  waiting for transfers between devices: 187 us -> 0 us
  blocking collectives: 162 us -> 0 us
  local copies, waits for them, and re-layouts: 143 us -> 25.3 us
  Pallas kernels: 69.5 us -> 164 us
  other arithmetic: 55.1 us -> 2.36 us
  between operations: 30.2 us -> 4.38 us
  starting transfers between devices: 16.7 us -> 0 us
  matrix products: 8.31 us -> 0 us
    psum x3 -> x0, blocking collectives: 113 us -> none  [the longest x1 40 us: lamb(): clip_norm = jnp.sqrt(lax.psum(owned_sq, BOTH) + shared_sq)]
    reduce_scatter x2 -> x0, waiting for transfers between devices: 104 us -> none  [the longest x1 104 us: per_device_strips(): lax.psum_scatter(packed, BOTH, scatter_dimension=0, tiled=False).astype(F32)]
    pallas_call x1, Pallas kernels: 69.5 us -> 164 us  [step(): pl.pallas_call(step_kernel, out_shape=tuple(outs), in_specs=[vmem] * len(...]
    reshape x38 -> x0, local copies, waits for them, and re-layouts: 82.2 us -> none  [the longest x8 25.2 us: dealt(): x = g.reshape(lead + (8, shape[-2], 4, shape[-1]))]
    psum x1 -> x0, waiting for transfers between devices: 76.8 us -> none  [per_device_strips(): total = lax.psum(jnp.concatenate(pieces), BOTH)]
    all_gather x2 -> x0, blocking collectives: 49.1 us -> none  [the longest x1 42.8 us: per_device_strips(): pre = lax.all_gather(pre_own, BOTH, axis=1, tiled=True)]
    reduce_sum x18 -> x0, other arithmetic: 29.7 us -> none  [the longest x6 12.8 us: matrix_squares(): return jnp.sum(values * values).reshape(1)]
    transpose x10 -> x0, local copies, waits for them, and re-layouts: 28 us -> none  [the longest x4 27 us: whole(): x = jnp.transpose(part, order)]
  transfers between devices with their start and end apart: 8 -> 0, of which waited for: 3 -> 0; matrix products, arithmetic and copies ran while one was open for 11% -> 0% of each run, Pallas kernels for 0% -> 0%
where the time goes in v3:
time: 196 us
  Pallas kernels  164 us (84%)
  local copies, waits for them, and re-layouts  25.3 us (13%)
  between operations  4.38 us (2%)
  other arithmetic  2.36 us (1%)
    pallas_call x1, Pallas kernels, step(): pl.pallas_call(step_kernel, out_shape=tuple(outs), in_specs=[vmem] * len(...  164 us
    unnamed x82, local copies, waits for them, and re-layouts  18.3 us

profile of v3, /device:TPU:0, one launch (start us, length us, event | category | flops | bytes accessed | tf_op | source)
XLA Modules:
  0.0 196.0 jit_solution(9940948349059091577)
XLA Ops:
  0.7 0.7 fusion.2
  1.4 1.3 copy.76
  2.8 0.7 maximum_bitcast_fusion.refs_1_
  3.5 1.1 copy.63
  4.6 0.7 copy.64
  5.3 1.6 reshape_squeeze.3
  6.9 0.7 copy.65
  8.8 0.7 pad_maximum_fusion.1.refs_3_
  9.5 164.0 %step.1 = (f32[9,9,128]{2,1,0:T(8,128)}, f32[9,9,128]{2,1,0:T(8,128)}, f32[9,9,128]{2,1,0:T(8,128)}, f32[4,9,16,32]{3,2,1,0:T(8,128)}, f32[4,9,16,32]{3,2,1,0:T(...) custom-call(s32[5,5]{1,0:T(8,128)} %bitcast.67, ...), custom_call_target="tpu_custom_call" | custom-call | tf_op jit(solution)/shard_map/step/pallas_call | solution.py:2253
  173.5 1.0 slice_bitcast_fusion.1
  174.7 0.7 copy.69
  175.4 1.0 copy.70
  176.5 0.6 copy.104
  177.1 0.6 copy.105
  177.7 0.6 copy.106
  178.4 0.7 copy.107
  179.1 0.7 copy.108
  179.8 0.7 copy.109
  180.5 0.7 copy.110
  181.3 0.7 copy.111
  182.0 0.7 copy.112
  182.7 0.6 copy.113
  183.3 0.6 copy.114
  184.0 0.6 copy.115
  184.6 0.7 copy.116
  185.3 0.7 copy.117
  186.0 0.7 copy.118
  186.6 0.7 copy.119
  187.3 0.7 copy.120
  188.1 0.7 copy.121
  188.8 0.6 copy.122
  190.0 0.6 copy.124
  (68 shorter events, 4.1 us)
Async XLA Ops:
  0.7 4.6 %copy-start.21 = (f32[1,32,64,3]{2,1,3,0:T(8,128)S(1)}, f32[1,32,64,3]{2,1,3,0:T(8,128)}, u32[]{:S(2)}) copy-start(f32[1,32,64,3]{2,1,3,0:T(8,128)} %param.31) | copy-start | bytes 73732
  174.5 1.9 copy-start.17
  174.6 2.5 %copy-start.16 = (f32[9,9,128]{2,1,0:T(8,128)S(1)}, f32[9,9,128]{2,1,0:T(8,128)}, u32[]{:S(2)}) copy-start(f32[9,9,128]{2,1,0:T(8,128)} %get-tuple-element.57) | copy-start | bytes 124420
  174.6 3.2 %copy-start.15 = (f32[9,9,128]{2,1,0:T(8,128)S(1)}, f32[9,9,128]{2,1,0:T(8,128)}, u32[]{:S(2)}) copy-start(f32[9,9,128]{2,1,0:T(8,128)} %get-tuple-element.58) | copy-start | bytes 124420
  174.6 3.8 %copy-start.5 = (f32[4,9,16,32]{3,2,1,0:T(8,128)S(1)}, f32[4,9,16,32]{3,2,1,0:T(8,128)}, u32[]{:S(2)}) copy-start(f32[4,9,16,32]{3,2,1,0:T(8,128)} %get-tuple-element.149) | copy-start | bytes 221188
  174.7 4.3 %copy-start.4 = (f32[4,9,16,32]{3,2,1,0:T(8,128)S(1)}, f32[4,9,16,32]{3,2,1,0:T(8,128)}, u32[]{:S(2)}) copy-start(f32[4,9,16,32]{3,2,1,0:T(8,128)} %get-tuple-element.150) | copy-start | bytes 221188
  175.4 4.4 %copy-start.3 = (f32[4,9,16,32]{3,2,1,0:T(8,128)S(1)}, f32[4,9,16,32]{3,2,1,0:T(8,128)}, u32[]{:S(2)}) copy-start(f32[4,9,16,32]{3,2,1,0:T(8,128)} %get-tuple-element.151) | copy-start | bytes 221188
  175.4 5.1 %copy-start.2 = (f32[2,9,32,64]{3,2,1,0:T(8,128)S(1)}, f32[2,9,32,64]{3,2,1,0:T(8,128)}, u32[]{:S(2)}) copy-start(f32[2,9,32,64]{3,2,1,0:T(8,128)} %get-tuple-element.152) | copy-start | bytes 442372
  176.5 4.8 %copy-start.1 = (f32[2,9,32,64]{3,2,1,0:T(8,128)S(1)}, f32[2,9,32,64]{3,2,1,0:T(8,128)}, u32[]{:S(2)}) copy-start(f32[2,9,32,64]{3,2,1,0:T(8,128)} %get-tuple-element.153) | copy-start | bytes 442372
  177.7 4.3 %copy-start = (f32[2,9,32,64]{3,2,1,0:T(8,128)S(1)}, f32[2,9,32,64]{3,2,1,0:T(8,128)}, u32[]{:S(2)}) copy-start(f32[2,9,32,64]{3,2,1,0:T(8,128)} %get-tuple-element.154) | copy-start | bytes 442372
  179.1 3.6 %copy-start.14 = (f32[9,16,64]{2,1,0:T(8,128)S(1)}, f32[9,16,64]{2,1,0:T(8,128)}, u32[]{:S(2)}) copy-start(f32[9,16,64]{2,1,0:T(8,128)} %get-tuple-element.155) | copy-start | bytes 110596
  179.1 4.3 %copy-start.13 = (f32[9,16,64]{2,1,0:T(8,128)S(1)}, f32[9,16,64]{2,1,0:T(8,128)}, u32[]{:S(2)}) copy-start(f32[9,16,64]{2,1,0:T(8,128)} %get-tuple-element.156) | copy-start | bytes 110596
  179.1 4.9 %copy-start.12 = (f32[9,16,64]{2,1,0:T(8,128)S(1)}, f32[9,16,64]{2,1,0:T(8,128)}, u32[]{:S(2)}) copy-start(f32[9,16,64]{2,1,0:T(8,128)} %get-tuple-element.157) | copy-start | bytes 110596
  179.1 5.6 %copy-start.11 = (f32[9,32,32]{2,1,0:T(8,128)S(1)}, f32[9,32,32]{2,1,0:T(8,128)}, u32[]{:S(2)}) copy-start(f32[9,32,32]{2,1,0:T(8,128)} %get-tuple-element.158) | copy-start | bytes 110596
  179.8 5.5 %copy-start.10 = (f32[9,32,32]{2,1,0:T(8,128)S(1)}, f32[9,32,32]{2,1,0:T(8,128)}, u32[]{:S(2)}) copy-start(f32[9,32,32]{2,1,0:T(8,128)} %get-tuple-element.159) | copy-start | bytes 110596
  179.8 6.1 %copy-start.9 = (f32[9,32,32]{2,1,0:T(8,128)S(1)}, f32[9,32,32]{2,1,0:T(8,128)}, u32[]{:S(2)}) copy-start(f32[9,32,32]{2,1,0:T(8,128)} %get-tuple-element.160) | copy-start | bytes 110596
  180.5 6.1 %copy-start.8 = (f32[16,4224]{1,0:T(8,128)S(1)}, f32[16,4224]{1,0:T(8,128)}, u32[]{:S(2)}) copy-start(f32[16,4224]{1,0:T(8,128)} %get-tuple-element.71) | copy-start | bytes 811012
  181.3 6.1 %copy-start.7 = (f32[16,4224]{1,0:T(8,128)S(1)}, f32[16,4224]{1,0:T(8,128)}, u32[]{:S(2)}) copy-start(f32[16,4224]{1,0:T(8,128)} %get-tuple-element.72) | copy-start | bytes 811012
  182.0 6.1 %copy-start.6 = (f32[16,4224]{1,0:T(8,128)S(1)}, f32[16,4224]{1,0:T(8,128)}, u32[]{:S(2)}) copy-start(f32[16,4224]{1,0:T(8,128)} %get-tuple-element.73) | copy-start | bytes 811012
  182.7 6.1 %copy-start.20 = (f32[64,256]{1,0:T(8,128)S(1)}, f32[64,256]{1,0:T(8,128)}, u32[]{:S(2)}) copy-start(f32[64,256]{1,0:T(8,128)} %get-tuple-element.164) | copy-start | bytes 196612
  182.7 6.7 %copy-start.19 = (f32[64,256]{1,0:T(8,128)S(1)}, f32[64,256]{1,0:T(8,128)}, u32[]{:S(2)}) copy-start(f32[64,256]{1,0:T(8,128)} %get-tuple-element.165) | copy-start | bytes 196612
  182.7 7.3 %copy-start.18 = (f32[64,256]{1,0:T(8,128)S(1)}, f32[64,256]{1,0:T(8,128)}, u32[]{:S(2)}) copy-start(f32[64,256]{1,0:T(8,128)} %get-tuple-element.166) | copy-start | bytes 196612
  183.3 7.3 %copy-start.24 = (f32[2,1152]{1,0:T(2,128)S(1)}, f32[2,1152]{1,0:T(2,128)}, u32[]{:S(2)}) copy-start(f32[2,1152]{1,0:T(2,128)} %get-tuple-element.167) | copy-start | bytes 27652
  183.3 7.9 %copy-start.23 = (f32[2,1152]{1,0:T(2,128)S(1)}, f32[2,1152]{1,0:T(2,128)}, u32[]{:S(2)}) copy-start(f32[2,1152]{1,0:T(2,128)} %get-tuple-element.168) | copy-start | bytes 27652
  184.0 7.9 %copy-start.22 = (f32[2,1152]{1,0:T(2,128)S(1)}, f32[2,1152]{1,0:T(2,128)}, u32[]{:S(2)}) copy-start(f32[2,1152]{1,0:T(2,128)} %get-tuple-element.169) | copy-start | bytes 27652
  184.0 8.5 %copy-start.27 = (f32[1,128]{1,0:T(1,128)S(1)}, f32[1,128]{1,0:T(1,128)}, u32[]{:S(2)}) copy-start(f32[1,128]{1,0:T(1,128)} %get-tuple-element.80) | copy-start | bytes 1540
  184.0 8.5 %copy-start.26 = (f32[1,128]{1,0:T(1,128)S(1)}, f32[1,128]{1,0:T(1,128)}, u32[]{:S(2)}) copy-start(f32[1,128]{1,0:T(1,128)} %get-tuple-element.81) | copy-start | bytes 1540
  184.0 8.6 %copy-start.25 = (f32[1,128]{1,0:T(1,128)S(1)}, f32[1,128]{1,0:T(1,128)}, u32[]{:S(2)}) copy-start(f32[1,128]{1,0:T(1,128)} %get-tuple-element.82) | copy-start | bytes 1540
